TPU v7x, 32 devices: a whole 2x2x4 slice. The times are simulated.
32 devices in a mesh: cam: 4 (over x, core), clip: 8 (over z, y).
Axes of the slice: x: 2, y: 2, z: 4, core: 2. Of those that a mesh axis runs over, the one named last changes fastest.
Arguments:
- tokens: bfloat16 [16, 4, 256, 1024], P('clip', 'cam'), may hold values from -6 to 6
- w_query: bfloat16 [1024, 1024], replicated, may hold values from -0.1875 to 0.1875
- w_key: bfloat16 [1024, 1024], replicated, may hold values from -0.1875 to 0.1875
- w_value: bfloat16 [1024, 1024], replicated, may hold values from -0.1875 to 0.1875
- w_proj: bfloat16 [1024, 256], replicated, may hold values from -0.1875 to 0.1875
- prototypes: bfloat16 [256, 65536], P(None, ('cam', 'clip')), may hold values from -6 to 6
Outputs:
- codes: float32 [16, 65536], P(None, ('cam', 'clip'))
- prototype_gradient: float32 [256, 65536], P(None, ('cam', 'clip'))
- grad_proj: float32 [1024, 256], P('clip')
- grad_value: float32 [1024, 1024], P('clip', 'cam')
All inputs are finite; a program needn't handle non-finite values.
Results may differ from a plain program's by a relative error of at most 0.015.
Values may be sent and summed in bfloat16 or wider, within the bound.
No kernel may reach another device: no remote copies, remote signals or barrier semaphores. Data moves between devices by JAX's collectives and lax.ppermute only.
A program may use at most 128 MiB of HBM per device.

v0:
```python
import jax
import jax.numpy as jnp
from jax import lax
from jax.sharding import PartitionSpec as P

D = 1024
HD = 64
PROTOS = 65536
TOK = 256
ITERS = 3
H = 16


SINK_EPS = 0.05
SOFTMAX_TEMP = 0.1
NORM_EPS = 1e-06
heads_per_group = 4


def column_sums(query_rows, key_rows, total):
    scores = jnp.einsum(
        "ihe,jhe->hij", query_rows, key_rows, preferred_element_type=jnp.float32
    ) * HD ** (-0.5)
    exponent_values = jnp.exp(scores)
    probs = exponent_values / jnp.sum(exponent_values, axis=2, keepdims=True)
    return jnp.sum(probs, axis=1) / total


def camera_block(query_clip, key_clip, total):
    tokens_here = query_clip.shape[0]
    width = heads_per_group * HD
    parts = []
    for group in range(H // heads_per_group):
        query_group = query_clip[:, group * width : (group + 1) * width].reshape(
            tokens_here, heads_per_group, HD
        )
        key_group = key_clip[:, group * width : (group + 1) * width].reshape(
            total, heads_per_group, HD
        )
        parts.append(column_sums(query_group, key_group, total))
    return jnp.concatenate(parts, axis=0)


def local(tokens, w_query, w_key, w_value, w_proj, prototypes):
    clips = tokens.shape[0]
    own = tokens.reshape(clips, TOK, D)
    query_vectors = jnp.einsum(
        "ctd,de->cte", own, w_query, preferred_element_type=jnp.float32
    ).astype(jnp.bfloat16)
    key_rows = jnp.einsum("ctd,de->cte", own, w_key, preferred_element_type=jnp.float32).astype(
        jnp.bfloat16
    )
    collected_rows = lax.all_gather(key_rows.reshape(clips, 1, TOK, D), "cam", axis=1, tiled=True)
    cameras = collected_rows.shape[1]
    total = cameras * TOK

    def per_clip(clip_pair):
        return camera_block(clip_pair[0], clip_pair[1], total)

    partial_sums = lax.map(per_clip, (query_vectors, collected_rows.reshape(clips, total, D)))
    weights = lax.psum_scatter(
        partial_sums.reshape(clips, H, cameras, TOK), "cam", scatter_dimension=2, tiled=True
    )
    weights = weights.reshape(clips, H, TOK).astype(jnp.bfloat16)
    mixture = jnp.einsum("chj,cjd->chd", weights, own, preferred_element_type=jnp.float32).astype(
        jnp.bfloat16
    )
    head_out = jnp.einsum(
        "chd,dhe->che", mixture, w_value.reshape(D, H, HD), preferred_element_type=jnp.float32
    )
    pooled = lax.psum(head_out.reshape(clips, D), "cam").astype(jnp.bfloat16)
    share_rows = D // lax.axis_size("clip")
    mixed_views = lax.psum_scatter(
        mixture.astype(jnp.float32).astype(jnp.bfloat16), "cam", scatter_dimension=1, tiled=True
    ).astype(jnp.float32)
    mixed_rows, pooled_rows = (
        lax.all_to_all(mixed_views, "clip", split_axis=2, concat_axis=0, tiled=True),
        lax.all_to_all(
            pooled.astype(jnp.float32).reshape(clips, 1, D),
            "clip",
            split_axis=2,
            concat_axis=0,
            tiled=True,
        ),
    )
    embed = jnp.dot(pooled, w_proj, preferred_element_type=jnp.float32)
    embed_norm = jnp.sqrt(jnp.sum(embed * embed, axis=1, keepdims=True) + NORM_EPS)
    unit = embed / embed_norm
    unit_b = unit.astype(jnp.bfloat16)
    all_units = lax.all_gather(unit_b, "clip", axis=0, tiled=True)
    proto_f = prototypes.astype(jnp.float32)
    column_norm = jnp.sqrt(jnp.sum(proto_f * proto_f, axis=0, keepdims=True) + NORM_EPS)
    unit_proto = proto_f / column_norm
    proto_b = unit_proto.astype(jnp.bfloat16)
    logit_scores = jnp.dot(all_units, proto_b, preferred_element_type=jnp.float32)
    exponent_values = jnp.exp(logit_scores / SOFTMAX_TEMP)
    assign = jnp.exp(logit_scores / SINK_EPS)
    prob_total = lax.psum(jnp.sum(exponent_values, axis=1), ("cam", "clip"))
    first_step = 0
    for step in range(first_step, ITERS):
        assign = assign / jnp.sum(assign, axis=0, keepdims=True)
        row_total = lax.psum(jnp.sum(assign, axis=1), ("cam", "clip"))
        assign = assign / row_total[:, None]
    prob = exponent_values / prob_total[:, None]
    grad_logits = (PROTOS * (prob - assign)).astype(jnp.bfloat16)
    codes = PROTOS * assign
    grad_unit = lax.psum_scatter(
        jnp.dot(grad_logits, proto_b.T, preferred_element_type=jnp.float32),
        "clip",
        scatter_dimension=0,
        tiled=True,
    )
    grad_unit = lax.psum(grad_unit, "cam")
    grad_embed = (grad_unit - unit * jnp.sum(unit * grad_unit, axis=1, keepdims=True)) / embed_norm
    grad_embed_b = grad_embed.astype(jnp.bfloat16)
    grad_pooled = jnp.dot(grad_embed_b, w_proj.T, preferred_element_type=jnp.float32).astype(
        jnp.bfloat16
    )
    cam_cols = D // lax.axis_size("cam")
    heads_here = cam_cols // HD
    head_block = lax.dynamic_slice_in_dim(
        grad_pooled, lax.axis_index("cam") * cam_cols, cam_cols, 1
    )
    all_heads, all_embed = (
        lax.all_gather(head_block, "clip", axis=0, tiled=True),
        lax.all_gather(grad_embed_b, "clip", axis=0, tiled=True),
    )
    pooled_share = pooled_rows.reshape(all_embed.shape[0], share_rows).astype(jnp.bfloat16)
    grad_proj = jnp.einsum("cd,ce->de", pooled_share, all_embed, preferred_element_type=jnp.float32)
    head_grads = all_heads.astype(jnp.float32).reshape(all_heads.shape[0], heads_here, HD)
    grad_value = jnp.einsum(
        "bhd,bhe->dhe", mixed_rows, head_grads, precision=lax.Precision.HIGHEST
    ).reshape(share_rows, cam_cols)
    grad_unit_proto = jnp.einsum(
        "be,bk->ek", all_units, grad_logits, preferred_element_type=jnp.float32
    )
    prototype_gradient = (
        grad_unit_proto - unit_proto * jnp.sum(unit_proto * grad_unit_proto, axis=0, keepdims=True)
    ) / column_norm
    return (codes, prototype_gradient, grad_proj, grad_value)


def solution(mesh):
    in_specs = (P("clip", "cam", None, None), P(), P(), P(), P(), P(None, ("cam", "clip")))
    out_specs = (
        P(None, ("cam", "clip")),
        P(None, ("cam", "clip")),
        P("clip", None),
        P("clip", "cam"),
    )
    return jax.shard_map(local, mesh=mesh, in_specs=in_specs, out_specs=out_specs, check_vma=False)
```

profile of v0, /device:TPU:0, one launch (start us, length us, event | category | flops | bytes accessed | tf_op | source)
XLA Modules:
  0.0 427.0 jit_solution(16833356773032230240)
XLA Ops:
  7.2 1.5 copy-done
  8.8 3.5 fusion.33
  12.3 4.0 copy.55
  19.7 4.5 %fusion.30 = bf16[2,256,1024]{2,1,0:T(8,128)(2,1)} fusion(bf16[1024,1024]{1,0:T(8,128)(2,1)} %param.9, bf16[2,1,256,1024]{3,2,1,0:T(8,128)(2,1)} %param.8), kind=kOutput, calls=%fused_computation.45 | convolution fusion | flops 1074266112 | bytes 4194304 | tf_op jit(solution)/shard_map/ctd,de->cte/dot_general | solution.py:47
  24.1 25.4 %all-gather.6.cloned.1.call-done = bf16[2,1024,1024]{2,1,0:T(8,128)(2,1)} async-done(((bf16[2,256,1024]{2,1,0:T(8,128)(2,1)}), bf16[2,1024,1024]{2,1,0:T(8,128)(2,1)}) %all-gather.6.cloned.1.call-update) | async-done | bytes 4194320 | tf_op jit(solution)/shard_map/all_gather | solution.py:53
  49.6 81.7 %while.10 = (s32[]{:T(128)}, f32[2,16,1024]{2,1,0:T(8,128)}, bf16[2,256,1024]{2,1,0:T(8,128)(2,1)}, bf16[2,1024,1024]{2,1,0:T(8,128)(2,1)}, s32[]{:T(128)}) while((s32[]{:T(128)}, f32[2,16,1024]{2,1,0:T(8,128)}, bf16[2,256,1024]{2,1,0:T(8,128)(2,1)}, bf16[2,1024,1024]{2,1,0:T(8,128)(2,1)}, s32[]{:T(128)}) %tuple.53), condition=%wide.region_9.10_spmd, body=%wide.region_0.9_spmd.sunk | while | flops 1090576384 | bytes 69009704 | solution.py:60
  49.6 3.1 constant_dynamic-slice_fusion.6
  52.7 3.9 copy.82
  56.6 3.0 fusion.140
  60.6 3.8 fusion.143
  64.3 4.0 divide_reduce_fusion.11
  68.4 2.7 fusion.144
  71.1 4.6 %divide_reduce_fusion.12 = f32[4,1024]{1,0:T(4,128)} fusion(f32[4,256,1024]{2,1,0:T(8,128)} %fusion.144, bf16[256,4,64]{0,2,1:T(8,128)(2,1)S(1)} %bitcast.176, bf16[1024,4,64]{0,2,1:T(8,128)(2,1)S(1)} %bitcast.168), kind=kOutput, calls=%fused_computation.11.clone.1 | convolution fusion | flops 138409984 | bytes 4866048 | tf_op jit(solution)/shard_map/while/body/eval_jaxpr/div | solution.py:25
  75.6 0.7 broadcast_multiply_fusion.8
  76.4 2.7 fusion.142
  79.1 4.0 divide_reduce_fusion.10
  83.1 2.7 fusion.141
  85.8 3.9 divide_reduce_fusion.9
  90.4 3.1 constant_dynamic-slice_fusion.6
  93.5 3.9 copy.82
  97.5 3.0 fusion.140
  100.8 0.6 copy-done.5
  101.4 3.8 fusion.143
  105.2 4.0 divide_reduce_fusion.11
  109.2 2.7 fusion.144
  111.9 4.6 %divide_reduce_fusion.12 = f32[4,1024]{1,0:T(4,128)} fusion(f32[4,256,1024]{2,1,0:T(8,128)} %fusion.144, bf16[256,4,64]{0,2,1:T(8,128)(2,1)S(1)} %bitcast.176, bf16[1024,4,64]{0,2,1:T(8,128)(2,1)S(1)} %bitcast.168), kind=kOutput, calls=%fused_computation.11.clone.1 | convolution fusion | flops 138409984 | bytes 4866048 | tf_op jit(solution)/shard_map/while/body/eval_jaxpr/div | solution.py:25
  116.5 0.7 broadcast_multiply_fusion.8
  117.2 2.7 fusion.142
  119.9 4.0 divide_reduce_fusion.10
  123.9 2.7 fusion.141
  126.6 3.9 divide_reduce_fusion.9
  131.3 1.6 copy.77
  132.9 2.5 fusion.39
  135.4 17.3 %reduce-scatter.3.cloned.1.call-done = f32[2,16,1,256]{3,1,0,2:T(8,128)} async-done(((f32[2,16,4,256]{3,1,0,2:T(8,128)}), f32[2,16,1,256]{3,1,0,2:T(8,128)}) %reduce-scatter.3.cloned.1.call-update) | async-done | bytes 32784 | tf_op jit(solution)/shard_map/reduce_scatter | solution.py:61
  152.6 1.5 convolution_convert_fusion
  154.1 2.3 convolution_bitcast_fusion
  156.5 5.9 %psum.42 = bf16[2,1024]{1,0:T(2,128)(2,1)S(1)} all-reduce(f32[2,1024]{1,0:T(2,128)S(1)} %reshape.98), channel_id=1, replica_groups=mesh['cam'=4,'clip'=8] {'cam'}, use_global_device_ids=true, to_apply=%region_11.12 | all-reduce | flops 2048 | bytes 12288 | tf_op jit(solution)/shard_map/psum | solution.py:71
  162.3 1.3 multiply_reduce_fusion.2
  163.7 20.7 %all-gather.1 = bf16[8,2,256]{2,1,0:T(2,128)(2,1)S(1)} all-gather(bf16[1,2,256]{2,1,0:T(2,128)(2,1)S(1)} %get-tuple-element.79), channel_id=1, replica_groups=mesh['cam'=4,'clip'=8] {'clip'}, dimensions={0}, use_global_device_ids=true | all-gather | bytes 9216 | tf_op jit(solution)/shard_map/all_gather | solution.py:90
  184.5 1.5 fusion.53
  186.2 36.9 %psum.43 = f32[16]{0:T(128)S(1)} all-reduce(f32[16]{0:T(128)S(1)} %get-tuple-element.68), channel_id=1, replica_groups=mesh['cam'=4,'clip'=8] {'cam','clip'}, use_global_device_ids=true, to_apply=%region_16.17 | all-reduce | flops 16 | bytes 128 | tf_op jit(solution)/shard_map/psum | solution.py:102
  223.4 41.5 %psum.44 = f32[16]{0:T(128)S(1)} all-reduce(f32[16]{0:T(128)S(1)} %fusion.48), channel_id=1, replica_groups=mesh['cam'=4,'clip'=8] {'cam','clip'}, use_global_device_ids=true, to_apply=%region_19.20 | all-reduce | flops 16 | bytes 128 | tf_op jit(solution)/shard_map/psum | solution.py:102
  265.3 39.2 %all-reduce.2 = (f32[16]{0:T(128)S(1)}, f32[16]{0:T(128)S(1)}) all-reduce(f32[16]{0:T(128)S(1)} %fusion.50, f32[16]{0:T(128)S(1)} %get-tuple-element.67), channel_id=1, replica_groups=mesh['cam'=4,'clip'=8] {'cam','clip'}, use_global_device_ids=true, to_apply=%region_22.23 | all-reduce | flops 32 | bytes 256 | tf_op jit(solution)/shard_map/psum | solution.py:102
  304.5 1.6 fusion.62
  306.1 1.8 multiply_reduce_fusion
  308.0 0.8 broadcast_multiply_fusion.4
  308.7 36.1 %all-reduce = f32[16,256]{1,0:T(8,128)S(1)} all-reduce(f32[16,256]{1,0:T(8,128)S(1)} %fusion.62), channel_id=4, replica_groups=mesh['cam'=4,'clip'=8] {'clip'}, use_global_device_ids=true, to_apply=%region_26.27.clone | all-reduce | flops 4096 | bytes 32768
  344.9 5.6 %psum.47 = f32[2,256]{1,0:T(2,128)S(1)} all-reduce(f32[2,256]{1,0:T(2,128)S(1)} %constant_dynamic-slice_fusion.2), channel_id=1, replica_groups=mesh['cam'=4,'clip'=8] {'cam'}, use_global_device_ids=true, to_apply=%region_27.28 | all-reduce | flops 512 | bytes 4096 | tf_op jit(solution)/shard_map/psum | solution.py:113
  350.7 1.3 fusion.71
  352.0 1.1 copy.58
  353.6 3.1 reduce
  356.7 0.9 reshape.120
  357.6 3.3 all-to-all-start
  361.0 3.4 subtract_divide_fusion
  364.4 20.9 %all-gather.3 = bf16[8,2,256]{2,1,0:T(2,128)(2,1)S(1)} all-gather(bf16[1,2,256]{2,1,0:T(2,128)(2,1)S(1)} %fusion.61), channel_id=1, replica_groups=mesh['cam'=4,'clip'=8] {'clip'}, dimensions={0}, use_global_device_ids=true | all-gather | bytes 9216 | tf_op jit(solution)/shard_map/all_gather | solution.py:125
  385.4 16.3 %all-gather.2 = bf16[8,2,256]{2,1,0:T(2,128)(2,1)S(1)} all-gather(bf16[1,2,256]{2,1,0:T(2,128)(2,1)S(1)} %bitcast.192), channel_id=1, replica_groups=mesh['cam'=4,'clip'=8] {'clip'}, dimensions={0}, use_global_device_ids=true | all-gather | bytes 9216 | tf_op jit(solution)/shard_map/all_gather | solution.py:126
  402.6 0.8 dynamic-slice_convert_fusion
  404.0 2.1 reshape.122
  406.1 3.3 all-to-all-start.1
  409.4 0.9 fusion.70
  410.3 5.8 %all-to-all-done.1 = f32[8,1,1024]{2,1,0:T(1,128)S(1)} async-done(((f32[8,1,1024]{2,1,0:T(1,128)}), f32[8,1,1024]{2,1,0:T(1,128)S(1)}, u32[]{:S(2)}, u32[]{:S(2)}) %all-to-all-start.1) | async-done | bytes 32800 | tf_op jit(solution)/shard_map/all_to_all | solution.py:77
  416.6 0.7 reduce.1
  417.3 1.6 reshape.123
  419.7 0.8 copy.64
  (92 shorter events, 9.4 us)
Async XLA Ops:
  7.2 1.6 copy-start
  7.2 42.4 %all-gather.6.cloned.1.call-start = ((), (), s32[]{:S(2)}) async-start(), calls=%async_computation.4 | async-start | bytes 5242880 | tf_op jit(solution)/shard_map/all_gather | solution.py:53
  12.2 4.1 copy-start.14
  12.2 4.7 %copy-start.13 = (u32[32]{0:T(128)S(1)}, u32[32]{0:T(128)}, u32[]{:S(2)}) copy-start(u32[32]{0:T(128)} %constant.53) | copy-start | bytes 388
  12.2 6.6 %copy-start.6 = (bf16[256,2048]{1,0:T(8,128)(2,1)S(1)}, bf16[256,2048]{1,0:T(8,128)(2,1)}, u32[]{:S(2)}) copy-start(bf16[256,2048]{1,0:T(8,128)(2,1)} %param.13) | copy-start | bytes 3145732
  12.2 140.4 %reduce-scatter.3.cloned.1.call-start = ((), (), s32[]{:S(2)}) async-start(), calls=%async_computation.3 | async-start | bytes 163840 | tf_op jit(solution)/shard_map/reduce_scatter | solution.py:61
  56.6 3.0 copy-start.8
  59.8 4.5 %copy-start.4 = (bf16[1024,256]{0,1:T(8,128)(2,1)S(1)}, bf16[1024,256]{0,1:T(8,128)(2,1)}, u32[]{:S(2)}) copy-start(bf16[1024,256]{0,1:T(8,128)(2,1)} %get-tuple-element.143) | copy-start | bytes 1572868 | tf_op jit(solution)/shard_map/while
  59.9 0.7 copy-start.5
  64.3 4.0 copy-start.3
  71.1 5.3 %copy-start.2 = (bf16[1024,256]{0,1:T(8,128)(2,1)S(1)}, bf16[1024,256]{0,1:T(8,128)(2,1)}, u32[]{:S(2)}) copy-start(bf16[1024,256]{0,1:T(8,128)(2,1)} %get-tuple-element.139) | copy-start | bytes 1572868 | tf_op jit(solution)/shard_map/while
  79.1 4.0 copy-start.1
  85.8 4.0 copy-start.10
  89.8 0.7 copy-start.11
  97.5 3.0 copy-start.8
  100.7 4.5 %copy-start.4 = (bf16[1024,256]{0,1:T(8,128)(2,1)S(1)}, bf16[1024,256]{0,1:T(8,128)(2,1)}, u32[]{:S(2)}) copy-start(bf16[1024,256]{0,1:T(8,128)(2,1)} %get-tuple-element.143) | copy-start | bytes 1572868 | tf_op jit(solution)/shard_map/while
  100.7 0.7 copy-start.5
  105.2 4.0 copy-start.3
  111.9 5.3 %copy-start.2 = (bf16[1024,256]{0,1:T(8,128)(2,1)S(1)}, bf16[1024,256]{0,1:T(8,128)(2,1)}, u32[]{:S(2)}) copy-start(bf16[1024,256]{0,1:T(8,128)(2,1)} %get-tuple-element.139) | copy-start | bytes 1572868 | tf_op jit(solution)/shard_map/while
  119.9 4.0 copy-start.1
  126.6 4.0 copy-start.10
  130.6 0.7 copy-start.11
  135.4 170.8 %copy-start.7 = (bf16[256,2048]{1,0:T(8,128)(2,1)S(1)}, bf16[256,2048]{1,0:T(8,128)(2,1)}, u32[]{:S(2)}) copy-start(bf16[256,2048]{1,0:T(8,128)(2,1)} %param.13) | copy-start | bytes 3145732
  135.4 170.8 %copy-start.12 = (f32[2048]{0:T(1024)S(1)}, f32[2048]{0:T(1024)}, u32[]{:S(2)}) copy-start(f32[2048]{0:T(1024)} %add_sqrt_fusion) | copy-start | bytes 24580
  154.1 69.3 %copy-start.9 = (bf16[2,16,1024]{2,1,0:T(8,128)(2,1)}, bf16[2,16,1024]{2,1,0:T(8,128)(2,1)S(1)}, u32[]{:S(2)}) copy-start(bf16[2,16,1024]{2,1,0:T(8,128)(2,1)S(1)} %convolution_convert_fusion) | copy-start | bytes 196612
  156.4 246.3 %all-reduce.5.cloned.1.call-start = ((), (), s32[]{:S(2)}) async-start(), calls=%async_computation.5 | async-start | bytes 131072
  357.6 44.0 %all-to-all-start = ((bf16[8,2,128]{2,1,0:T(2,128)(2,1)}), bf16[8,2,128]{2,1,0:T(2,128)(2,1)S(1)}, u32[]{:S(2)}, u32[]{:S(2)}) async-start(bf16[8,2,128]{2,1,0:T(2,128)(2,1)} %reshape.120), calls=%async_computation.1 | async-start | bytes 8192 | tf_op jit(solution)/shard_map/all_to_all | solution.py:78
  406.1 10.0 %all-to-all-start.1 = ((f32[8,1,1024]{2,1,0:T(1,128)}), f32[8,1,1024]{2,1,0:T(1,128)S(1)}, u32[]{:S(2)}, u32[]{:S(2)}) async-start(f32[8,1,1024]{2,1,0:T(1,128)} %reshape.122), calls=%async_computation.2 | async-start | bytes 65536 | tf_op jit(solution)/shard_map/all_to_all | solution.py:77
Sparse Core Ops, SparseCore 0:
  12.4 37.1 all-gather.5
  133.0 19.5 reduce-scatter.2
  223.5 31.6 all-reduce.4
where the time goes:
time: 428 us; the launch traced here: 427 us
  blocking collectives  223 us (52%)
  matrix products  77.1 us (18%)
  waiting for transfers between devices  48.6 us (11%)
  local copies, waits for them, and re-layouts  41.3 us (10%)
  between operations  15.2 us (4%)
  other arithmetic  14.7 us (3%)
  starting transfers between devices  6.73 us (2%)
    psum x3, blocking collectives, local(): row_total = lax.psum(jnp.sum(assign, axis=1), ('cam', 'clip'))  118 us
    unnamed x1, blocking collectives  36.1 us
    div x8, matrix products, column_sums(): probs = exponent_values / jnp.sum(exponent_values, axis=2, keepdims=True)  33 us
    all_gather x1, waiting for transfers between devices, local(): lax.all_gather(key_rows.reshape(clips, 1, TOK, D), 'cam', axis=1, tiled=T...  25.4 us
    dot_general x8, matrix products, column_sums(): jnp.einsum('ihe,jhe->hij', query_rows, key_rows, preferred_element_type=j...  23.8 us
    all_gather x1, blocking collectives, local(): lax.all_gather(head_block, 'clip', axis=0, tiled=True)  20.9 us
    all_gather x1, blocking collectives, local(): all_units = lax.all_gather(unit_b, 'clip', axis=0, tiled=True)  20.7 us
    reduce_scatter x1, waiting for transfers between devices, local(): lax.psum_scatter(partial_sums.reshape(clips, H, cameras, TOK), 'cam', sca...  17.3 us
  transfers between devices with their start and end apart: 5, of which 3 were waited for; matrix products, arithmetic and copies ran while one was open for 7% of the time, Pallas kernels for 0%

commit v1 on v0

v1 whole, which is shorter than its diff:
```python
import functools

import jax
import jax.numpy as jnp
from jax import lax
from jax.experimental import pallas as pl
from jax.experimental.pallas import tpu as pltpu
from jax.sharding import PartitionSpec as P

HD = 64
SINK_EPS = 0.05
SOFTMAX_TEMP = 0.1
NORM_EPS = 1e-06
LANES = 128
ALL = ("cam", "clip")
F32 = jnp.float32
BF16 = jnp.bfloat16


def pool_kernel(blocks, *refs):
    x_refs = refs[:blocks]
    wq_ref, wk_ref, wv_ref, pooled_ref, mix_ref, q_s, kt_s, w_s = refs[blocks:]
    tok = x_refs[0].shape[0]
    total = tok * blocks
    heads = mix_ref.shape[0]
    cols = heads * HD
    for c in range(blocks):
        x = x_refs[c][...]
        rows = slice(c * tok, (c + 1) * tok)
        q = jnp.dot(x, wq_ref[...], preferred_element_type=F32).astype(BF16)
        q_s[rows, :] = q * BF16(HD**-0.5)
        k = jnp.dot(x, wk_ref[...], preferred_element_type=F32).astype(BF16)
        kt_s[:, rows] = k.T
    lane = lax.broadcasted_iota(jnp.int32, (total, LANES), 1)

    @pl.loop(0, cols // LANES)
    def _(p):
        here = pl.ds(pl.multiple_of(p * LANES, LANES), LANES)
        q_pair = q_s[:, here]
        k_pair = kt_s[here, :]
        for e in range(LANES // HD):
            q_head = jnp.where(lane // HD == e, q_pair, BF16(0))
            s = jnp.dot(q_head, k_pair, preferred_element_type=F32)
            a = jnp.exp(s)
            a = a * (1.0 / jnp.sum(a, axis=1, keepdims=True))
            w = jnp.sum(a, axis=0, keepdims=True) * (1.0 / total)
            w_s[pl.ds(p * (LANES // HD) + e, 1), :] = w

    weights = w_s[...].astype(BF16)
    mixtures = []
    mix_sum = jnp.zeros(mix_ref.shape, F32)
    for c in range(blocks):
        m = jnp.dot(weights[:, c * tok : (c + 1) * tok], x_refs[c][...], preferred_element_type=F32)
        mixtures.append(m.astype(BF16).astype(F32))
        mix_sum = mix_sum + mixtures[-1]
    mix_ref[...] = mix_sum
    stacked = jnp.concatenate(mixtures, axis=0).astype(BF16)
    out = jnp.dot(stacked, wv_ref[...], preferred_element_type=F32)
    row_head = lax.broadcasted_iota(jnp.int32, out.shape, 0) % heads
    col_head = lax.broadcasted_iota(jnp.int32, out.shape, 1) // HD
    pooled_ref[...] = jnp.sum(jnp.where(row_head == col_head, out, 0.0), axis=0, keepdims=True)


def pool(blocks, wq, wk, wv):
    tok, d = blocks[0].shape
    cols = wq.shape[1]
    heads = cols // HD
    total = tok * len(blocks)
    return pl.pallas_call(
        functools.partial(pool_kernel, len(blocks)),
        out_shape=(
            jax.ShapeDtypeStruct((1, cols), F32),
            jax.ShapeDtypeStruct((heads, d), F32),
        ),
        in_specs=[pl.BlockSpec(memory_space=pltpu.VMEM)] * (len(blocks) + 3),
        out_specs=[pl.BlockSpec(memory_space=pltpu.VMEM)] * 2,
        scratch_shapes=[
            pltpu.VMEM((total, cols), BF16),
            pltpu.VMEM((cols, total), BF16),
            pltpu.VMEM((heads, total), F32),
        ],
        compiler_params=pltpu.CompilerParams(vmem_limit_bytes=52 * 2**20),
        cost_estimate=pl.CostEstimate(
            flops=2 * total * d * cols * 2 + 2 * total * total * cols,
            bytes_accessed=total * d * 2 + 3 * d * cols * 2,
            transcendentals=heads * total * total,
        ),
    )(*blocks, wq, wk, wv)


def gather_clip(tokens, n_cam):
    clips = tokens.shape[0]
    ranks = n_cam // clips
    group = lax.axis_index("cam") // ranks
    mine = lax.dynamic_index_in_dim(tokens, group, 0, keepdims=False)
    held = [mine]
    for s in range(1, clips):
        other = lax.dynamic_index_in_dim(tokens, (group + s) % clips, 0, keepdims=False)
        perm = [(i, ((i // ranks + s) % clips) * ranks + i % ranks) for i in range(n_cam)]
        held.append(lax.ppermute(other, "cam", perm))
    blocks = list(held)
    for t in range(1, ranks):
        perm = [(i, (i // ranks) * ranks + (i % ranks + t) % ranks) for i in range(n_cam)]
        blocks.extend(lax.ppermute(b, "cam", perm) for b in held)
    return blocks


def exchange(message):
    devices, length = message.shape
    padded = -(-length // LANES) * LANES
    message = jnp.pad(message, ((0, 0), (0, padded - length)))
    message = message.reshape(devices, padded // LANES, LANES)
    out = lax.all_to_all(message, ALL, split_axis=0, concat_axis=0, tiled=True)
    return out.reshape(devices, padded)[:, :length]


def tell_all(values, devices):
    return exchange(jnp.broadcast_to(values[None], (devices,) + values.shape))


def local(tokens, w_query, w_key, w_value, w_proj, prototypes):
    clips, _, tok, d = tokens.shape
    n_cam, n_clip = lax.axis_size("cam"), lax.axis_size("clip")
    devices = n_cam * n_clip
    ranks = n_cam // clips
    batch = clips * n_clip
    cols = d // ranks
    heads = cols // HD
    heads_here = heads // clips
    share = d // n_clip
    bottleneck = w_proj.shape[1]
    cam, clip = lax.axis_index("cam"), lax.axis_index("clip")
    rank = cam % ranks

    with jax.named_scope("prototypes"):
        proto_f = prototypes.astype(F32)
        column_norm = jnp.sqrt(jnp.sum(proto_f * proto_f, axis=0, keepdims=True) + NORM_EPS)
        unit_proto = proto_f / column_norm
        proto_b = unit_proto.astype(BF16)

    with jax.named_scope("pooling"):
        wq, wk, wv = (
            lax.dynamic_slice_in_dim(w, rank * cols, cols, 1) for w in (w_query, w_key, w_value)
        )
        blocks = gather_clip(tokens.reshape(clips, tok, d), n_cam)
        pooled, mix = pool(blocks, wq, wk, wv)

    with jax.named_scope("features_of_all_clips"):
        pooled_to = jnp.broadcast_to(pooled.astype(BF16), (devices, cols))
        mix_to = mix.astype(BF16).reshape(clips, heads_here, n_clip, share).transpose(0, 2, 1, 3)
        mix_to = mix_to.reshape(clips * n_clip, heads_here * share)
        mix_to = jnp.tile(mix_to, (ranks, 1))
        came = exchange(jnp.concatenate([pooled_to, mix_to], axis=1))
        came = came.reshape(clips, ranks, n_clip, cols + heads_here * share)
        pooled = came[..., :cols].transpose(2, 0, 1, 3).reshape(batch, d)
        mixed = lax.dynamic_index_in_dim(came[..., cols:], cam // clips, 1, keepdims=False)
        mixed = mixed.transpose(1, 0, 2).reshape(batch, heads_here, share)

    with jax.named_scope("logits"):
        embed = jnp.dot(pooled, w_proj, preferred_element_type=F32)
        embed_norm = jnp.sqrt(jnp.sum(embed * embed, axis=1, keepdims=True) + NORM_EPS)
        unit = embed / embed_norm
        unit_b = unit.astype(BF16)
        logits = jnp.dot(unit_b, proto_b, preferred_element_type=F32)
        exponents = jnp.exp(logits / SOFTMAX_TEMP)
        assign = jnp.exp(logits / SINK_EPS)
        prob_part = lax.dot_general(
            exponents.astype(BF16), proto_b, (((1,), (1,)), ((), ())), preferred_element_type=F32
        )
        prob_sum = jnp.sum(exponents, axis=1)

    with jax.named_scope("row_total_1"):
        assign = assign / jnp.sum(assign, axis=0, keepdims=True)
        piece = batch * bottleneck // devices
        sums = jnp.concatenate([jnp.sum(assign, axis=1), prob_sum])
        came = exchange(
            jnp.concatenate(
                [
                    prob_part.reshape(devices, piece),
                    jnp.broadcast_to(sums[None], (devices, 2 * batch)),
                ],
                axis=1,
            )
        )
        came = jnp.sum(came, axis=0)
        prob_piece, row_total, prob_total = (
            came[:piece],
            came[piece : piece + batch],
            came[piece + batch :],
        )
        assign = assign / row_total[:, None]

    with jax.named_scope("row_total_2"):
        assign = assign / jnp.sum(assign, axis=0, keepdims=True)
        came = tell_all(jnp.concatenate([prob_piece, jnp.sum(assign, axis=1)]), devices)
        prob_grad = came[:, :piece].reshape(batch, bottleneck)
        assign = assign / jnp.sum(came[:, piece:], axis=0)[:, None]

    with jax.named_scope("row_total_3"):
        assign = assign / jnp.sum(assign, axis=0, keepdims=True)
        assign_part = lax.dot_general(
            assign.astype(BF16), proto_b, (((1,), (1,)), ((), ())), preferred_element_type=F32
        )
        rest = jnp.sum(assign, axis=1)
        digits = []
        for _ in range(3):
            digits.append(lax.reduce_precision(rest, 8, 7))
            rest = rest - digits[-1]
        message = jnp.concatenate([assign_part.reshape(-1)] + digits).astype(BF16)
        came = jnp.sum(tell_all(message, devices).astype(F32), axis=0)
        assign_grad = came[: batch * bottleneck].reshape(batch, bottleneck)
        row_total = jnp.sum(came[batch * bottleneck :].reshape(3, batch), axis=0)
        assign = assign / row_total[:, None]

    protos = prototypes.shape[1] * devices
    with jax.named_scope("outputs"):
        grad_logits = (protos * (exponents / prob_total[:, None] - assign)).astype(BF16)
        codes = protos * assign
        grad_unit_proto = lax.dot_general(
            unit_b, grad_logits, (((0,), (0,)), ((), ())), preferred_element_type=F32
        )
        prototype_gradient = (
            grad_unit_proto
            - unit_proto * jnp.sum(unit_proto * grad_unit_proto, axis=0, keepdims=True)
        ) / column_norm
        grad_unit = protos * (prob_grad / prob_total[:, None] - assign_grad / row_total[:, None])
        grad_embed = (
            grad_unit - unit * jnp.sum(unit * grad_unit, axis=1, keepdims=True)
        ) / embed_norm
        grad_embed_b = grad_embed.astype(BF16)
        pooled_share = lax.dynamic_slice_in_dim(pooled, clip * share, share, 1)
        grad_proj = lax.dot_general(
            pooled_share, grad_embed_b, (((0,), (0,)), ((), ())), preferred_element_type=F32
        )
        width = heads_here * HD
        proj_rows = lax.dynamic_slice_in_dim(w_proj, cam * width, width, 0)
        grad_pooled = lax.dot_general(
            grad_embed_b, proj_rows, (((1,), (1,)), ((), ())), preferred_element_type=F32
        ).astype(BF16)
        grad_value = jnp.einsum(
            "bhd,bhe->dhe",
            mixed,
            grad_pooled.reshape(batch, heads_here, HD),
            preferred_element_type=F32,
        ).reshape(share, width)
    return (codes, prototype_gradient, grad_proj, grad_value)


def solution(mesh):
    in_specs = (P("clip", "cam", None, None), P(), P(), P(), P(), P(None, ALL))
    out_specs = (P(None, ALL), P(None, ALL), P("clip", None), P("clip", "cam"))
    return jax.shard_map(local, mesh=mesh, in_specs=in_specs, out_specs=out_specs, check_vma=False)
```

time: 428 us -> 98.3 us (0.23)
  blocking collectives: 223 us -> 17.9 us
  matrix products: 77.1 us -> 7.67 us
  local copies, waits for them, and re-layouts: 41.3 us -> 10.3 us
  waiting for transfers between devices: 48.6 us -> 27.5 us
  between operations: 15.2 us -> 0.96 us
  Pallas kernels: 0 us -> 13.3 us
  other arithmetic: 14.7 us -> 7.87 us
  starting transfers between devices: 6.73 us -> 12.3 us
    psum x5 -> x0, blocking collectives: 129 us -> none  [the longest x3 118 us: local(): row_total = lax.psum(jnp.sum(assign, axis=1), ('cam', 'clip'))]
    all_gather x3 -> x0, blocking collectives: 57.9 us -> none  [the longest x1 20.9 us: local(): lax.all_gather(head_block, 'clip', axis=0, tiled=True)]
    dot_general x19 -> x8, matrix products: 44.1 us -> 7.67 us  [the longest x1 1.85 us: local(): lax.dot_general(unit_b, grad_logits, (((0,), (0,)), ((), ())), preferred_...]
    unnamed x1 -> x0, blocking collectives: 36.1 us -> none
    div x8 -> x0, matrix products: 33 us -> none  [column_sums(): probs = exponent_values / jnp.sum(exponent_values, axis=2, keepdims=True)]
    all_gather x1 -> x0, waiting for transfers between devices: 25.4 us -> none  [local(): lax.all_gather(key_rows.reshape(clips, 1, TOK, D), 'cam', axis=1, tiled=T...]
    all_to_all x0 -> x2, blocking collectives: none -> 17.9 us  [exchange(): out = lax.all_to_all(message, ALL, split_axis=0, concat_axis=0, tiled=True)]
    reduce_scatter x1 -> x0, waiting for transfers between devices: 17.3 us -> none  [local(): lax.psum_scatter(partial_sums.reshape(clips, H, cameras, TOK), 'cam', sca...]
  transfers between devices with their start and end apart: 5 -> 5, of which waited for: 3 -> 4; matrix products, arithmetic and copies ran while one was open for 7% -> 6% of each run, Pallas kernels for 0% -> 0%
where the time goes in v1:
time: 98.3 us; the launch traced here: 97.8 us
  waiting for transfers between devices  27.5 us (28%)
  blocking collectives  17.9 us (18%)
  Pallas kernels  13.3 us (14%)
  starting transfers between devices  12.3 us (13%)
  local copies, waits for them, and re-layouts  10.3 us (10%)
  other arithmetic  7.87 us (8%)
  matrix products  7.67 us (8%)
    all_to_all x2, blocking collectives, exchange(): out = lax.all_to_all(message, ALL, split_axis=0, concat_axis=0, tiled=True)  17.9 us
    all_to_all x2, waiting for transfers between devices, exchange(): out = lax.all_to_all(message, ALL, split_axis=0, concat_axis=0, tiled=True)  17.8 us
    pallas_call x1, Pallas kernels, pool(): pl.pallas_call(functools.partial(pool_kernel, len(blocks)), out_shape=(ja...  13.3 us
    all_to_all x2, starting transfers between devices, exchange(): out = lax.all_to_all(message, ALL, split_axis=0, concat_axis=0, tiled=True)  9.4 us
    ppermute x1, waiting for transfers between devices, gather_clip(): held.append(lax.ppermute(other, 'cam', perm))  9.1 us
    dynamic_slice x2, local copies, waits for them, and re-layouts, local(): lax.dynamic_slice_in_dim(w, rank * cols, cols, 1)  4.1 us
    div x1, other arithmetic, local(): (grad_unit_proto - unit_proto * jnp.sum(unit_proto * grad_unit_proto, axi...  3.41 us
    ppermute x1, starting transfers between devices, gather_clip(): held.append(lax.ppermute(other, 'cam', perm))  2.94 us
  transfers between devices with their start and end apart: 5, of which 4 were waited for; matrix products, arithmetic and copies ran while one was open for 6% of the time, Pallas kernels for 0%

profile of v1, /device:TPU:0, one launch (start us, length us, event | category | flops | bytes accessed | tf_op | source)
XLA Modules:
  0.0 97.8 jit_solution(8078565335735258230)
XLA Ops:
  0.6 0.0 copy-start
  0.7 2.2 %dynamic-slice_bitcast_fusion = (bf16[256,1024]{1,0:T(8,128)(2,1)}, bf16[256,1024]{1,0:T(8,128)(2,1)S(1)}) fusion(bf16[2,1,256,1024]{3,2,1,0:T(8,128)(2,1)} %param.6, s32[]{:T(128)S(6)} %select_n.39, s32[]{:T(128)S(6)} %select_n.37), kind=kLoop, calls=%fused_computation.10 | loop fusion | bytes 2097160 | tf_op jit(solution)/shard_map/pooling/jit(dynamic_index_in_dim)/squeeze | solution.py:98
  2.9 2.9 %collective-permute-start = (bf16[256,1024]{1,0:T(8,128)(2,1)}, bf16[256,1024]{1,0:T(8,128)(2,1)S(1)}, u32[]{:S(2)}, u32[]{:S(2)}) collective-permute-start(bf16[256,1024]{1,0:T(8,128)(2,1)} %get-tuple-element.24), channel_id=1, source_target_pairs={{0,16},{8,24},{16,0},{24,8},{1,17},{9,25},{17,1},{25,9},{2,18},{10... | collective-permute-start | bytes 1572872 | tf_op jit(solution)/shard_map/pooling/ppermute | solution.py:100
  5.8 0.0 collective-permute-start.1
  5.8 3.0 %constant_dynamic-slice_fusion = (bf16[1024,512]{1,0:T(8,128)(2,1)}, bf16[1024,512]{1,0:T(8,128)(2,1)}) fusion(bf16[1024,1024]{1,0:T(8,128)(2,1)} %param.9, s32[]{:T(128)S(6)} %select_n.41, bf16[1024,1024]{1,0:T(8,128)(2,1)} %param.8), kind=kLoop, calls=%fused_computation.68 | loop fusion | bytes 4194308 | tf_op jit(solution)/shard_map/pooling/dynamic_slice | solution.py:143
  8.9 0.0 copy-start.1
  8.9 9.1 %collective-permute-done.refs_1_ = bf16[256,1024]{1,0:T(8,128)(2,1)S(1)} collective-permute-done((bf16[256,1024]{1,0:T(8,128)(2,1)}, bf16[256,1024]{1,0:T(8,128)(2,1)S(1)}, u32[]{:S(2)}, u32[]{:S(2)}) %collective-permute-start) | collective-permute-done | bytes 524320 | tf_op jit(solution)/shard_map/pooling/ppermute | solution.py:100
  18.0 0.0 collective-permute-start.2
  18.0 0.0 copy-done
  18.0 1.1 %constant_dynamic-slice_fusion.2.refs_4_ = bf16[1024,512]{1,0:T(8,128)(2,1)} fusion(bf16[1024,1024]{1,0:T(8,128)(2,1)S(1)} %copy-done, s32[]{:T(128)S(6)} %select_n.41), kind=kLoop, calls=%fused_computation.70 | loop fusion | bytes 2097156 | tf_op jit(solution)/shard_map/pooling/dynamic_slice | solution.py:143
  19.0 0.0 copy-done.1
  19.0 0.2 fusion
  19.3 0.0 collective-permute-done.1.refs_2_
  19.3 0.6 collective-permute-done.2.refs_3_
  19.9 0.0 copy-start.4
  19.9 0.8 copy-done.4
  20.7 13.3 %pooling.1 = (f32[1,512]{1,0:T(1,128)S(1)}, f32[8,1024]{1,0:T(8,128)S(1)}) custom-call(bf16[256,1024]{1,0:T(8,128)(2,1)S(1)} %get-tuple-element.25.refs_0_, bf16[256,1024]{1,0:T(8,128)(2,1)S(1)} %collective-permute-done.refs_1_, bf16[256,1024]{1,0:T(8,128)(2,1)} %collective-permute-done.1.refs_2_, bf16[256,1024]{1,0:T(8,128)(2,1)} %copy-done.4, ...), custom_call_target="tpu_custom_call" | custom-call | flops 3221225472 | bytes 5242880 | tf_op jit(solution)/shard_map/pooling/pallas_call | solution.py:69
  34.1 0.7 pad_maximum_fusion
  34.8 6.1 %all-to-all-start = ((bf16[32,8,128]{2,1,0:T(8,128)(2,1)}), bf16[32,8,128]{2,1,0:T(8,128)(2,1)S(1)}, u32[]{:S(2)}, u32[]{:S(2)}) async-start(bf16[32,8,128]{2,1,0:T(8,128)(2,1)} %pad_maximum_fusion), calls=%async_computation | async-start | bytes 131072 | tf_op jit(solution)/shard_map/features_of_all_clips/all_to_all | solution.py:113
  40.9 1.5 %fusion.2 = bf16[256,2048]{1,0:T(8,128)(2,1)S(1)} fusion(f32[2048]{0:T(1024)S(1)} %add_sqrt_fusion, bf16[256,2048]{1,0:T(8,128)(2,1)} %param.11), kind=kLoop, calls=%fused_computation.8 | loop fusion | flops 1572864 | bytes 2105344 | tf_op jit(solution)/shard_map/prototypes/convert_element_type | solution.py:139
  42.4 0.0 copy-start.3
  42.4 5.8 %all-to-all-done = bf16[32,8,128]{2,1,0:T(8,128)(2,1)S(1)} async-done(((bf16[32,8,128]{2,1,0:T(8,128)(2,1)}), bf16[32,8,128]{2,1,0:T(8,128)(2,1)S(1)}, u32[]{:S(2)}, u32[]{:S(2)}) %all-to-all-start) | async-done | bytes 65568 | tf_op jit(solution)/shard_map/features_of_all_clips/all_to_all | solution.py:113
  48.3 1.3 %multiply_reduce_fusion.2 = (f32[16]{0:T(128)S(1)}, f32[16,256]{1,0:T(8,128)S(1)}) fusion(bf16[16,1024]{1,0:T(8,128)(2,1)S(1)} %bitcast.51, bf16[1024,256]{1,0:T(8,128)(2,1)} %param.10), kind=kOutput, calls=%fused_computation.55 | convolution fusion | flops 8396784 | bytes 573504 | tf_op jit(solution)/shard_map/logits/dot_general | solution.py:160
  49.6 0.3 fusion.24
  49.9 0.4 fusion.16
  50.3 0.2 divide_reduce_fusion
  50.5 0.1 pad_maximum_fusion.2
  50.6 8.9 %all_to_all.20 = f32[32,2,128]{2,1,0:T(2,128)S(1)} all-to-all(f32[32,2,128]{2,1,0:T(2,128)S(1)} %reshape.143), channel_id=1, replica_groups=mesh['cam'=4,'clip'=8] {'cam','clip'}, dimensions={0} | all-to-all | bytes 65536 | tf_op jit(solution)/shard_map/row_total_1/all_to_all | solution.py:113
  59.5 0.1 fusion.45
  59.6 0.1 fusion.11
  59.7 0.2 fusion.12
  59.9 0.0 copy-done.3
  60.0 0.0 copy-start.2
  60.0 9.0 %all_to_all.21 = f32[32,2,128]{2,1,0:T(2,128)S(1)} all-to-all(f32[32,2,128]{2,1,0:T(2,128)S(1)} %pad.23), channel_id=1, replica_groups=mesh['cam'=4,'clip'=8] {'cam','clip'}, dimensions={0} | all-to-all | bytes 65536 | tf_op jit(solution)/shard_map/row_total_2/all_to_all | solution.py:113
  69.0 0.1 fusion.13
  69.1 0.2 fusion.42
  69.4 1.6 %fusion.1 = bf16[2,2,8,128]{3,2,1,0:T(8,128)(2,1)S(1)} fusion(bf16[256,2048]{1,0:T(8,128)(2,1)} %copy-done.3, f32[2048]{0:T(1024)S(1)} %fusion.13, f32[16]{0:T(128)S(1)} %slice_reduce_fusion.1, f32[2048]{0:T(1024)S(1)} %fusion.11, f32[16]{0:T(128)S(1)} %get-tuple-element.29, f32[2048]{0:T(1024)S(1)} %get-tuple-element.35, f32[16,2048]{1,0:T(8,128)S(1)} %get-tuple-element.36), kind=kOutput, calls=%fused_computation.7 | convolution fusion | flops 17010688 | bytes 1212544 | tf_op jit(solution)/shard_map/row_total_3/dot_general | solution.py:201
  71.0 0.1 concatenate.31
  71.1 0.8 pad.26
  71.9 3.3 %all-to-all-start.3 = ((bf16[32,33,128]{2,1,0:T(8,128)(2,1)}), bf16[32,33,128]{2,1,0:T(8,128)(2,1)}, u32[]{:S(2)}, u32[]{:S(2)}) async-start(bf16[32,33,128]{2,1,0:T(8,128)(2,1)} %pad.26), calls=%async_computation.3 | async-start | bytes 655360 | tf_op jit(solution)/shard_map/row_total_3/all_to_all | solution.py:113
  75.3 12.0 %all-to-all-done.3 = bf16[32,33,128]{2,1,0:T(8,128)(2,1)} async-done(((bf16[32,33,128]{2,1,0:T(8,128)(2,1)}), bf16[32,33,128]{2,1,0:T(8,128)(2,1)}, u32[]{:S(2)}, u32[]{:S(2)}) %all-to-all-start.3) | async-done | bytes 270368 | tf_op jit(solution)/shard_map/row_total_3/all_to_all | solution.py:113
  87.3 1.0 %copy.33 = bf16[4,8,33,128]{3,1,2,0:T(8,128)(2,1)S(1)} copy(bf16[4,8,33,128]{3,2,1,0:T(8,128)(2,1)} %bitcast.27) | data formatting | bytes 540672
  88.3 0.1 convert_reduce_fusion
  88.4 0.1 reshape.147
  88.6 0.8 broadcast_multiply_fusion
  89.3 0.0 copy-done.2
  89.3 1.9 %multiply_reduce_fusion = (f32[2048]{0:T(1024)S(1)}, f32[256,2048]{1,0:T(8,128)}) fusion(f32[2048]{0:T(1024)S(1)} %add_sqrt_fusion, bf16[256,2048]{1,0:T(8,128)(2,1)S(1)} %copy-done.2, f32[16,2048]{1,0:T(8,128)S(1)} %get-tuple-element.36, f32[16]{0:T(128)S(1)} %get-tuple-element.28, f32[16]{0:T(128)S(1)} %reduce_sum.147, f32[2048]{0:T(1024)S(1)} %fusion.13, ...), kind=kOutput, calls=%fused_computation.4 | convolution fusion | flops 19273728 | bytes 3334464 | tf_op jit(solution)/shard_map/outputs/dot_general | solution.py:219
  91.2 0.2 multiply_reduce_fusion.1
  91.4 1.1 %convolution_convert_fusion = bf16[16,256]{1,0:T(8,128)(2,1)S(1)} fusion(bf16[1024,256]{1,0:T(8,128)(2,1)} %param.10, s32[]{:T(128)S(6)} %select_n.43, f32[16,256]{1,0:T(8,128)S(1)} %get-tuple-element.23, f32[16]{0:T(128)S(1)} %get-tuple-element.22, f32[16]{0:T(128)S(1)} %add_sqrt_fusion.1, f32[16,256]{1,0:T(8,128)S(1)} %get-tuple-element.34), kind=kOutput, calls=%fused_computation.5 | convolution fusion | flops 2121728 | bytes 172164 | tf_op jit(solution)/shard_map/outputs/dot_general | solution.py:237
  92.5 0.1 reshape.150
  92.6 0.2 fusion.25
  92.8 0.8 copy.19
  93.5 0.9 fusion.28
  94.4 3.4 %subtract_divide_fusion = f32[256,2048]{1,0:T(8,128)} fusion(f32[256,2048]{1,0:T(8,128)} %get-tuple-element.38, f32[2048]{0:T(1024)S(1)} %get-tuple-element.37, f32[2048]{0:T(1024)S(1)} %add_sqrt_fusion, bf16[256,2048]{1,0:T(8,128)(2,1)S(1)} %copy-done.2), kind=kLoop, calls=%fused_computation.3 | loop fusion | flops 2621440 | bytes 5259264 | tf_op jit(solution)/shard_map/outputs/div | solution.py:222
  (35 shorter events, 0.4 us)
Async XLA Ops:
  0.6 17.3 %copy-start = (bf16[1024,1024]{1,0:T(8,128)(2,1)S(1)}, bf16[1024,1024]{1,0:T(8,128)(2,1)}, u32[]{:S(2)}) copy-start(bf16[1024,1024]{1,0:T(8,128)(2,1)} %param.7) | copy-start | bytes 6291460
  2.9 15.1 %collective-permute-start = (bf16[256,1024]{1,0:T(8,128)(2,1)}, bf16[256,1024]{1,0:T(8,128)(2,1)S(1)}, u32[]{:S(2)}, u32[]{:S(2)}) collective-permute-start(bf16[256,1024]{1,0:T(8,128)(2,1)} %get-tuple-element.24), channel_id=1, source_target_pairs={{0,16},{8,24},{16,0},{24,8},{1,17},{9,25},{17,1},{25,9},{2,18},{10... | collective-permute-start | bytes 1572872 | tf_op jit(solution)/shard_map/pooling/ppermute | solution.py:100
  5.8 13.5 %collective-permute-start.1 = (bf16[256,1024]{1,0:T(8,128)(2,1)S(1)}, bf16[256,1024]{1,0:T(8,128)(2,1)}, u32[]{:S(2)}, u32[]{:S(2)}) collective-permute-start(bf16[256,1024]{1,0:T(8,128)(2,1)S(1)} %get-tuple-element.25.refs_0_), channel_id=1, source_target_pairs={{0,8},{8,0},{16,24},{24,16},{1,9},{9,1},{17,25},{25,17},{2,10},{10... | collective-permute-start | bytes 1572872 | tf_op jit(solution)/shard_map/pooling/ppermute | solution.py:104
  8.9 10.2 %copy-start.1 = (bf16[256,2048]{1,0:T(8,128)(2,1)S(1)}, bf16[256,2048]{1,0:T(8,128)(2,1)}, u32[]{:S(2)}) copy-start(bf16[256,2048]{1,0:T(8,128)(2,1)} %param.11) | copy-start | bytes 3145732
  18.0 1.9 %collective-permute-start.2 = (bf16[256,1024]{1,0:T(8,128)(2,1)S(1)}, bf16[256,1024]{1,0:T(8,128)(2,1)S(1)}, u32[]{:S(2)}, u32[]{:S(2)}) collective-permute-start(bf16[256,1024]{1,0:T(8,128)(2,1)S(1)} %collective-permute-done.refs_1_), channel_id=1, source_target_pairs={{0,8},{8,0},{16,24},{24,16},{1,9},{9,1},{17,25},{25,17},{2,10},{10... | collective-permute-start | bytes 1572872 | tf_op jit(solution)/shard_map/pooling/ppermute | solution.py:104
  19.9 0.8 copy-start.4
  34.8 13.4 %all-to-all-start = ((bf16[32,8,128]{2,1,0:T(8,128)(2,1)}), bf16[32,8,128]{2,1,0:T(8,128)(2,1)S(1)}, u32[]{:S(2)}, u32[]{:S(2)}) async-start(bf16[32,8,128]{2,1,0:T(8,128)(2,1)} %pad_maximum_fusion), calls=%async_computation | async-start | bytes 131072 | tf_op jit(solution)/shard_map/features_of_all_clips/all_to_all | solution.py:113
  42.4 17.6 %copy-start.3 = (bf16[256,2048]{1,0:T(8,128)(2,1)}, bf16[256,2048]{1,0:T(8,128)(2,1)S(1)}, u32[]{:S(2)}) copy-start(bf16[256,2048]{1,0:T(8,128)(2,1)S(1)} %fusion.2) | copy-start | bytes 3145732
  60.0 29.4 %copy-start.2 = (bf16[256,2048]{1,0:T(8,128)(2,1)S(1)}, bf16[256,2048]{1,0:T(8,128)(2,1)}, u32[]{:S(2)}) copy-start(bf16[256,2048]{1,0:T(8,128)(2,1)} %param.11) | copy-start | bytes 3145732
  71.9 15.4 %all-to-all-start.3 = ((bf16[32,33,128]{2,1,0:T(8,128)(2,1)}), bf16[32,33,128]{2,1,0:T(8,128)(2,1)}, u32[]{:S(2)}, u32[]{:S(2)}) async-start(bf16[32,33,128]{2,1,0:T(8,128)(2,1)} %pad.26), calls=%async_computation.3 | async-start | bytes 655360 | tf_op jit(solution)/shard_map/row_total_3/all_to_all | solution.py:113

commit v2 on v1

v2 whole, which is shorter than its diff:
```python
import functools

import jax
import jax.numpy as jnp
from jax import lax
from jax.experimental import pallas as pl
from jax.experimental.pallas import tpu as pltpu
from jax.sharding import PartitionSpec as P

HD = 64
SINK_EPS = 0.05
SOFTMAX_TEMP = 0.1
NORM_EPS = 1e-06
LANES = 128
DIGITS = 3
CHUNKS = 2
ALL = ("cam", "clip")
F32 = jnp.float32
BF16 = jnp.bfloat16
TRANSPOSED = (((1,), (1,)), ((), ()))
OUTER = (((0,), (0,)), ((), ()))
WHOLE = pl.BlockSpec(memory_space=pltpu.VMEM)
SCALARS = pl.BlockSpec(memory_space=pltpu.SMEM)


def call(kernel, outs, ins, flops, extra=0, scratch=(), grid=None, out_specs=None, in_specs=None):
    moved = sum(a.size * a.dtype.itemsize for a in ins)
    return pl.pallas_call(
        kernel,
        out_shape=tuple(jax.ShapeDtypeStruct(*o) for o in outs),
        in_specs=in_specs or [WHOLE] * len(ins),
        out_specs=out_specs or [WHOLE] * len(outs),
        scratch_shapes=list(scratch),
        grid=grid or (),
        compiler_params=pltpu.CompilerParams(vmem_limit_bytes=52 * 2**20),
        cost_estimate=pl.CostEstimate(flops=flops, bytes_accessed=moved, transcendentals=extra),
    )(*ins)


def project(x, wq, wk, wv):
    q = jnp.dot(x, wq, preferred_element_type=F32).astype(BF16) * BF16(HD**-0.5)
    kt = jnp.dot(x, wk, preferred_element_type=F32).astype(BF16).T
    v = jnp.dot(x, wv, preferred_element_type=F32).astype(BF16)
    return q, kt, v


def project_kernel(blocks, *refs):
    wq, wk, wv = refs[blocks : blocks + 3]
    q_ref, kt_ref, v_ref = refs[blocks + 3 :]
    at = 0
    for x_ref in refs[:blocks]:
        rows = slice(at, at + x_ref.shape[0])
        at += x_ref.shape[0]
        q_ref[rows, :], kt_ref[:, rows], v_ref[rows, :] = project(
            x_ref[...], wq[...], wk[...], wv[...]
        )


def project_blocks(blocks, weights):
    d, cols = weights[0].shape
    rows = sum(b.shape[0] for b in blocks)
    return call(
        functools.partial(project_kernel, len(blocks)),
        [((rows, cols), BF16), ((cols, rows), BF16), ((rows, cols), BF16)],
        [*blocks, *weights],
        2 * rows * d * cols * 3,
    )


def pool_kernel(parts, late, *refs):
    early = [refs[3 * i : 3 * i + 3] for i in range(parts)]
    refs = refs[3 * parts :]
    x_refs, (wq, wk, wv, wp) = refs[:late], refs[late : late + 4]
    weight_ref, pooled_ref, embed_ref, q_s, kt_s, v_s, w_s = refs[late + 4 :]
    project_kernel(late, *x_refs, wq, wk, wv, q_s, kt_s, v_s)
    pieces = early + [(q_s, kt_s, v_s)]
    heads, total = w_s.shape
    cols = heads * HD
    lane = lax.broadcasted_iota(jnp.int32, (total, LANES), 1)

    @pl.loop(0, cols // LANES)
    def _(p):
        here = pl.ds(pl.multiple_of(p * LANES, LANES), LANES)
        q_pair = jnp.concatenate([q[:, here] for q, _, _ in pieces], axis=0)
        k_pair = jnp.concatenate([kt[here, :] for _, kt, _ in pieces], axis=1)
        for e in range(LANES // HD):
            q_head = jnp.where(lane // HD == e, q_pair, BF16(0))
            a = jnp.exp(jnp.dot(q_head, k_pair, preferred_element_type=F32))
            a = a * (1.0 / jnp.sum(a, axis=1, keepdims=True))
            w = jnp.sum(a, axis=0, keepdims=True) * (1.0 / total)
            w_s[pl.ds(p * (LANES // HD) + e, 1), :] = w

    weights = w_s[...].astype(BF16)
    weight_ref[...] = weights
    out, at = jnp.zeros((heads, cols), F32), 0
    for _, _, v in pieces:
        rows = slice(at, at + v.shape[0])
        at += v.shape[0]
        out = out + jnp.dot(weights[:, rows], v[...], preferred_element_type=F32)
    row_head = lax.broadcasted_iota(jnp.int32, out.shape, 0)
    col_head = lax.broadcasted_iota(jnp.int32, out.shape, 1) // HD
    pooled = jnp.sum(jnp.where(row_head == col_head, out, 0.0), axis=0, keepdims=True)
    pooled_ref[...] = pooled
    pooled_b = jnp.broadcast_to(pooled, (8, cols)).astype(BF16)
    embed = jnp.dot(pooled_b, wp[...], preferred_element_type=F32)[:1]
    for i in range(embed_ref.shape[0]):
        embed_ref[i : i + 1, :] = embed[:, i * LANES : (i + 1) * LANES]


def pool(parts, late, weights, wp):
    d, cols = weights[0].shape
    heads = cols // HD
    fresh = sum(b.shape[0] for b in late)
    total = fresh + sum(q.shape[0] for q, _, _ in parts)
    bottleneck = wp.shape[1]
    ins = [a for part in parts for a in part] + [*late, *weights, wp]
    return call(
        functools.partial(pool_kernel, len(parts), len(late)),
        [((heads, total), BF16), ((1, cols), F32), ((bottleneck // LANES, LANES), F32)],
        ins,
        2 * fresh * d * cols * 3 + 2 * total * total * cols * 4,
        heads * total * total,
        scratch=[
            pltpu.VMEM((fresh, cols), BF16),
            pltpu.VMEM((cols, fresh), BF16),
            pltpu.VMEM((fresh, cols), BF16),
            pltpu.VMEM((heads, total), F32),
        ],
    )


def mixture_kernel(cameras, w_ref, *refs):
    x_refs, out_ref = refs[:-1], refs[-1]
    mix = jnp.zeros(out_ref.shape, F32)
    for camera in cameras:
        m = jnp.zeros(out_ref.shape, F32)
        for block, at in camera:
            w = w_ref[:, at : at + x_refs[block].shape[0]]
            m = m + jnp.dot(w, x_refs[block][...], preferred_element_type=F32)
        mix = mix + m.astype(BF16).astype(F32)
    out_ref[...] = mix


def gather_clip(tokens, n_cam):
    clips, tok, _ = tokens.shape
    ranks = n_cam // clips
    group = lax.axis_index("cam") // ranks
    size = tok // CHUNKS
    held = [[] for _ in range(CHUNKS + 1)]
    for c in range(CHUNKS):
        for s in range(1, clips):
            start = ((group + s) % clips, c * size, 0)
            sent = lax.dynamic_slice(tokens, start, (1, size, tokens.shape[2]))[0]
            perm = [(i, ((i // ranks + s) % clips) * ranks + i % ranks) for i in range(n_cam)]
            held[c + 1].append((s * ranks, lax.ppermute(sent, "cam", perm)))
    held[0].append((0, lax.dynamic_index_in_dim(tokens, group, 0, keepdims=False)))
    stages = []
    for blocks in held:
        stage = list(blocks)
        for t in range(1, ranks):
            perm = [(i, (i // ranks) * ranks + (i % ranks + t) % ranks) for i in range(n_cam)]
            stage.extend((camera + t, lax.ppermute(b, "cam", perm)) for camera, b in blocks)
        stages.append(stage)
    return stages


def to_lanes(column, offset=0):
    shape = (column.shape[0], LANES)
    row = lax.broadcasted_iota(jnp.int32, shape, 0) + offset
    lane = lax.broadcasted_iota(jnp.int32, shape, 1)
    return jnp.sum(jnp.where(lane == row, column, 0.0), axis=0, keepdims=True)


def from_lanes(line, size, offset=0):
    row = lax.broadcasted_iota(jnp.int32, (size, LANES), 0) + offset
    lane = lax.broadcasted_iota(jnp.int32, (size, LANES), 1)
    return jnp.sum(jnp.where(lane == row, line, 0.0), axis=1, keepdims=True)


def spread(column):
    return jnp.broadcast_to(column, (column.shape[0], LANES))


def exchange(message):
    return lax.all_to_all(message, ALL, split_axis=0, concat_axis=0, tiled=True)


def logits_kernel(
    clips, ranks, n_clip, came, proto, proto_t, unit_ref, norm_ref, exp_ref, assign_ref, message
):
    rows = []
    for g in range(clips):
        for p in range(n_clip):
            z = sum(came[(g * ranks + r) * n_clip + p] for r in range(ranks))
            rows.append(jnp.concatenate([z[i : i + 1] for i in range(z.shape[0])], axis=1))
    embed = jnp.concatenate(rows, axis=0)
    norm = jnp.sqrt(jnp.sum(embed * embed, axis=1, keepdims=True) + NORM_EPS)
    unit = embed / norm
    unit_ref[...] = unit
    norm_ref[...] = spread(norm)
    logits = jnp.dot(unit.astype(BF16), proto[...], preferred_element_type=F32)
    exponents = jnp.exp(logits / SOFTMAX_TEMP)
    assign = jnp.exp(logits / SINK_EPS)
    exp_ref[...] = exponents
    assign = assign / jnp.sum(assign, axis=0, keepdims=True)
    assign_ref[...] = assign
    part = jnp.dot(exponents.astype(BF16), proto_t[...], preferred_element_type=F32)
    batch = part.shape[0]
    line = to_lanes(jnp.sum(assign, axis=1, keepdims=True)) + to_lanes(
        jnp.sum(exponents, axis=1, keepdims=True), batch
    )
    halves = part.shape[1] // LANES
    for i in range(message.shape[0]):
        if i < halves * batch:
            h, b = divmod(i, batch)
            piece = part[b : b + 1, h * LANES : (h + 1) * LANES]
        else:
            piece = jnp.zeros((1, LANES), F32)
        message[i] = jnp.concatenate([piece, line], axis=0)


def second_kernel(came, assign_ref, assign_out, message, total_ref):
    batch = assign_ref.shape[0]
    came = jnp.sum(came[...], axis=0)
    total_ref[...] = spread(from_lanes(came[1:2], batch, batch))
    assign = assign_ref[...] / from_lanes(came[1:2], batch)
    assign = assign / jnp.sum(assign, axis=0, keepdims=True)
    assign_out[...] = assign
    line = to_lanes(jnp.sum(assign, axis=1, keepdims=True))
    out = jnp.concatenate([came[0:1], line], axis=0)
    for i in range(message.shape[0]):
        message[i] = out


def third_kernel(
    parity, came, assign_ref, proto_t, assign_out, keep_ref, send_ref, digits_ref, grad_ref
):
    batch = assign_ref.shape[0]
    halves = proto_t.shape[1] // LANES
    total = jnp.sum(came[...], axis=0)[1:2]
    assign = assign_ref[...] / from_lanes(total, batch)
    assign = assign / jnp.sum(assign, axis=0, keepdims=True)
    assign_out[...] = assign
    part = jnp.dot(assign.astype(BF16), proto_t[...], preferred_element_type=F32)
    half = part.shape[1] // 2
    odd = parity[0] == 1
    low, high = part[:, :half], part[:, half:]
    keep_ref[...] = jnp.where(odd, high, low)
    send_ref[...] = jnp.where(odd, low, high)
    rest = to_lanes(jnp.sum(assign, axis=1, keepdims=True))
    digits_ref[...] = jnp.zeros(digits_ref.shape, F32)
    for i in range(DIGITS):
        digit = rest.astype(BF16).astype(F32)
        digits_ref[i : i + 1, :] = digit
        rest = rest - digit
    for h in range(halves):
        for b in range(batch):
            grad_ref[b : b + 1, h * LANES : (h + 1) * LANES] = came[h * batch + b][0:1]


def message_kernel(keep, got, digits, side, message):
    part = (keep[...] + got[...]).astype(BF16)
    batch = part.shape[0]
    message[:, :batch, :] = jnp.broadcast_to(part[None], (message.shape[0],) + part.shape)
    message[:, batch:, :] = (side[...] + digits[...][None]).astype(BF16)


def output_kernel(
    protos,
    n_cam,
    pick,
    came,
    unit_ref,
    norm_ref,
    exp_ref,
    assign_ref,
    total_ref,
    prob_grad,
    proto,
    scale,
    wp,
    codes,
    proto_grad,
    grad_proj,
    grad_value,
    factor_s,
):
    clips, ranks, n_clip = came.shape[:3]
    batch = unit_ref.shape[0]
    share = grad_proj.shape[0]
    width = codes.shape[1]
    step = pl.program_id(0)

    @pl.when(step == 0)
    def _():
        sums = [jnp.zeros(came.shape[3:], F32) for _ in range(2)]
        for cam in range(n_cam):
            part = jnp.sum(came[cam // ranks, cam % ranks].astype(F32), axis=0)
            sums[cam % 2] = sums[cam % 2] + part
        line = jnp.sum((sums[0] + sums[1])[batch : batch + DIGITS], axis=0, keepdims=True)
        by_assign = protos / from_lanes(line, batch)
        by_prob = protos / total_ref[:, :1]
        factor_s[0] = spread(by_prob)
        factor_s[1] = spread(by_assign)
        assign_grad = jnp.concatenate([s[:batch] for s in sums], axis=1)
        grad_unit = prob_grad[...] * by_prob - assign_grad * by_assign
        unit = unit_ref[...]
        grad_embed = (
            grad_unit - unit * jnp.sum(unit * grad_unit, axis=1, keepdims=True)
        ) / norm_ref[:, :1]
        grad_embed = grad_embed.astype(BF16)

        def rows(rank, at):
            picked = [came[g, rank].astype(F32)[:, at, :] for g in range(clips)]
            return jnp.concatenate(picked, axis=0)[:, :share].astype(BF16)

        grad_proj[...] = lax.dot_general(
            rows(pick[0], batch + DIGITS), grad_embed, OUTER, preferred_element_type=F32
        )
        grad_pooled = lax.dot_general(
            grad_embed, wp[...], TRANSPOSED, preferred_element_type=F32
        ).astype(BF16)
        col_head = lax.broadcasted_iota(jnp.int32, grad_value.shape, 1) // HD
        value = jnp.zeros(grad_value.shape, F32)
        for head in range(grad_value.shape[1] // HD):
            mixed = rows(pick[1], batch + DIGITS + 1 + head)
            out = lax.dot_general(mixed, grad_pooled, OUTER, preferred_element_type=F32)
            value = jnp.where(col_head == head, out, value)
        grad_value[...] = value

    here = pl.ds(pl.multiple_of(step * width, width), width)
    assign = assign_ref[:, here] * factor_s[1][:, :1]
    grad_logits = (exp_ref[:, here] * factor_s[0][:, :1] - assign).astype(BF16)
    for g in range(clips):
        for p in range(n_clip):
            at = g * n_clip + p
            codes[p * clips + g : p * clips + g + 1, :] = assign[at : at + 1]
    grad = lax.dot_general(
        unit_ref[...].astype(BF16), grad_logits, OUTER, preferred_element_type=F32
    )
    inverse = scale[:, here]
    unit_proto = proto[:, here].astype(F32) * inverse
    along = jnp.sum(unit_proto * grad, axis=0, keepdims=True)
    proto_grad[...] = (grad - unit_proto * along) * inverse


def local(tokens, w_query, w_key, w_value, w_proj, prototypes):
    clips, _, tok, d = tokens.shape
    n_cam, n_clip = lax.axis_size("cam"), lax.axis_size("clip")
    devices = n_cam * n_clip
    ranks = n_cam // clips
    batch = clips * n_clip
    cols = d // ranks
    heads = cols // HD
    heads_here = heads // clips
    share = d // n_clip
    bottleneck, columns = prototypes.shape
    protos = columns * devices
    halves = bottleneck // LANES
    cam, clip = lax.axis_index("cam"), lax.axis_index("clip")
    rank = cam % ranks

    with jax.named_scope("tokens_of_a_clip"):
        stages = gather_clip(tokens.reshape(clips, tok, d), n_cam)

    with jax.named_scope("pooling"):
        weights = [
            lax.dynamic_slice_in_dim(w, rank * cols, cols, 1) for w in (w_query, w_key, w_value)
        ]
        wp = lax.dynamic_slice_in_dim(w_proj, rank * cols, cols, 0)
        parts = [project_blocks([b for _, b in stage], weights) for stage in stages[:-1]]
        key_weights, pooled, embed = pool(parts, [b for _, b in stages[-1]], weights, wp)

    with jax.named_scope("prototypes"):
        proto_f = prototypes.astype(F32)
        column_norm = jnp.sqrt(jnp.sum(proto_f * proto_f, axis=0, keepdims=True) + NORM_EPS)
        scale = 1.0 / column_norm
        proto_b = (proto_f / column_norm).astype(BF16)
        proto_t = proto_b.T

    with jax.named_scope("mixtures"):
        cameras, blocks, at = {}, [], 0
        for stage in stages:
            for camera, block in stage:
                cameras.setdefault(camera, []).append((len(blocks), at))
                blocks.append(block)
                at += block.shape[0]
        (mix,) = call(
            functools.partial(mixture_kernel, list(cameras.values())),
            [((heads, d), F32)],
            [key_weights, *blocks],
            2 * at * d * 32,
        )
        mix_to = mix.reshape(clips, heads_here, n_clip, share).transpose(0, 2, 1, 3)
        mix_to = jnp.tile(mix_to.reshape(batch, heads_here, share), (ranks, 1, 1))
        pooled_to = jnp.tile(pooled.reshape(cols // share, 1, share), (devices * share // cols, 1, 1))
        side = jnp.concatenate([pooled_to, mix_to], axis=1)
        side = jnp.pad(side, ((0, 0), (DIGITS, 0), (0, LANES - share)))

    with jax.named_scope("logits"):
        came = exchange(jnp.broadcast_to(embed[None], (devices,) + embed.shape))
        unit, norm, exponents, assign, message = call(
            functools.partial(logits_kernel, clips, ranks, n_clip),
            [
                ((batch, bottleneck), F32),
                ((batch, LANES), F32),
                ((batch, columns), F32),
                ((batch, columns), F32),
                ((devices, 2, LANES), F32),
            ],
            [came, proto_b, proto_t],
            4 * batch * bottleneck * columns,
            2 * batch * columns,
        )

    with jax.named_scope("row_total_1"):
        came = exchange(message)
        assign, message, total = call(
            second_kernel,
            [((batch, columns), F32), ((devices, 2, LANES), F32), ((batch, LANES), F32)],
            [came, assign],
            8 * batch * columns,
        )

    with jax.named_scope("row_total_2"):
        came = exchange(message)
        parity = (cam % 2).reshape(1)
        assign, keep, send, digits, prob_grad = call(
            third_kernel,
            [
                ((batch, columns), F32),
                ((batch, bottleneck // 2), F32),
                ((batch, bottleneck // 2), F32),
                (side.shape[1:], F32),
                ((batch, bottleneck), F32),
            ],
            [parity, came, assign, proto_t],
            2 * batch * bottleneck * columns,
            in_specs=[SCALARS] + [WHOLE] * 3,
        )

    with jax.named_scope("row_total_3"):
        got = lax.ppermute(send, "cam", [(i, i ^ 1) for i in range(n_cam)])
        (message,) = call(
            message_kernel,
            [((devices, batch + side.shape[1], LANES), BF16)],
            [keep, got, digits, side],
            devices * batch * LANES,
        )
        came = exchange(message)

    with jax.named_scope("outputs"):
        width = heads_here * HD
        pick = jnp.stack([clip * share // cols, cam // clips])
        proj_rows = lax.dynamic_slice_in_dim(w_proj, cam * width, width, 0)
        block = min(columns, 512)
        ins = [
            pick,
            came.reshape((clips, ranks, n_clip) + came.shape[1:]),
            unit,
            norm,
            exponents,
            assign,
            total,
            prob_grad,
            prototypes,
            scale,
            proj_rows,
        ]
        return call(
            functools.partial(output_kernel, protos, n_cam),
            [
                ((batch, columns), F32),
                ((bottleneck, columns), F32),
                ((share, bottleneck), F32),
                ((share, width), F32),
            ],
            ins,
            2 * batch * bottleneck * columns,
            scratch=[pltpu.VMEM((2, batch, LANES), F32)],
            grid=(columns // block,),
            in_specs=[SCALARS] + [WHOLE] * (len(ins) - 1),
            out_specs=[
                pl.BlockSpec((batch, block), lambda i: (0, i)),
                pl.BlockSpec((bottleneck, block), lambda i: (0, i)),
                pl.BlockSpec((share, bottleneck), lambda i: (0, 0)),
                pl.BlockSpec((share, width), lambda i: (0, 0)),
            ],
        )


def solution(mesh):
    in_specs = (P("clip", "cam", None, None), P(), P(), P(), P(), P(None, ALL))
    out_specs = (P(None, ALL), P(None, ALL), P("clip", None), P("clip", "cam"))
    return jax.shard_map(local, mesh=mesh, in_specs=in_specs, out_specs=out_specs, check_vma=False)
```

time: 98.3 us -> 108 us (1.099)
  local copies, waits for them, and re-layouts: 10.3 us -> 29.9 us
  Pallas kernels: 13.3 us -> 28.5 us
  waiting for transfers between devices: 27.5 us -> 16.7 us
  blocking collectives: 17.9 us -> 9.32 us
  matrix products: 7.67 us -> 0 us
  starting transfers between devices: 12.3 us -> 16.2 us
  other arithmetic: 7.87 us -> 5.6 us
    pallas_call x1 -> x9, Pallas kernels: 13.3 us -> 28.5 us  [call(): pl.pallas_call(kernel, out_shape=tuple((jax.ShapeDtypeStruct(*o) for o in...]
    unnamed x17 -> x58, local copies, waits for them, and re-layouts: 2.64 us -> 15.9 us
    all_to_all x2 -> x1, blocking collectives: 17.9 us -> 9.32 us  [exchange(): return lax.all_to_all(message, ALL, split_axis=0, concat_axis=0, tiled=True)]
    dot_general x8 -> x0, matrix products: 7.67 us -> none  [the longest x1 1.85 us: local(): lax.dot_general(unit_b, grad_logits, (((0,), (0,)), ((), ())), preferred_...]
    ppermute x3 -> x6, waiting for transfers between devices: 9.67 us -> 3.32 us  [the longest x2 3.31 us: gather_clip(): held[c + 1].append((s * ranks, lax.ppermute(sent, 'cam', perm)))]
    all_to_all x2 -> x3, waiting for transfers between devices: 17.8 us -> 13.3 us  [exchange(): return lax.all_to_all(message, ALL, split_axis=0, concat_axis=0, tiled=True)]
    all_to_all x2 -> x3, starting transfers between devices: 9.4 us -> 13.1 us  [exchange(): return lax.all_to_all(message, ALL, split_axis=0, concat_axis=0, tiled=True)]
    div x1 -> x0, other arithmetic: 3.41 us -> none  [local(): (grad_unit_proto - unit_proto * jnp.sum(unit_proto * grad_unit_proto, axi...]
  transfers between devices with their start and end apart: 5 -> 9, of which waited for: 4 -> 5; matrix products, arithmetic and copies ran while one was open for 6% -> 17% of each run, Pallas kernels for 0% -> 8%
where the time goes in v2:
time: 108 us; the launch traced here: 107 us
  local copies, waits for them, and re-layouts  29.9 us (28%)
  Pallas kernels  28.5 us (26%)
  waiting for transfers between devices  16.7 us (15%)
  starting transfers between devices  16.2 us (15%)
  blocking collectives  9.32 us (9%)
  other arithmetic  5.6 us (5%)
    pallas_call x9, Pallas kernels, call(): pl.pallas_call(kernel, out_shape=tuple((jax.ShapeDtypeStruct(*o) for o in...  28.5 us
    unnamed x58, local copies, waits for them, and re-layouts  15.9 us
    all_to_all x3, waiting for transfers between devices, exchange(): return lax.all_to_all(message, ALL, split_axis=0, concat_axis=0, tiled=True)  13.3 us
    all_to_all x3, starting transfers between devices, exchange(): return lax.all_to_all(message, ALL, split_axis=0, concat_axis=0, tiled=True)  13.1 us
    all_to_all x1, blocking collectives, exchange(): return lax.all_to_all(message, ALL, split_axis=0, concat_axis=0, tiled=True)  9.32 us
    dynamic_slice x2, local copies, waits for them, and re-layouts, local(): lax.dynamic_slice_in_dim(w, rank * cols, cols, 1)  4.08 us
    ppermute x2, waiting for transfers between devices, gather_clip(): held[c + 1].append((s * ranks, lax.ppermute(sent, 'cam', perm)))  3.31 us
    convert_element_type x1, other arithmetic, local(): proto_b = (proto_f / column_norm).astype(BF16)  2.58 us
  transfers between devices with their start and end apart: 9, of which 5 were waited for; matrix products, arithmetic and copies ran while one was open for 17% of the time, Pallas kernels for 8%

profile of v2, /device:TPU:0, one launch (start us, length us, event | category | flops | bytes accessed | tf_op | source)
XLA Modules:
  0.0 107.0 jit_solution(1953163052442528393)
XLA Ops:
  0.6 0.0 copy-start
  0.6 0.0 copy-start.2
  0.7 2.0 %dynamic-slice_bitcast_fusion.refs_0_ = bf16[256,1024]{1,0:T(8,128)(2,1)} fusion(bf16[2,1,256,1024]{3,2,1,0:T(8,128)(2,1)} %param.6, s32[]{:T(128)S(6)} %select_n.43), kind=kLoop, calls=%fused_computation.4 | loop fusion | bytes 1048580 | tf_op jit(solution)/shard_map/tokens_of_a_clip/jit(dynamic_index_in_dim)/squeeze | solution.py:156
  2.7 0.5 collective-permute-start
  3.2 1.9 %dynamic-slice_bitcast_fusion.1 = (bf16[128,1024]{1,0:T(8,128)(2,1)}, bf16[128,1024]{1,0:T(8,128)(2,1)}) fusion(bf16[2,1,256,1024]{3,2,1,0:T(8,128)(2,1)} %param.6, s32[]{:T(128)S(6)} %select_n.46), kind=kLoop, calls=%fused_computation.5 | loop fusion | bytes 1048580 | tf_op jit(solution)/shard_map/tokens_of_a_clip/squeeze | solution.py:153
  5.0 2.5 %collective-permute-start.1 = (bf16[128,1024]{1,0:T(8,128)(2,1)}, bf16[128,1024]{1,0:T(8,128)(2,1)S(1)}, u32[]{:S(2)}, u32[]{:S(2)}) collective-permute-start(bf16[128,1024]{1,0:T(8,128)(2,1)} %get-tuple-element.49), channel_id=1, source_target_pairs={{0,16},{8,24},{16,0},{24,8},{1,17},{9,25},{17,1},{25,9},{2,18},{10... | collective-permute-start | bytes 786440 | tf_op jit(solution)/shard_map/tokens_of_a_clip/ppermute | solution.py:155
  7.5 0.0 collective-permute-start.3
  7.6 1.3 %copy.12 = bf16[256,2048]{0,1:T(8,128)(2,1)} copy(bf16[256,2048]{1,0:T(8,128)(2,1)S(1)} %copy-done.2) | data formatting | bytes 2097152 | tf_op args[5]
  8.9 1.6 %fusion = f32[2048]{0:T(1024)S(1)} fusion(bf16[256,2048]{0,1:T(8,128)(2,1)} %copy.12), kind=kLoop, calls=%fused_computation.2 | loop fusion | flops 1570816 | bytes 1056768 | tf_op jit(solution)/shard_map/prototypes/reduce_sum | solution.py:376
  10.5 2.6 %fusion.1 = bf16[256,2048]{0,1:T(8,128)(2,1)} fusion(bf16[256,2048]{0,1:T(8,128)(2,1)} %copy.12, f32[2048]{0:T(1024)S(1)} %get-tuple-element.51), kind=kLoop, calls=%fused_computation.3 | loop fusion | flops 1572864 | bytes 2105344 | tf_op jit(solution)/shard_map/prototypes/convert_element_type | solution.py:378
  13.0 1.9 %collective-permute-done.1.refs_0_.refs_2_ = bf16[128,1024]{1,0:T(8,128)(2,1)S(1)} collective-permute-done((bf16[128,1024]{1,0:T(8,128)(2,1)}, bf16[128,1024]{1,0:T(8,128)(2,1)S(1)}, u32[]{:S(2)}, u32[]{:S(2)}) %collective-permute-start.1) | collective-permute-done | bytes 262176 | tf_op jit(solution)/shard_map/tokens_of_a_clip/ppermute | solution.py:155
  14.9 0.0 collective-permute-start.2
  14.9 3.0 %constant_dynamic-slice_fusion.2 = (bf16[1024,512]{1,0:T(8,128)(2,1)}, bf16[1024,512]{1,0:T(8,128)(2,1)}) fusion(bf16[1024,1024]{1,0:T(8,128)(2,1)} %param.9, s32[]{:T(128)S(6)} %select_n.44, bf16[1024,1024]{1,0:T(8,128)(2,1)} %param.8), kind=kLoop, calls=%fused_computation.14 | loop fusion | bytes 4194308 | tf_op jit(solution)/shard_map/pooling/dynamic_slice | solution.py:368
  17.9 1.1 %constant_dynamic-slice_fusion.4.refs_2_.refs_8_ = bf16[1024,512]{1,0:T(8,128)(2,1)} fusion(bf16[1024,1024]{1,0:T(8,128)(2,1)S(1)} %copy-done, s32[]{:T(128)S(6)} %select_n.44), kind=kLoop, calls=%fused_computation.16 | loop fusion | bytes 2097156 | tf_op jit(solution)/shard_map/pooling/dynamic_slice | solution.py:368
  19.0 1.5 %collective-permute-done.3.refs_6_.refs_4_ = bf16[128,1024]{1,0:T(8,128)(2,1)} collective-permute-done((bf16[128,1024]{1,0:T(8,128)(2,1)}, bf16[128,1024]{1,0:T(8,128)(2,1)}, u32[]{:S(2)}, u32[]{:S(2)}) %collective-permute-start.3) | collective-permute-done | bytes 262176 | tf_op jit(solution)/shard_map/tokens_of_a_clip/ppermute | solution.py:155
  20.4 0.0 collective-permute-start.4
  20.5 0.0 collective-permute-done.2.refs_1_.refs_3_
  20.5 2.9 %pooling.4 = (bf16[256,512]{1,0:T(8,128)(2,1)S(1)}, bf16[512,256]{1,0:T(8,128)(2,1)S(1)}, bf16[256,512]{1,0:T(8,128)(2,1)S(1)}) custom-call(bf16[128,1024]{1,0:T(8,128)(2,1)S(1)} %collective-permute-done.1.refs_0_.refs_2_, bf16[128,1024]{1,0:T(8,128)(2,1)S(1)} %collective-permute-done.2.refs_1_.refs_3_, ...), custom_call_target="tpu_custom_call" | custom-call | flops 805306368 | bytes 3670016 | tf_op jit(solution)/shard_map/pooling/pallas_call | solution.py:28
  23.3 0.7 copy-done.5
  24.0 0.0 collective-permute-done.refs_1_
  24.0 4.0 %pooling.3 = (bf16[512,512]{1,0:T(8,128)(2,1)S(1)}, bf16[512,512]{1,0:T(8,128)(2,1)S(1)}, bf16[512,512]{1,0:T(8,128)(2,1)S(1)}) custom-call(bf16[256,1024]{1,0:T(8,128)(2,1)} %dynamic-slice_bitcast_fusion.refs_0_, bf16[256,1024]{1,0:T(8,128)(2,1)} %collective-permute-done.refs_1_, bf16[1024,512]{1,0:T(8,128)(2,1)} %constant_dynamic-slice_fusion.4.refs_2_.refs_8_, ...), custom_call_target="tpu_custom_call" | custom-call | flops 1610612736 | bytes 4194304 | tf_op jit(solution)/shard_map/pooling/pallas_call | solution.py:28
  28.0 0.8 copy-done.23
  28.8 0.8 copy-done.24
  29.6 0.8 copy-done.25
  30.4 12.2 %pooling.5 = (bf16[8,1024]{1,0:T(8,128)(2,1)S(1)}, f32[1,512]{1,0:T(1,128)S(1)}, f32[2,128]{1,0:T(2,128)S(1)}) custom-call(bf16[512,512]{1,0:T(8,128)(2,1)} %copy-done.23, bf16[512,512]{1,0:T(8,128)(2,1)} %copy-done.24, bf16[512,512]{1,0:T(8,128)(2,1)} %copy-done.25, bf16[256,512]{1,0:T(8,128)(2,1)S(1)} %get-tuple-element.29.refs_3_, ...), custom_call_target="tpu_custom_call" | custom-call | flops 5100273664 | bytes 6291456 | tf_op jit(solution)/shard_map/pooling/pallas_call | solution.py:28
  42.7 0.6 copy-done.18
  43.3 0.6 broadcast_in_dim.2
  43.9 6.2 %all-to-all-start = ((f32[32,2,128]{2,1,0:T(2,128)}), f32[32,2,128]{2,1,0:T(2,128)S(1)}, u32[]{:S(2)}, u32[]{:S(2)}) async-start(f32[32,2,128]{2,1,0:T(2,128)} %broadcast_in_dim.2), calls=%async_computation | async-start | bytes 65536 | tf_op jit(solution)/shard_map/logits/all_to_all | solution.py:185
  50.1 1.3 %fusion.2.proto_t = bf16[2048,256]{1,0:T(8,128)(2,1)} fusion(f32[2048]{0:T(1024)S(1)} %get-tuple-element.51, bf16[256,2048]{0,1:T(8,128)(2,1)S(1)} %copy-done.26), kind=kLoop, calls=%fused_computation.18 | loop fusion | flops 1572864 | bytes 2105344 | tf_op jit(solution)/shard_map/prototypes/transpose | solution.py:379
  51.5 2.3 %copy.13.proto = bf16[256,2048]{1,0:T(8,128)(2,1)} copy(bf16[256,2048]{0,1:T(8,128)(2,1)} %fusion.1) | data formatting | bytes 2097152 | tf_op jit(solution)/shard_map/prototypes/convert_element_type | solution.py:378
  53.7 3.6 %all-to-all-done.came = f32[32,2,128]{2,1,0:T(2,128)S(1)} async-done(((f32[32,2,128]{2,1,0:T(2,128)}), f32[32,2,128]{2,1,0:T(2,128)S(1)}, u32[]{:S(2)}, u32[]{:S(2)}) %all-to-all-start) | async-done | bytes 32800 | tf_op jit(solution)/shard_map/logits/all_to_all | solution.py:185
  57.3 1.2 %copy-done.4 = bf16[256,2048]{1,0:T(8,128)(2,1)S(1)} copy-done((bf16[256,2048]{1,0:T(8,128)(2,1)S(1)}, bf16[256,2048]{1,0:T(8,128)(2,1)}, u32[]{:S(2)}) %copy-start.4) | copy-done | bytes 1048600
  58.5 1.8 %logits.1 = (f32[16,256]{1,0:T(8,128)S(1)}, f32[16,128]{1,0:T(8,128)S(1)}, f32[16,2048]{1,0:T(8,128)S(1)}, f32[16,2048]{1,0:T(8,128)S(1)}, f32[32,2,128]{2,1,0:T(2,128)S(1)}) custom-call(f32[32,2,128]{2,1,0:T(2,128)S(1)} %all-to-all-done.came, bf16[256,2048]{1,0:T(8,128)(2,1)S(1)} %copy-done.4, bf16[2048,256]{1,0:T(8,128)(2,1)} %fusion.2.proto_t), custom_call_target="tpu_custom_call" | custom-call | flops 33554432 | bytes 2129920 | tf_op jit(solution)/shard_map/logits/pallas_call | solution.py:28
  60.4 0.0 copy-start.9
  60.4 0.6 copy-done.9
  61.0 9.3 %all_to_all.20.came = f32[32,2,128]{2,1,0:T(2,128)S(1)} all-to-all(f32[32,2,128]{2,1,0:T(2,128)S(1)} %get-tuple-element.33), channel_id=1, replica_groups=mesh['cam'=4,'clip'=8] {'cam','clip'}, dimensions={0} | all-to-all | bytes 65536 | tf_op jit(solution)/shard_map/row_total_1/all_to_all | solution.py:185
  70.3 0.2 row_total_1.1
  70.6 0.0 copy-start.13
  70.6 0.6 copy-done.13
  71.2 0.6 copy-done.20
  71.8 3.3 %all-to-all-start.2 = ((f32[32,2,128]{2,1,0:T(2,128)}), f32[32,2,128]{2,1,0:T(2,128)}, u32[]{:S(2)}, u32[]{:S(2)}) async-start(f32[32,2,128]{2,1,0:T(2,128)} %copy-done.13), calls=%async_computation.2 | async-start | bytes 65536 | tf_op jit(solution)/shard_map/row_total_2/all_to_all | solution.py:185
  75.1 0.9 copy-done.6
  76.1 0.9 copy-done.8
  77.0 0.7 copy-done.19
  77.7 1.6 %mixtures.1 = f32[8,1024]{1,0:T(8,128)S(1)} custom-call(bf16[8,1024]{1,0:T(8,128)(2,1)S(1)} %copy-done.19, bf16[256,1024]{1,0:T(8,128)(2,1)} %dynamic-slice_bitcast_fusion.refs_0_, bf16[256,1024]{1,0:T(8,128)(2,1)} %collective-permute-done.refs_1_, bf16[128,1024]{1,0:T(8,128)(2,1)S(1)} %collective-permute-done.1.refs_0_.refs_2_, ...), custom_call_target="tpu_custom_call" | custom-call | flops 67108864 | bytes 2113536 | tf_op jit(solution)/shard_map/mixtures/pallas_call | solution.py:28
  79.4 0.6 copy.15
  80.0 2.2 %all-to-all-done.2.came = f32[32,2,128]{2,1,0:T(2,128)} async-done(((f32[32,2,128]{2,1,0:T(2,128)}), f32[32,2,128]{2,1,0:T(2,128)}, u32[]{:S(2)}, u32[]{:S(2)}) %all-to-all-start.2) | async-done | bytes 32800 | tf_op jit(solution)/shard_map/row_total_2/all_to_all | solution.py:185
  82.3 1.1 %row_total_2.1 = (f32[16,2048]{1,0:T(8,128)S(1)}, f32[16,128]{1,0:T(8,128)S(1)}, f32[16,128]{1,0:T(8,128)S(1)}, f32[8,128]{1,0:T(8,128)S(1)}, f32[16,256]{1,0:T(8,128)S(1)}) custom-call(s32[1]{0:T(128)} %bitcast.2.parity, f32[32,2,128]{2,1,0:T(2,128)} %all-to-all-done.2.came, f32[16,2048]{1,0:T(8,128)S(1)} %get-tuple-element.36.assign_ref, ...), custom_call_target="tpu_custom_call" | custom-call | flops 16777216 | bytes 1212420 | tf_op jit(solution)/shard_map/row_total_2/pallas_call | solution.py:28
  83.4 0.7 copy-done.11
  84.0 0.6 copy-done.16
  84.6 0.1 collective-permute-start.5
  84.8 0.8 tile.24
  85.6 0.7 tile.21
  86.3 0.7 row_total_3.1
  87.0 3.6 %all-to-all-start.3 = ((bf16[32,24,128]{2,1,0:T(8,128)(2,1)}), bf16[32,24,128]{2,1,0:T(8,128)(2,1)S(1)}, u32[]{:S(2)}, u32[]{:S(2)}) async-start(bf16[32,24,128]{2,1,0:T(8,128)(2,1)} %row_total_3.1), calls=%async_computation.3 | async-start | bytes 393216 | tf_op jit(solution)/shard_map/row_total_3/all_to_all | solution.py:185
  90.6 0.1 pad_add_fusion.pick
  90.7 0.9 constant_dynamic-slice_fusion.wp
  91.6 7.5 %all-to-all-done.3 = bf16[32,24,128]{2,1,0:T(8,128)(2,1)S(1)} async-done(((bf16[32,24,128]{2,1,0:T(8,128)(2,1)}), bf16[32,24,128]{2,1,0:T(8,128)(2,1)S(1)}, u32[]{:S(2)}, u32[]{:S(2)}) %all-to-all-start.3) | async-done | bytes 196640 | tf_op jit(solution)/shard_map/row_total_3/all_to_all | solution.py:185
  99.2 0.9 copy-done.10
  100.1 0.9 copy-done.12
  101.0 0.7 copy-done.15
  101.7 0.7 copy-done.17
  102.4 0.7 copy-done.21
  103.1 3.9 %outputs.1 = (f32[16,2048]{1,0:T(8,128)}, f32[256,2048]{1,0:T(8,128)}, f32[128,256]{1,0:T(8,128)}, f32[128,256]{1,0:T(8,128)}) custom-call(s32[2]{0:T(128)S(1)} %pad_add_fusion.pick, bf16[2,2,8,24,128]{4,3,2,1,0:T(8,128)(2,1)S(1)} %bitcast.24, f32[16,256]{1,0:T(8,128)S(1)} %copy-done.15, f32[16,128]{1,0:T(8,128)S(1)} %get-tuple-element.43.norm_ref, ...), custom_call_target="tpu_custom_call" | custom-call | flops 16777216 | bytes 1695752 | tf_op jit(solution)/shard_map/outputs/pallas_call | solution.py:28
  (40 shorter events, 0.2 us)
Async XLA Ops:
  0.6 17.3 %copy-start = (bf16[1024,1024]{1,0:T(8,128)(2,1)S(1)}, bf16[1024,1024]{1,0:T(8,128)(2,1)}, u32[]{:S(2)}) copy-start(bf16[1024,1024]{1,0:T(8,128)(2,1)} %param.7) | copy-start | bytes 6291460
  0.6 6.9 %copy-start.2 = (bf16[256,2048]{1,0:T(8,128)(2,1)S(1)}, bf16[256,2048]{1,0:T(8,128)(2,1)}, u32[]{:S(2)}) copy-start(bf16[256,2048]{1,0:T(8,128)(2,1)} %proto.1) | copy-start | bytes 3145732
  2.7 21.3 %collective-permute-start = (bf16[256,1024]{1,0:T(8,128)(2,1)}, bf16[256,1024]{1,0:T(8,128)(2,1)}, u32[]{:S(2)}, u32[]{:S(2)}) collective-permute-start(bf16[256,1024]{1,0:T(8,128)(2,1)} %dynamic-slice_bitcast_fusion.refs_0_), channel_id=1, source_target_pairs={{0,8},{8,0},{16,24},{24,16},{1,9},{9,1},{17,25},{25,17},{2,10},{10... | collective-permute-start | bytes 1572872 | tf_op jit(solution)/shard_map/tokens_of_a_clip/ppermute | solution.py:162
  5.0 9.9 %collective-permute-start.1 = (bf16[128,1024]{1,0:T(8,128)(2,1)}, bf16[128,1024]{1,0:T(8,128)(2,1)S(1)}, u32[]{:S(2)}, u32[]{:S(2)}) collective-permute-start(bf16[128,1024]{1,0:T(8,128)(2,1)} %get-tuple-element.49), channel_id=1, source_target_pairs={{0,16},{8,24},{16,0},{24,8},{1,17},{9,25},{17,1},{25,9},{2,18},{10... | collective-permute-start | bytes 786440 | tf_op jit(solution)/shard_map/tokens_of_a_clip/ppermute | solution.py:155
  7.5 12.9 %collective-permute-start.3 = (bf16[128,1024]{1,0:T(8,128)(2,1)}, bf16[128,1024]{1,0:T(8,128)(2,1)}, u32[]{:S(2)}, u32[]{:S(2)}) collective-permute-start(bf16[128,1024]{1,0:T(8,128)(2,1)} %get-tuple-element.48), channel_id=1, source_target_pairs={{0,16},{8,24},{16,0},{24,8},{1,17},{9,25},{17,1},{25,9},{2,18},{10... | collective-permute-start | bytes 786440 | tf_op jit(solution)/shard_map/tokens_of_a_clip/ppermute | solution.py:155
  14.9 5.6 %collective-permute-start.2 = (bf16[128,1024]{1,0:T(8,128)(2,1)S(1)}, bf16[128,1024]{1,0:T(8,128)(2,1)S(1)}, u32[]{:S(2)}, u32[]{:S(2)}) collective-permute-start(bf16[128,1024]{1,0:T(8,128)(2,1)S(1)} %collective-permute-done.1.refs_0_.refs_2_), channel_id=1, source_target_pairs={{0,8},{8,0},{16,24},{24,16},{1,9},{9,1},{17,25},{25,17},{2,10},{10... | collective-permute-start | bytes 786440 | tf_op jit(solution)/shard_map/tokens_of_a_clip/ppermute | solution.py:162
  17.9 2.5 %copy-start.27 = (bf16[1024,256]{1,0:T(8,128)(2,1)S(1)}, bf16[1024,256]{1,0:T(8,128)(2,1)}, u32[]{:S(2)}) copy-start(bf16[1024,256]{1,0:T(8,128)(2,1)} %param.10) | copy-start | bytes 1572868
  20.4 10.0 %collective-permute-start.4 = (bf16[128,1024]{1,0:T(8,128)(2,1)}, bf16[128,1024]{1,0:T(8,128)(2,1)S(1)}, u32[]{:S(2)}, u32[]{:S(2)}) collective-permute-start(bf16[128,1024]{1,0:T(8,128)(2,1)} %collective-permute-done.3.refs_6_.refs_4_), channel_id=1, source_target_pairs={{0,8},{8,0},{16,24},{24,16},{1,9},{9,1},{17,25},{25,17},{2,10},{10... | collective-permute-start | bytes 786440 | tf_op jit(solution)/shard_map/tokens_of_a_clip/ppermute | solution.py:162
  23.3 0.7 copy-start.5
  28.0 0.8 copy-start.23
  28.8 0.8 copy-start.24
  29.6 0.8 copy-start.25
  30.4 12.3 %copy-start.7 = (bf16[128,1024]{1,0:T(8,128)(2,1)}, bf16[128,1024]{1,0:T(8,128)(2,1)S(1)}, u32[]{:S(2)}) copy-start(bf16[128,1024]{1,0:T(8,128)(2,1)S(1)} %collective-permute-done.4.refs_7_.refs_5_) | copy-start | bytes 786436
  30.4 19.7 %copy-start.26 = (bf16[256,2048]{0,1:T(8,128)(2,1)S(1)}, bf16[256,2048]{0,1:T(8,128)(2,1)}, u32[]{:S(2)}) copy-start(bf16[256,2048]{0,1:T(8,128)(2,1)} %copy.12) | copy-start | bytes 3145732
  42.7 0.6 copy-start.18
  43.3 10.4 %copy-start.22 = (f32[1,512]{1,0:T(1,128)}, f32[1,512]{1,0:T(1,128)S(1)}, u32[]{:S(2)}) copy-start(f32[1,512]{1,0:T(1,128)S(1)} %get-tuple-element.40) | copy-start | bytes 6148
  43.9 13.4 %all-to-all-start = ((f32[32,2,128]{2,1,0:T(2,128)}), f32[32,2,128]{2,1,0:T(2,128)S(1)}, u32[]{:S(2)}, u32[]{:S(2)}) async-start(f32[32,2,128]{2,1,0:T(2,128)} %broadcast_in_dim.2), calls=%async_computation | async-start | bytes 65536 | tf_op jit(solution)/shard_map/logits/all_to_all | solution.py:185
  53.7 28.5 %copy-start.1 = (bf16[2048,256]{1,0:T(8,128)(2,1)S(1)}, bf16[2048,256]{1,0:T(8,128)(2,1)}, u32[]{:S(2)}) copy-start(bf16[2048,256]{1,0:T(8,128)(2,1)} %fusion.2.proto_t) | copy-start | bytes 3145732
  57.3 1.2 %copy-start.4 = (bf16[256,2048]{1,0:T(8,128)(2,1)S(1)}, bf16[256,2048]{1,0:T(8,128)(2,1)}, u32[]{:S(2)}) copy-start(bf16[256,2048]{1,0:T(8,128)(2,1)} %copy.13.proto) | copy-start | bytes 3145732
  60.4 0.7 copy-start.9
  61.0 9.6 %copy-start.14 = (f32[16,256]{1,0:T(8,128)}, f32[16,256]{1,0:T(8,128)S(1)}, u32[]{:S(2)}) copy-start(f32[16,256]{1,0:T(8,128)S(1)} %get-tuple-element.42.unit_ref) | copy-start | bytes 49156
  70.6 0.6 copy-start.13
  71.2 0.6 copy-start.20
  71.8 10.4 %all-to-all-start.2 = ((f32[32,2,128]{2,1,0:T(2,128)}), f32[32,2,128]{2,1,0:T(2,128)}, u32[]{:S(2)}, u32[]{:S(2)}) async-start(f32[32,2,128]{2,1,0:T(2,128)} %copy-done.13), calls=%async_computation.2 | async-start | bytes 65536 | tf_op jit(solution)/shard_map/row_total_2/all_to_all | solution.py:185
  75.1 1.0 copy-start.6
  76.1 0.9 copy-start.8
  77.0 0.7 copy-start.19
  83.4 0.7 copy-start.11
  84.0 0.6 copy-start.16
  84.6 14.5 %copy-start.3 = (bf16[256,2048]{1,0:T(8,128)(2,1)S(1)}, bf16[256,2048]{1,0:T(8,128)(2,1)}, u32[]{:S(2)}) copy-start(bf16[256,2048]{1,0:T(8,128)(2,1)} %proto.1) | copy-start | bytes 3145732
  84.6 1.7 %collective-permute-start.5 = (f32[16,128]{1,0:T(8,128)S(1)}, f32[16,128]{1,0:T(8,128)S(1)}, u32[]{:S(2)}, u32[]{:S(2)}) collective-permute-start(f32[16,128]{1,0:T(8,128)S(1)} %get-tuple-element.38), channel_id=1, source_target_pairs={{0,8},{8,0},{16,24},{24,16},{1,9},{9,1},{17,25},{25,17},{2,10},{10... | collective-permute-start | bytes 24584 | tf_op jit(solution)/shard_map/row_total_3/ppermute | solution.py:443
  87.0 12.1 %all-to-all-start.3 = ((bf16[32,24,128]{2,1,0:T(8,128)(2,1)}), bf16[32,24,128]{2,1,0:T(8,128)(2,1)S(1)}, u32[]{:S(2)}, u32[]{:S(2)}) async-start(bf16[32,24,128]{2,1,0:T(8,128)(2,1)} %row_total_3.1), calls=%async_computation.3 | async-start | bytes 393216 | tf_op jit(solution)/shard_map/row_total_3/all_to_all | solution.py:185
  99.2 0.9 copy-start.10
  100.1 0.9 copy-start.12
  101.0 0.7 copy-start.15
  101.7 0.7 copy-start.17
  102.4 0.7 copy-start.21

commit v3 on v2

--- a/solution.py
+++ b/solution.py
@@ -13,7 +13,7 @@
 NORM_EPS = 1e-06
 LANES = 128
 DIGITS = 3
-CHUNKS = 2
+CHUNKS = 1
 ALL = ("cam", "clip")
 F32 = jnp.float32
 BF16 = jnp.bfloat16
@@ -23,7 +23,9 @@
 SCALARS = pl.BlockSpec(memory_space=pltpu.SMEM)
 
 
-def call(kernel, outs, ins, flops, extra=0, scratch=(), grid=None, out_specs=None, in_specs=None):
+def call(
+    kernel, outs, ins, flops, extra=0, scratch=(), grid=None, out_specs=None, in_specs=None, mib=4
+):
     moved = sum(a.size * a.dtype.itemsize for a in ins)
     return pl.pallas_call(
         kernel,
@@ -32,8 +34,8 @@
         out_specs=out_specs or [WHOLE] * len(outs),
         scratch_shapes=list(scratch),
         grid=grid or (),
-        compiler_params=pltpu.CompilerParams(vmem_limit_bytes=52 * 2**20),
-        cost_estimate=pl.CostEstimate(flops=flops, bytes_accessed=moved, transcendentals=extra),
+        compiler_params=pltpu.CompilerParams(vmem_limit_bytes=mib * 2**20),
+        cost_estimate=pl.CostEstimate(flops=1, bytes_accessed=1, transcendentals=0),
     )(*ins)
 
 
@@ -71,7 +73,7 @@
     early = [refs[3 * i : 3 * i + 3] for i in range(parts)]
     refs = refs[3 * parts :]
     x_refs, (wq, wk, wv, wp) = refs[:late], refs[late : late + 4]
-    weight_ref, pooled_ref, embed_ref, q_s, kt_s, v_s, w_s = refs[late + 4 :]
+    weight_ref, pooled_ref, message, q_s, kt_s, v_s, w_s = refs[late + 4 :]
     project_kernel(late, *x_refs, wq, wk, wv, q_s, kt_s, v_s)
     pieces = early + [(q_s, kt_s, v_s)]
     heads, total = w_s.shape
@@ -103,11 +105,14 @@
     pooled_ref[...] = pooled
     pooled_b = jnp.broadcast_to(pooled, (8, cols)).astype(BF16)
     embed = jnp.dot(pooled_b, wp[...], preferred_element_type=F32)[:1]
-    for i in range(embed_ref.shape[0]):
-        embed_ref[i : i + 1, :] = embed[:, i * LANES : (i + 1) * LANES]
-
-
-def pool(parts, late, weights, wp):
+    embed = jnp.concatenate(
+        [embed[:, i * LANES : (i + 1) * LANES] for i in range(message.shape[1])], axis=0
+    )
+    for i in range(message.shape[0]):
+        message[i] = embed
+
+
+def pool(parts, late, weights, wp, devices):
     d, cols = weights[0].shape
     heads = cols // HD
     fresh = sum(b.shape[0] for b in late)
@@ -116,7 +121,7 @@
     ins = [a for part in parts for a in part] + [*late, *weights, wp]
     return call(
         functools.partial(pool_kernel, len(parts), len(late)),
-        [((heads, total), BF16), ((1, cols), F32), ((bottleneck // LANES, LANES), F32)],
+        [((heads, total), BF16), ((1, cols), F32), ((devices, bottleneck // LANES, LANES), F32)],
         ins,
         2 * fresh * d * cols * 3 + 2 * total * total * cols * 4,
         heads * total * total,
@@ -126,42 +131,107 @@
             pltpu.VMEM((fresh, cols), BF16),
             pltpu.VMEM((heads, total), F32),
         ],
-    )
-
-
-def mixture_kernel(cameras, w_ref, *refs):
-    x_refs, out_ref = refs[:-1], refs[-1]
-    mix = jnp.zeros(out_ref.shape, F32)
+        mib=4 + 4 * total * total * 5 // 2**20,
+    )
+
+
+def mixture_kernel(cameras, clips, n_clip, w_ref, pooled_ref, *refs):
+    x_refs, side = refs[:-1], refs[-1]
+    heads, d = w_ref.shape[0], x_refs[0].shape[1]
+    heads_here, share = heads // clips, d // n_clip
+    mix = jnp.zeros((heads, d), F32)
     for camera in cameras:
-        m = jnp.zeros(out_ref.shape, F32)
+        m = jnp.zeros((heads, d), F32)
         for block, at in camera:
             w = w_ref[:, at : at + x_refs[block].shape[0]]
             m = m + jnp.dot(w, x_refs[block][...], preferred_element_type=F32)
         mix = mix + m.astype(BF16).astype(F32)
-    out_ref[...] = mix
-
-
-def gather_clip(tokens, n_cam):
-    clips, tok, _ = tokens.shape
+
+    def lanes(x, i):
+        x = x[:, i * share : (i + 1) * share]
+        if share == LANES:
+            return x
+        return jnp.concatenate([x, jnp.zeros((x.shape[0], LANES - share), F32)], axis=1)
+
+    for i in range(side.shape[0]):
+        j, p = divmod(i % (clips * n_clip), n_clip)
+        side[i] = jnp.concatenate(
+            [
+                jnp.zeros((DIGITS, LANES), F32),
+                lanes(pooled_ref[...], i % (pooled_ref.shape[1] // share)),
+                lanes(mix[j * heads_here : (j + 1) * heads_here], p),
+            ],
+            axis=0,
+        )
+
+
+FAR = pl.BlockSpec(memory_space=pltpu.HBM)
+
+
+def slice_kernel(plan, at, *refs):
+    ins = 1 + max(which for which, _ in plan)
+    outs, sems = refs[ins:-1], refs[-1]
+    copies = []
+    for i, (which, where) in enumerate(plan):
+        source = refs[which].at[where(at)]
+        copies.append(pltpu.make_async_copy(source, outs[i], sems.at[i]))
+        copies[-1].start()
+    for copy in copies:
+        copy.wait()
+
+
+def slices(at, arrays, plan, shapes):
+    return call(
+        functools.partial(slice_kernel, plan),
+        [(shape, BF16) for shape in shapes],
+        [at, *(pltpu.with_memory_space_constraint(a, pltpu.HBM) for a in arrays)],
+        0,
+        scratch=[pltpu.SemaphoreType.DMA((len(plan),))],
+        in_specs=[SCALARS] + [FAR] * len(arrays),
+    )
+
+
+def after(x, *others):
+    return lax.optimization_barrier((x, others))[0]
+
+
+def first_blocks(tokens, n_cam):
+    clips, tok, d = tokens.shape
     ranks = n_cam // clips
     group = lax.axis_index("cam") // ranks
     size = tok // CHUNKS
-    held = [[] for _ in range(CHUNKS + 1)]
-    for c in range(CHUNKS):
-        for s in range(1, clips):
-            start = ((group + s) % clips, c * size, 0)
-            sent = lax.dynamic_slice(tokens, start, (1, size, tokens.shape[2]))[0]
-            perm = [(i, ((i // ranks + s) % clips) * ranks + i % ranks) for i in range(n_cam)]
-            held[c + 1].append((s * ranks, lax.ppermute(sent, "cam", perm)))
-    held[0].append((0, lax.dynamic_index_in_dim(tokens, group, 0, keepdims=False)))
-    stages = []
-    for blocks in held:
-        stage = list(blocks)
-        for t in range(1, ranks):
-            perm = [(i, (i // ranks) * ranks + (i % ranks + t) % ranks) for i in range(n_cam)]
-            stage.extend((camera + t, lax.ppermute(b, "cam", perm)) for camera, b in blocks)
-        stages.append(stage)
-    return stages
+    at = jnp.stack([(group + s) % clips for s in range(clips)]).astype(jnp.int32)
+    pieces = [(s, c) for c in range(CHUNKS) for s in range(1, clips)]
+
+    def piece(s, c):
+        return 0, lambda at: (at[s], pl.ds(c * size, size), slice(None))
+
+    *sent, mine = slices(
+        at,
+        [tokens],
+        [piece(s, c) for s, c in pieces] + [(0, lambda at: (at[0], slice(None), slice(None)))],
+        [(size, d)] * len(pieces) + [(tok, d)],
+    )
+    held = [[(0, mine)]] + [[] for _ in range(CHUNKS)]
+    for (s, c), block in zip(pieces, sent):
+        perm = [(i, ((i // ranks + s) % clips) * ranks + i % ranks) for i in range(n_cam)]
+        held[c + 1].append((s * ranks, lax.ppermute(block, "cam", perm)))
+    return held
+
+
+def relay(blocks, n_cam, ranks):
+    stage = list(blocks)
+    for t in range(1, ranks):
+        perm = [(i, (i // ranks) * ranks + (i % ranks + t) % ranks) for i in range(n_cam)]
+        stage.extend((camera + t, lax.ppermute(b, "cam", perm)) for camera, b in blocks)
+    return stage
+
+
+def prototype_kernel(proto, scale, proto_b):
+    proto_f = proto[...].astype(F32)
+    norm = jnp.sqrt(jnp.sum(proto_f * proto_f, axis=0, keepdims=True) + NORM_EPS)
+    scale[...] = 1.0 / norm
+    proto_b[...] = (proto_f / norm).astype(BF16)
 
 
 def to_lanes(column, offset=0):
@@ -186,7 +256,7 @@
 
 
 def logits_kernel(
-    clips, ranks, n_clip, came, proto, proto_t, unit_ref, norm_ref, exp_ref, assign_ref, message
+    clips, ranks, n_clip, came, proto, unit_ref, norm_ref, exp_ref, assign_ref, message
 ):
     rows = []
     for g in range(clips):
@@ -204,7 +274,9 @@
     exp_ref[...] = exponents
     assign = assign / jnp.sum(assign, axis=0, keepdims=True)
     assign_ref[...] = assign
-    part = jnp.dot(exponents.astype(BF16), proto_t[...], preferred_element_type=F32)
+    part = lax.dot_general(
+        exponents.astype(BF16), proto[...], TRANSPOSED, preferred_element_type=F32
+    )
     batch = part.shape[0]
     line = to_lanes(jnp.sum(assign, axis=1, keepdims=True)) + to_lanes(
         jnp.sum(exponents, axis=1, keepdims=True), batch
@@ -233,15 +305,17 @@
 
 
 def third_kernel(
-    parity, came, assign_ref, proto_t, assign_out, keep_ref, send_ref, digits_ref, grad_ref
+    parity, came, assign_ref, proto, assign_out, keep_ref, send_ref, digits_ref, grad_ref
 ):
     batch = assign_ref.shape[0]
-    halves = proto_t.shape[1] // LANES
+    halves = proto.shape[0] // LANES
     total = jnp.sum(came[...], axis=0)[1:2]
     assign = assign_ref[...] / from_lanes(total, batch)
     assign = assign / jnp.sum(assign, axis=0, keepdims=True)
     assign_out[...] = assign
-    part = jnp.dot(assign.astype(BF16), proto_t[...], preferred_element_type=F32)
+    part = lax.dot_general(
+        assign.astype(BF16), proto[...], TRANSPOSED, preferred_element_type=F32
+    )
     half = part.shape[1] // 2
     odd = parity[0] == 1
     low, high = part[:, :half], part[:, half:]
@@ -356,27 +430,41 @@
     share = d // n_clip
     bottleneck, columns = prototypes.shape
     protos = columns * devices
-    halves = bottleneck // LANES
     cam, clip = lax.axis_index("cam"), lax.axis_index("clip")
     rank = cam % ranks
 
     with jax.named_scope("tokens_of_a_clip"):
-        stages = gather_clip(tokens.reshape(clips, tok, d), n_cam)
+        held = first_blocks(tokens.reshape(clips, tok, d), n_cam)
+
+    with jax.named_scope("prototypes"):
+        scale, proto_b = call(
+            prototype_kernel,
+            [((1, columns), F32), ((bottleneck, columns), BF16)],
+            [prototypes],
+            4 * bottleneck * columns,
+            mib=8,
+        )
 
     with jax.named_scope("pooling"):
-        weights = [
-            lax.dynamic_slice_in_dim(w, rank * cols, cols, 1) for w in (w_query, w_key, w_value)
+        columns_of = [
+            (i, lambda at: (slice(None), pl.ds(pl.multiple_of(at[0], cols), cols))) for i in range(3)
         ]
-        wp = lax.dynamic_slice_in_dim(w_proj, rank * cols, cols, 0)
-        parts = [project_blocks([b for _, b in stage], weights) for stage in stages[:-1]]
-        key_weights, pooled, embed = pool(parts, [b for _, b in stages[-1]], weights, wp)
-
-    with jax.named_scope("prototypes"):
-        proto_f = prototypes.astype(F32)
-        column_norm = jnp.sqrt(jnp.sum(proto_f * proto_f, axis=0, keepdims=True) + NORM_EPS)
-        scale = 1.0 / column_norm
-        proto_b = (proto_f / column_norm).astype(BF16)
-        proto_t = proto_b.T
+        rows_of = (3, lambda at: (pl.ds(pl.multiple_of(at[0], cols), cols), slice(None)))
+        *weights, wp = slices(
+            (rank * cols).reshape(1),
+            [w_query, w_key, w_value, w_proj],
+            columns_of + [rows_of],
+            [(d, cols)] * 3 + [(cols, bottleneck)],
+        )
+        stages, parts = [], []
+        for i, blocks in enumerate(held):
+            if i:
+                blocks = [(camera, after(b, proto_b, *parts)) for camera, b in blocks]
+            stages.append(relay(blocks, n_cam, ranks))
+            if i < CHUNKS:
+                parts.append(project_blocks([b for _, b in stages[-1]], weights))
+        late = [b for _, b in stages[-1]]
+        key_weights, pooled, message = pool(parts, late, weights, wp, devices)
 
     with jax.named_scope("mixtures"):
         cameras, blocks, at = {}, [], 0
@@ -385,20 +473,16 @@
                 cameras.setdefault(camera, []).append((len(blocks), at))
                 blocks.append(block)
                 at += block.shape[0]
-        (mix,) = call(
-            functools.partial(mixture_kernel, list(cameras.values())),
-            [((heads, d), F32)],
-            [key_weights, *blocks],
+        (side,) = call(
+            functools.partial(mixture_kernel, list(cameras.values()), clips, n_clip),
+            [((devices, DIGITS + 1 + heads_here, LANES), F32)],
+            [key_weights, pooled, *blocks],
             2 * at * d * 32,
-        )
-        mix_to = mix.reshape(clips, heads_here, n_clip, share).transpose(0, 2, 1, 3)
-        mix_to = jnp.tile(mix_to.reshape(batch, heads_here, share), (ranks, 1, 1))
-        pooled_to = jnp.tile(pooled.reshape(cols // share, 1, share), (devices * share // cols, 1, 1))
-        side = jnp.concatenate([pooled_to, mix_to], axis=1)
-        side = jnp.pad(side, ((0, 0), (DIGITS, 0), (0, LANES - share)))
+            mib=8,
+        )
 
     with jax.named_scope("logits"):
-        came = exchange(jnp.broadcast_to(embed[None], (devices,) + embed.shape))
+        came = after(exchange(message), side)
         unit, norm, exponents, assign, message = call(
             functools.partial(logits_kernel, clips, ranks, n_clip),
             [
@@ -408,7 +492,7 @@
                 ((batch, columns), F32),
                 ((devices, 2, LANES), F32),
             ],
-            [came, proto_b, proto_t],
+            [came, proto_b],
             4 * batch * bottleneck * columns,
             2 * batch * columns,
         )
@@ -434,7 +518,7 @@
                 (side.shape[1:], F32),
                 ((batch, bottleneck), F32),
             ],
-            [parity, came, assign, proto_t],
+            [parity, came, assign, proto_b],
             2 * batch * bottleneck * columns,
             in_specs=[SCALARS] + [WHOLE] * 3,
         )
@@ -478,6 +562,7 @@
             ins,
             2 * batch * bottleneck * columns,
             scratch=[pltpu.VMEM((2, batch, LANES), F32)],
+            mib=8,
             grid=(columns // block,),
             in_specs=[SCALARS] + [WHOLE] * (len(ins) - 1),
             out_specs=[

time: 108 us -> 80.9 us (0.75)
  local copies, waits for them, and re-layouts: 29.9 us -> 2.15 us
  blocking collectives: 9.32 us -> 17.8 us
  waiting for transfers between devices: 16.7 us -> 24.3 us
  other arithmetic: 5.6 us -> 0.15 us
  Pallas kernels: 28.5 us -> 23.5 us
  starting transfers between devices: 16.2 us -> 11.9 us
    unnamed x58 -> x4, local copies, waits for them, and re-layouts: 15.9 us -> 1.24 us
    all_to_all x1 -> x2, blocking collectives: 9.32 us -> 17.8 us  [exchange(): return lax.all_to_all(message, ALL, split_axis=0, concat_axis=0, tiled=True)]
    ppermute x5 -> x3, waiting for transfers between devices: 3.31 us -> 8.95 us  [the longest x1 7.04 us: first_blocks(): held[c + 1].append((s * ranks, lax.ppermute(block, 'cam', perm)))]
    pallas_call x9 -> x11, Pallas kernels: 28.5 us -> 23.5 us  [call(): pl.pallas_call(kernel, out_shape=tuple((jax.ShapeDtypeStruct(*o) for o in...]
    all_to_all x3 -> x2, starting transfers between devices: 13.1 us -> 8.71 us  [exchange(): return lax.all_to_all(message, ALL, split_axis=0, concat_axis=0, tiled=True)]
    dynamic_slice x3 -> x0, local copies, waits for them, and re-layouts: 4.1 us -> none  [the longest x2 4.08 us: local(): lax.dynamic_slice_in_dim(w, rank * cols, cols, 1)]
    squeeze x2 -> x0, local copies, waits for them, and re-layouts: 3.9 us -> none  [the longest x1 2.05 us: gather_clip(): lax.dynamic_index_in_dim(tokens, group, 0, keepdims=False)]
    convert_element_type x1 -> x0, other arithmetic: 2.58 us -> none  [local(): proto_b = (proto_f / column_norm).astype(BF16)]
  transfers between devices with their start and end apart: 9 -> 6, of which waited for: 5 -> 5; matrix products, arithmetic and copies ran while one was open for 17% -> 1% of each run, Pallas kernels for 8% -> 6%
where the time goes in v3:
time: 80.9 us; the launch traced here: 80.5 us
  waiting for transfers between devices  24.3 us (30%)
  Pallas kernels  23.5 us (29%)
  blocking collectives  17.8 us (22%)
  starting transfers between devices  11.9 us (15%)
  local copies, waits for them, and re-layouts  2.15 us (3%)
    pallas_call x11, Pallas kernels, call(): pl.pallas_call(kernel, out_shape=tuple((jax.ShapeDtypeStruct(*o) for o in...  23.5 us
    all_to_all x2, blocking collectives, exchange(): return lax.all_to_all(message, ALL, split_axis=0, concat_axis=0, tiled=True)  17.8 us
    all_to_all x2, waiting for transfers between devices, exchange(): return lax.all_to_all(message, ALL, split_axis=0, concat_axis=0, tiled=True)  14.3 us
    all_to_all x2, starting transfers between devices, exchange(): return lax.all_to_all(message, ALL, split_axis=0, concat_axis=0, tiled=True)  8.71 us
    ppermute x1, waiting for transfers between devices, first_blocks(): held[c + 1].append((s * ranks, lax.ppermute(block, 'cam', perm)))  7.04 us
    ppermute x1, starting transfers between devices, first_blocks(): held[c + 1].append((s * ranks, lax.ppermute(block, 'cam', perm)))  2.56 us
    ppermute x2, waiting for transfers between devices, relay(): lax.ppermute(b, 'cam', perm)  1.91 us
  transfers between devices with their start and end apart: 6, of which 5 were waited for; matrix products, arithmetic and copies ran while one was open for 1% of the time, Pallas kernels for 6%

profile of v3, /device:TPU:0, one launch (start us, length us, event | category | flops | bytes accessed | tf_op | source)
XLA Modules:
  0.0 80.5 jit_solution(13462574295047524630)
XLA Ops:
  0.7 0.1 pad_add_fusion.1.at
  0.8 1.8 %tokens_of_a_clip.1 = (bf16[256,1024]{1,0:T(8,128)(2,1)S(1)}, bf16[256,1024]{1,0:T(8,128)(2,1)S(1)}) custom-call(s32[2]{0:T(128)S(1)} %pad_add_fusion.1.at, bf16[2,256,1024]{2,1,0:T(8,128)(2,1)} %bitcast.9), custom_call_target="tpu_custom_call" | custom-call | flops 1 | bytes 1 | tf_op jit(solution)/shard_map/tokens_of_a_clip/pallas_call | solution.py:30
  2.5 0.5 collective-permute-start
  3.0 2.6 %collective-permute-start.1 = (bf16[256,1024]{1,0:T(8,128)(2,1)S(1)}, bf16[256,1024]{1,0:T(8,128)(2,1)S(1)}, u32[]{:S(2)}, u32[]{:S(2)}) collective-permute-start(bf16[256,1024]{1,0:T(8,128)(2,1)S(1)} %get-tuple-element.40), channel_id=1, source_target_pairs={{0,16},{8,24},{16,0},{24,8},{1,17},{9,25},{17,1},{25,9},{2,18},{10... | collective-permute-start | bytes 1572872 | tf_op jit(solution)/shard_map/tokens_of_a_clip/ppermute | solution.py:218
  5.6 0.0 copy-start
  5.6 1.2 %copy-done = bf16[256,2048]{1,0:T(8,128)(2,1)S(1)} copy-done((bf16[256,2048]{1,0:T(8,128)(2,1)S(1)}, bf16[256,2048]{1,0:T(8,128)(2,1)}, u32[]{:S(2)}) %copy-start) | copy-done | bytes 1048600
  6.8 0.4 prototypes.1
  7.2 2.0 %pooling.3 = (bf16[1024,512]{1,0:T(8,128)(2,1)S(1)}, bf16[1024,512]{1,0:T(8,128)(2,1)S(1)}, bf16[1024,512]{1,0:T(8,128)(2,1)S(1)}, bf16[512,256]{1,0:T(8,128)(2,1)S(1)}) custom-call(s32[1]{0:T(128)} %bitcast.6.at, bf16[1024,1024]{1,0:T(8,128)(2,1)} %refs_0_.1, bf16[1024,1024]{1,0:T(8,128)(2,1)} %refs_1_.1, bf16[1024,1024]{1,0:T(8,128)(2,1)} %refs_2_.1, ...), custom_call_target="tpu_custom_call" | custom-call | flops 1 | bytes 1 | tf_op jit(solution)/shard_map/pooling/pallas_call | solution.py:30
  9.2 0.0 collective-permute-done.refs_1_
  9.3 1.8 %pooling.4 = (bf16[512,512]{1,0:T(8,128)(2,1)S(1)}, bf16[512,512]{1,0:T(8,128)(2,1)S(1)}, bf16[512,512]{1,0:T(8,128)(2,1)S(1)}) custom-call(bf16[256,1024]{1,0:T(8,128)(2,1)S(1)} %get-tuple-element.33.refs_0_, bf16[256,1024]{1,0:T(8,128)(2,1)S(1)} %collective-permute-done.refs_1_, bf16[1024,512]{1,0:T(8,128)(2,1)S(1)} %get-tuple-element.34.refs_2_.refs_5_, ...), custom_call_target="tpu_custom_call" | custom-call | flops 1 | bytes 1 | tf_op jit(solution)/shard_map/pooling/pallas_call | solution.py:30
  11.1 7.0 %collective-permute-done.1.refs_3_.refs_2_ = bf16[256,1024]{1,0:T(8,128)(2,1)S(1)} collective-permute-done((bf16[256,1024]{1,0:T(8,128)(2,1)S(1)}, bf16[256,1024]{1,0:T(8,128)(2,1)S(1)}, u32[]{:S(2)}, u32[]{:S(2)}) %collective-permute-start.1) | collective-permute-done | bytes 524320 | tf_op jit(solution)/shard_map/tokens_of_a_clip/ppermute | solution.py:218
  18.1 0.0 collective-permute-start.2
  18.1 1.9 %collective-permute-done.2.refs_4_.refs_3_ = bf16[256,1024]{1,0:T(8,128)(2,1)S(1)} collective-permute-done((bf16[256,1024]{1,0:T(8,128)(2,1)S(1)}, bf16[256,1024]{1,0:T(8,128)(2,1)S(1)}, u32[]{:S(2)}, u32[]{:S(2)}) %collective-permute-start.2) | collective-permute-done | bytes 524320 | tf_op jit(solution)/shard_map/pooling/ppermute | solution.py:226
  20.0 11.2 %pooling.5 = (bf16[8,1024]{1,0:T(8,128)(2,1)S(1)}, f32[1,512]{1,0:T(1,128)S(1)}, f32[32,2,128]{2,1,0:T(2,128)}) custom-call(bf16[512,512]{1,0:T(8,128)(2,1)S(1)} %get-tuple-element.37.refs_0_, bf16[512,512]{1,0:T(8,128)(2,1)S(1)} %get-tuple-element.38.refs_1_, bf16[512,512]{1,0:T(8,128)(2,1)S(1)} %get-tuple-element.39.refs_2_, ...), custom_call_target="tpu_custom_call" | custom-call | flops 1 | bytes 1 | tf_op jit(solution)/shard_map/pooling/pallas_call | solution.py:30
  31.2 6.1 %all-to-all-start = ((f32[32,2,128]{2,1,0:T(2,128)}), f32[32,2,128]{2,1,0:T(2,128)S(1)}, u32[]{:S(2)}, u32[]{:S(2)}) async-start(f32[32,2,128]{2,1,0:T(2,128)} %get-tuple-element.44), calls=%async_computation | async-start | bytes 65536 | tf_op jit(solution)/shard_map/logits/all_to_all | solution.py:255
  37.3 0.4 mixtures.1.side
  37.7 0.0 copy-start.1
  37.7 6.8 %all-to-all-done.came = f32[32,2,128]{2,1,0:T(2,128)S(1)} async-done(((f32[32,2,128]{2,1,0:T(2,128)}), f32[32,2,128]{2,1,0:T(2,128)S(1)}, u32[]{:S(2)}, u32[]{:S(2)}) %all-to-all-start) | async-done | bytes 32800 | tf_op jit(solution)/shard_map/logits/all_to_all | solution.py:255
  44.5 0.6 logits.1
  45.1 8.9 %all_to_all.20.came = f32[32,2,128]{2,1,0:T(2,128)S(1)} all-to-all(f32[32,2,128]{2,1,0:T(2,128)S(1)} %get-tuple-element.48), channel_id=1, replica_groups=mesh['cam'=4,'clip'=8] {'cam','clip'}, dimensions={0} | all-to-all | bytes 65536 | tf_op jit(solution)/shard_map/row_total_1/all_to_all | solution.py:255
  54.0 0.2 row_total_1.1
  54.3 8.9 %all_to_all.21.came = f32[32,2,128]{2,1,0:T(2,128)S(1)} all-to-all(f32[32,2,128]{2,1,0:T(2,128)S(1)} %get-tuple-element.50), channel_id=1, replica_groups=mesh['cam'=4,'clip'=8] {'cam','clip'}, dimensions={0} | all-to-all | bytes 65536 | tf_op jit(solution)/shard_map/row_total_2/all_to_all | solution.py:255
  63.1 0.4 row_total_2.1
  63.6 0.1 collective-permute-start.3
  63.7 1.1 %collective-permute-done.3.got = f32[16,128]{1,0:T(8,128)S(1)} collective-permute-done((f32[16,128]{1,0:T(8,128)S(1)}, f32[16,128]{1,0:T(8,128)S(1)}, u32[]{:S(2)}, u32[]{:S(2)}) %collective-permute-start.3) | collective-permute-done | bytes 8224 | tf_op jit(solution)/shard_map/row_total_3/ppermute | solution.py:527
  64.8 0.7 row_total_3.1
  65.5 2.6 %all-to-all-start.3 = ((bf16[32,24,128]{2,1,0:T(8,128)(2,1)}), bf16[32,24,128]{2,1,0:T(8,128)(2,1)S(1)}, u32[]{:S(2)}, u32[]{:S(2)}) async-start(bf16[32,24,128]{2,1,0:T(8,128)(2,1)} %row_total_3.1), calls=%async_computation.3 | async-start | bytes 393216 | tf_op jit(solution)/shard_map/row_total_3/all_to_all | solution.py:255
  68.1 0.1 pad_add_fusion.pick
  68.2 0.9 %constant_dynamic-slice_fusion.wp = bf16[256,256]{1,0:T(8,128)(2,1)S(1)} fusion(bf16[1024,256]{1,0:T(8,128)(2,1)} %refs_3_.1, s32[]{:T(128)S(6)} %select_n.33), kind=kLoop, calls=%fused_computation.2 | loop fusion | bytes 262148 | tf_op jit(solution)/shard_map/outputs/dynamic_slice | solution.py:539
  69.1 7.5 %all-to-all-done.3 = bf16[32,24,128]{2,1,0:T(8,128)(2,1)S(1)} async-done(((bf16[32,24,128]{2,1,0:T(8,128)(2,1)}), bf16[32,24,128]{2,1,0:T(8,128)(2,1)S(1)}, u32[]{:S(2)}, u32[]{:S(2)}) %all-to-all-start.3) | async-done | bytes 196640 | tf_op jit(solution)/shard_map/row_total_3/all_to_all | solution.py:255
  76.6 0.0 copy-done.1
  76.6 3.9 %outputs.1 = (f32[16,2048]{1,0:T(8,128)}, f32[256,2048]{1,0:T(8,128)}, f32[128,256]{1,0:T(8,128)}, f32[128,256]{1,0:T(8,128)}) custom-call(s32[2]{0:T(128)S(1)} %pad_add_fusion.pick, bf16[2,2,8,24,128]{4,3,2,1,0:T(8,128)(2,1)S(1)} %bitcast.8, f32[16,256]{1,0:T(8,128)S(1)} %get-tuple-element.55.unit_ref, f32[16,128]{1,0:T(8,128)S(1)} %get-tuple-element.56.norm_ref, ...), custom_call_target="tpu_custom_call" | custom-call | flops 1 | bytes 1 | tf_op jit(solution)/shard_map/outputs/pallas_call | solution.py:30
Async XLA Ops:
  2.5 6.7 %collective-permute-start = (bf16[256,1024]{1,0:T(8,128)(2,1)S(1)}, bf16[256,1024]{1,0:T(8,128)(2,1)S(1)}, u32[]{:S(2)}, u32[]{:S(2)}) collective-permute-start(bf16[256,1024]{1,0:T(8,128)(2,1)S(1)} %get-tuple-element.33.refs_0_), channel_id=1, source_target_pairs={{0,8},{8,0},{16,24},{24,16},{1,9},{9,1},{17,25},{25,17},{2,10},{10... | collective-permute-start | bytes 1572872 | tf_op jit(solution)/shard_map/pooling/ppermute | solution.py:226
  3.0 15.1 %collective-permute-start.1 = (bf16[256,1024]{1,0:T(8,128)(2,1)S(1)}, bf16[256,1024]{1,0:T(8,128)(2,1)S(1)}, u32[]{:S(2)}, u32[]{:S(2)}) collective-permute-start(bf16[256,1024]{1,0:T(8,128)(2,1)S(1)} %get-tuple-element.40), channel_id=1, source_target_pairs={{0,16},{8,24},{16,0},{24,8},{1,17},{9,25},{17,1},{25,9},{2,18},{10... | collective-permute-start | bytes 1572872 | tf_op jit(solution)/shard_map/tokens_of_a_clip/ppermute | solution.py:218
  5.6 1.2 %copy-start = (bf16[256,2048]{1,0:T(8,128)(2,1)S(1)}, bf16[256,2048]{1,0:T(8,128)(2,1)}, u32[]{:S(2)}) copy-start(bf16[256,2048]{1,0:T(8,128)(2,1)} %proto.3) | copy-start | bytes 3145732
  18.1 1.9 %collective-permute-start.2 = (bf16[256,1024]{1,0:T(8,128)(2,1)S(1)}, bf16[256,1024]{1,0:T(8,128)(2,1)S(1)}, u32[]{:S(2)}, u32[]{:S(2)}) collective-permute-start(bf16[256,1024]{1,0:T(8,128)(2,1)S(1)} %collective-permute-done.1.refs_3_.refs_2_), channel_id=1, source_target_pairs={{0,8},{8,0},{16,24},{24,16},{1,9},{9,1},{17,25},{25,17},{2,10},{10... | collective-permute-start | bytes 1572872 | tf_op jit(solution)/shard_map/pooling/ppermute | solution.py:226
  31.2 13.3 %all-to-all-start = ((f32[32,2,128]{2,1,0:T(2,128)}), f32[32,2,128]{2,1,0:T(2,128)S(1)}, u32[]{:S(2)}, u32[]{:S(2)}) async-start(f32[32,2,128]{2,1,0:T(2,128)} %get-tuple-element.44), calls=%async_computation | async-start | bytes 65536 | tf_op jit(solution)/shard_map/logits/all_to_all | solution.py:255
  37.7 38.9 %copy-start.1 = (bf16[256,2048]{1,0:T(8,128)(2,1)S(1)}, bf16[256,2048]{1,0:T(8,128)(2,1)}, u32[]{:S(2)}) copy-start(bf16[256,2048]{1,0:T(8,128)(2,1)} %proto.3) | copy-start | bytes 3145732
  63.6 1.2 %collective-permute-start.3 = (f32[16,128]{1,0:T(8,128)S(1)}, f32[16,128]{1,0:T(8,128)S(1)}, u32[]{:S(2)}, u32[]{:S(2)}) collective-permute-start(f32[16,128]{1,0:T(8,128)S(1)} %get-tuple-element.53), channel_id=1, source_target_pairs={{0,8},{8,0},{16,24},{24,16},{1,9},{9,1},{17,25},{25,17},{2,10},{10... | collective-permute-start | bytes 24584 | tf_op jit(solution)/shard_map/row_total_3/ppermute | solution.py:527
  65.5 11.1 %all-to-all-start.3 = ((bf16[32,24,128]{2,1,0:T(8,128)(2,1)}), bf16[32,24,128]{2,1,0:T(8,128)(2,1)S(1)}, u32[]{:S(2)}, u32[]{:S(2)}) async-start(bf16[32,24,128]{2,1,0:T(8,128)(2,1)} %row_total_3.1), calls=%async_computation.3 | async-start | bytes 393216 | tf_op jit(solution)/shard_map/row_total_3/all_to_all | solution.py:255

commit v4 on v3

--- a/solution.py
+++ b/solution.py
@@ -195,28 +195,26 @@
     return lax.optimization_barrier((x, others))[0]
 
 
-def first_blocks(tokens, n_cam):
+def token_piece(s, c, size):
+    return lambda at: (at[s], pl.ds(c * size, size), slice(None))
+
+
+def from_other_groups(tokens, groups, n_cam):
     clips, tok, d = tokens.shape
     ranks = n_cam // clips
-    group = lax.axis_index("cam") // ranks
     size = tok // CHUNKS
-    at = jnp.stack([(group + s) % clips for s in range(clips)]).astype(jnp.int32)
     pieces = [(s, c) for c in range(CHUNKS) for s in range(1, clips)]
-
-    def piece(s, c):
-        return 0, lambda at: (at[s], pl.ds(c * size, size), slice(None))
-
     *sent, mine = slices(
-        at,
+        groups,
         [tokens],
-        [piece(s, c) for s, c in pieces] + [(0, lambda at: (at[0], slice(None), slice(None)))],
+        [(0, token_piece(s, c, size)) for s, c in pieces] + [(0, token_piece(0, 0, tok))],
         [(size, d)] * len(pieces) + [(tok, d)],
     )
-    held = [[(0, mine)]] + [[] for _ in range(CHUNKS)]
+    held = [[] for _ in range(CHUNKS)]
     for (s, c), block in zip(pieces, sent):
         perm = [(i, ((i // ranks + s) % clips) * ranks + i % ranks) for i in range(n_cam)]
-        held[c + 1].append((s * ranks, lax.ppermute(block, "cam", perm)))
-    return held
+        held[c].append((s * ranks, lax.ppermute(block, "cam", perm)))
+    return mine, held
 
 
 def relay(blocks, n_cam, ranks):
@@ -342,6 +340,7 @@
 def output_kernel(
     protos,
     n_cam,
+    block,
     pick,
     came,
     unit_ref,
@@ -353,69 +352,79 @@
     proto,
     scale,
     wp,
+    codes_out,
+    proto_grad_out,
+    grad_proj_out,
+    grad_value_out,
     codes,
     proto_grad,
     grad_proj,
     grad_value,
-    factor_s,
+    sems,
 ):
     clips, ranks, n_clip = came.shape[:3]
-    batch = unit_ref.shape[0]
+    batch, columns = exp_ref.shape
     share = grad_proj.shape[0]
-    width = codes.shape[1]
-    step = pl.program_id(0)
-
-    @pl.when(step == 0)
-    def _():
-        sums = [jnp.zeros(came.shape[3:], F32) for _ in range(2)]
-        for cam in range(n_cam):
-            part = jnp.sum(came[cam // ranks, cam % ranks].astype(F32), axis=0)
-            sums[cam % 2] = sums[cam % 2] + part
-        line = jnp.sum((sums[0] + sums[1])[batch : batch + DIGITS], axis=0, keepdims=True)
-        by_assign = protos / from_lanes(line, batch)
-        by_prob = protos / total_ref[:, :1]
-        factor_s[0] = spread(by_prob)
-        factor_s[1] = spread(by_assign)
-        assign_grad = jnp.concatenate([s[:batch] for s in sums], axis=1)
-        grad_unit = prob_grad[...] * by_prob - assign_grad * by_assign
-        unit = unit_ref[...]
-        grad_embed = (
-            grad_unit - unit * jnp.sum(unit * grad_unit, axis=1, keepdims=True)
-        ) / norm_ref[:, :1]
-        grad_embed = grad_embed.astype(BF16)
-
-        def rows(rank, at):
-            picked = [came[g, rank].astype(F32)[:, at, :] for g in range(clips)]
-            return jnp.concatenate(picked, axis=0)[:, :share].astype(BF16)
-
-        grad_proj[...] = lax.dot_general(
-            rows(pick[0], batch + DIGITS), grad_embed, OUTER, preferred_element_type=F32
-        )
-        grad_pooled = lax.dot_general(
-            grad_embed, wp[...], TRANSPOSED, preferred_element_type=F32
-        ).astype(BF16)
-        col_head = lax.broadcasted_iota(jnp.int32, grad_value.shape, 1) // HD
-        value = jnp.zeros(grad_value.shape, F32)
-        for head in range(grad_value.shape[1] // HD):
-            mixed = rows(pick[1], batch + DIGITS + 1 + head)
-            out = lax.dot_general(mixed, grad_pooled, OUTER, preferred_element_type=F32)
-            value = jnp.where(col_head == head, out, value)
-        grad_value[...] = value
-
-    here = pl.ds(pl.multiple_of(step * width, width), width)
-    assign = assign_ref[:, here] * factor_s[1][:, :1]
-    grad_logits = (exp_ref[:, here] * factor_s[0][:, :1] - assign).astype(BF16)
-    for g in range(clips):
-        for p in range(n_clip):
-            at = g * n_clip + p
-            codes[p * clips + g : p * clips + g + 1, :] = assign[at : at + 1]
-    grad = lax.dot_general(
-        unit_ref[...].astype(BF16), grad_logits, OUTER, preferred_element_type=F32
-    )
-    inverse = scale[:, here]
-    unit_proto = proto[:, here].astype(F32) * inverse
-    along = jnp.sum(unit_proto * grad, axis=0, keepdims=True)
-    proto_grad[...] = (grad - unit_proto * along) * inverse
+    copies = []
+
+    def send(source, target):
+        copies.append(pltpu.make_async_copy(source, target, sems.at[len(copies)]))
+        copies[-1].start()
+
+    sums = [jnp.zeros(came.shape[3:], F32) for _ in range(2)]
+    for cam in range(n_cam):
+        part = jnp.sum(came[cam // ranks, cam % ranks].astype(F32), axis=0)
+        sums[cam % 2] = sums[cam % 2] + part
+    line = jnp.sum((sums[0] + sums[1])[batch : batch + DIGITS], axis=0, keepdims=True)
+    by_assign = protos / from_lanes(line, batch)
+    by_prob = protos / total_ref[:, :1]
+    unit = unit_ref[...]
+    unit_b = unit.astype(BF16)
+
+    for start in range(0, columns, block):
+        here = slice(start, start + block)
+        assign = assign_ref[:, here] * by_assign
+        grad_logits = (exp_ref[:, here] * by_prob - assign).astype(BF16)
+        for g in range(clips):
+            for p in range(n_clip):
+                at, to = g * n_clip + p, p * clips + g
+                codes[to : to + 1, here] = assign[at : at + 1]
+        grad = lax.dot_general(unit_b, grad_logits, OUTER, preferred_element_type=F32)
+        inverse = scale[:, here]
+        unit_proto = proto[:, here].astype(F32) * inverse
+        along = jnp.sum(unit_proto * grad, axis=0, keepdims=True)
+        proto_grad[:, here] = (grad - unit_proto * along) * inverse
+        send(proto_grad.at[:, here], proto_grad_out.at[:, here])
+    send(codes, codes_out)
+
+    assign_grad = jnp.concatenate([s[:batch] for s in sums], axis=1)
+    grad_unit = prob_grad[...] * by_prob - assign_grad * by_assign
+    grad_embed = (
+        grad_unit - unit * jnp.sum(unit * grad_unit, axis=1, keepdims=True)
+    ) / norm_ref[:, :1]
+    grad_embed = grad_embed.astype(BF16)
+
+    def rows(rank, at):
+        picked = [came[g, rank].astype(F32)[:, at, :] for g in range(clips)]
+        return jnp.concatenate(picked, axis=0)[:, :share].astype(BF16)
+
+    grad_proj[...] = lax.dot_general(
+        rows(pick[0], batch + DIGITS), grad_embed, OUTER, preferred_element_type=F32
+    )
+    send(grad_proj, grad_proj_out)
+    grad_pooled = lax.dot_general(
+        grad_embed, wp[...], TRANSPOSED, preferred_element_type=F32
+    ).astype(BF16)
+    col_head = lax.broadcasted_iota(jnp.int32, grad_value.shape, 1) // HD
+    value = jnp.zeros(grad_value.shape, F32)
+    for head in range(grad_value.shape[1] // HD):
+        mixed = rows(pick[1], batch + DIGITS + 1 + head)
+        out = lax.dot_general(mixed, grad_pooled, OUTER, preferred_element_type=F32)
+        value = jnp.where(col_head == head, out, value)
+    grad_value[...] = value
+    send(grad_value, grad_value_out)
+    for copy in copies:
+        copy.wait()
 
 
 def local(tokens, w_query, w_key, w_value, w_proj, prototypes):
@@ -434,7 +443,10 @@
     rank = cam % ranks
 
     with jax.named_scope("tokens_of_a_clip"):
-        held = first_blocks(tokens.reshape(clips, tok, d), n_cam)
+        tokens = tokens.reshape(clips, tok, d)
+        groups = [(cam // ranks + s) % clips for s in range(clips)]
+        groups = jnp.stack(groups + [rank * cols]).astype(jnp.int32)
+        mine, held = from_other_groups(tokens, groups, n_cam)
 
     with jax.named_scope("prototypes"):
         scale, proto_b = call(
@@ -446,24 +458,28 @@
         )
 
     with jax.named_scope("pooling"):
-        columns_of = [
-            (i, lambda at: (slice(None), pl.ds(pl.multiple_of(at[0], cols), cols))) for i in range(3)
-        ]
-        rows_of = (3, lambda at: (pl.ds(pl.multiple_of(at[0], cols), cols), slice(None)))
+        def columns_of(at):
+            return slice(None), pl.ds(pl.multiple_of(at[clips], cols), cols)
+
+        def rows_of(at):
+            return pl.ds(pl.multiple_of(at[clips], cols), cols), slice(None)
+
         *weights, wp = slices(
-            (rank * cols).reshape(1),
+            groups,
             [w_query, w_key, w_value, w_proj],
-            columns_of + [rows_of],
+            [(i, columns_of) for i in range(3)] + [(3, rows_of)],
             [(d, cols)] * 3 + [(cols, bottleneck)],
         )
-        stages, parts = [], []
-        for i, blocks in enumerate(held):
-            if i:
-                blocks = [(camera, after(b, proto_b, *parts)) for camera, b in blocks]
+        stages, parts = [relay([(0, mine)], n_cam, ranks)], []
+        parts.append(project_blocks([b for _, b in stages[0]], weights))
+        for blocks in held:
+            blocks = [(camera, after(b, proto_b, *parts)) for camera, b in blocks]
             stages.append(relay(blocks, n_cam, ranks))
-            if i < CHUNKS:
+            if blocks is not held[-1] and len(stages) <= CHUNKS:
                 parts.append(project_blocks([b for _, b in stages[-1]], weights))
-        late = [b for _, b in stages[-1]]
+        own = len(held[-1])
+        parts.append(project_blocks([b for _, b in stages[-1][:own]], weights))
+        late = [b for _, b in stages[-1][own:]]
         key_weights, pooled, message = pool(parts, late, weights, wp, devices)
 
     with jax.named_scope("mixtures"):
@@ -551,26 +567,22 @@
             scale,
             proj_rows,
         ]
+        outs = [
+            ((batch, columns), F32),
+            ((bottleneck, columns), F32),
+            ((share, bottleneck), F32),
+            ((share, width), F32),
+        ]
         return call(
-            functools.partial(output_kernel, protos, n_cam),
-            [
-                ((batch, columns), F32),
-                ((bottleneck, columns), F32),
-                ((share, bottleneck), F32),
-                ((share, width), F32),
-            ],
+            functools.partial(output_kernel, protos, n_cam, block),
+            outs,
             ins,
             2 * batch * bottleneck * columns,
-            scratch=[pltpu.VMEM((2, batch, LANES), F32)],
+            scratch=[pltpu.VMEM(*o) for o in outs]
+            + [pltpu.SemaphoreType.DMA((columns // block + 3,))],
+            in_specs=[SCALARS] + [WHOLE] * (len(ins) - 1),
+            out_specs=[FAR] * len(outs),
             mib=8,
-            grid=(columns // block,),
-            in_specs=[SCALARS] + [WHOLE] * (len(ins) - 1),
-            out_specs=[
-                pl.BlockSpec((batch, block), lambda i: (0, i)),
-                pl.BlockSpec((bottleneck, block), lambda i: (0, i)),
-                pl.BlockSpec((share, bottleneck), lambda i: (0, 0)),
-                pl.BlockSpec((share, width), lambda i: (0, 0)),
-            ],
         )
 
 

time: 80.9 us -> 78.7 us (0.973)
  waiting for transfers between devices: 24.3 us -> 22.8 us
    ppermute x2, waiting for transfers between devices: 1.91 us -> 0.91 us  [relay(): lax.ppermute(b, 'cam', perm)]
    pallas_call x11 -> x12, Pallas kernels: 23.5 us -> 22.8 us  [call(): pl.pallas_call(kernel, out_shape=tuple((jax.ShapeDtypeStruct(*o) for o in...]
  transfers between devices with their start and end apart: 6 -> 6, of which waited for: 5 -> 5; matrix products, arithmetic and copies ran while one was open for 1% -> 1% of each run, Pallas kernels for 6% -> 8%
where the time goes in v4:
time: 78.7 us; the launch traced here: 78.4 us
  Pallas kernels  22.8 us (29%)
  waiting for transfers between devices  22.8 us (29%)
  blocking collectives  17.8 us (23%)
  starting transfers between devices  11.9 us (15%)
  local copies, waits for them, and re-layouts  2.15 us (3%)
  between operations  0.8 us (1%)
    pallas_call x12, Pallas kernels, call(): pl.pallas_call(kernel, out_shape=tuple((jax.ShapeDtypeStruct(*o) for o in...  22.8 us
    all_to_all x2, blocking collectives, exchange(): return lax.all_to_all(message, ALL, split_axis=0, concat_axis=0, tiled=True)  17.8 us
    all_to_all x2, waiting for transfers between devices, exchange(): return lax.all_to_all(message, ALL, split_axis=0, concat_axis=0, tiled=True)  14.3 us
    all_to_all x2, starting transfers between devices, exchange(): return lax.all_to_all(message, ALL, split_axis=0, concat_axis=0, tiled=True)  8.68 us
    ppermute x1, waiting for transfers between devices, from_other_groups(): held[c].append((s * ranks, lax.ppermute(block, 'cam', perm)))  6.51 us
    ppermute x1, starting transfers between devices, from_other_groups(): held[c].append((s * ranks, lax.ppermute(block, 'cam', perm)))  2.56 us
  transfers between devices with their start and end apart: 6, of which 5 were waited for; matrix products, arithmetic and copies ran while one was open for 1% of the time, Pallas kernels for 8%

profile of v4, /device:TPU:0, one launch (start us, length us, event | category | flops | bytes accessed | tf_op | source)
XLA Modules:
  0.0 78.4 jit_solution(14362460696219382814)
XLA Ops:
  0.7 0.1 pad_add_fusion.1.at
  0.8 1.8 %tokens_of_a_clip.1 = (bf16[256,1024]{1,0:T(8,128)(2,1)S(1)}, bf16[256,1024]{1,0:T(8,128)(2,1)S(1)}) custom-call(s32[3]{0:T(128)S(1)} %pad_add_fusion.1.at, bf16[2,256,1024]{2,1,0:T(8,128)(2,1)} %bitcast.9), custom_call_target="tpu_custom_call" | custom-call | flops 1 | bytes 1 | tf_op jit(solution)/shard_map/tokens_of_a_clip/pallas_call | solution.py:30
  2.5 0.5 collective-permute-start
  3.0 2.6 %collective-permute-start.1 = (bf16[256,1024]{1,0:T(8,128)(2,1)S(1)}, bf16[256,1024]{1,0:T(8,128)(2,1)S(1)}, u32[]{:S(2)}, u32[]{:S(2)}) collective-permute-start(bf16[256,1024]{1,0:T(8,128)(2,1)S(1)} %get-tuple-element.43), channel_id=1, source_target_pairs={{0,16},{8,24},{16,0},{24,8},{1,17},{9,25},{17,1},{25,9},{2,18},{10... | collective-permute-start | bytes 1572872 | tf_op jit(solution)/shard_map/tokens_of_a_clip/ppermute | solution.py:216
  5.6 0.0 copy-start
  5.6 1.2 %copy-done = bf16[256,2048]{1,0:T(8,128)(2,1)S(1)} copy-done((bf16[256,2048]{1,0:T(8,128)(2,1)S(1)}, bf16[256,2048]{1,0:T(8,128)(2,1)}, u32[]{:S(2)}) %copy-start) | copy-done | bytes 1048600
  6.8 0.4 prototypes.1
  7.2 2.6 %pooling.4 = (bf16[1024,512]{1,0:T(8,128)(2,1)S(1)}, bf16[1024,512]{1,0:T(8,128)(2,1)S(1)}, bf16[1024,512]{1,0:T(8,128)(2,1)S(1)}, bf16[512,256]{1,0:T(8,128)(2,1)S(1)}) custom-call(s32[3]{0:T(128)S(1)} %pad_add_fusion.1.at, bf16[1024,1024]{1,0:T(8,128)(2,1)} %refs_0_.1, bf16[1024,1024]{1,0:T(8,128)(2,1)} %refs_1_.1, bf16[1024,1024]{1,0:T(8,128)(2,1)} %refs_2_.1, ...), custom_call_target="tpu_custom_call" | custom-call | flops 1 | bytes 1 | tf_op jit(solution)/shard_map/pooling/pallas_call | solution.py:30
  9.8 0.0 collective-permute-done.refs_1_
  9.8 1.8 %pooling.5 = (bf16[512,512]{1,0:T(8,128)(2,1)S(1)}, bf16[512,512]{1,0:T(8,128)(2,1)S(1)}, bf16[512,512]{1,0:T(8,128)(2,1)S(1)}) custom-call(bf16[256,1024]{1,0:T(8,128)(2,1)S(1)} %get-tuple-element.36.refs_0_, bf16[256,1024]{1,0:T(8,128)(2,1)S(1)} %collective-permute-done.refs_1_, bf16[1024,512]{1,0:T(8,128)(2,1)S(1)} %get-tuple-element.37.refs_2_.refs_1_.refs_7_, ...), custom_call_target="tpu_custom_call" | custom-call | flops 1 | bytes 1 | tf_op jit(solution)/shard_map/pooling/pallas_call | solution.py:30
  11.6 6.5 %collective-permute-done.1.refs_0_.refs_2_ = bf16[256,1024]{1,0:T(8,128)(2,1)S(1)} collective-permute-done((bf16[256,1024]{1,0:T(8,128)(2,1)S(1)}, bf16[256,1024]{1,0:T(8,128)(2,1)S(1)}, u32[]{:S(2)}, u32[]{:S(2)}) %collective-permute-start.1) | collective-permute-done | bytes 524320 | tf_op jit(solution)/shard_map/tokens_of_a_clip/ppermute | solution.py:216
  18.1 0.0 collective-permute-start.2
  18.1 1.0 %pooling.6 = (bf16[256,512]{1,0:T(8,128)(2,1)S(1)}, bf16[512,256]{1,0:T(8,128)(2,1)S(1)}, bf16[256,512]{1,0:T(8,128)(2,1)S(1)}) custom-call(bf16[256,1024]{1,0:T(8,128)(2,1)S(1)} %collective-permute-done.1.refs_0_.refs_2_, bf16[1024,512]{1,0:T(8,128)(2,1)S(1)} %get-tuple-element.37.refs_2_.refs_1_.refs_7_, ...), custom_call_target="tpu_custom_call" | custom-call | flops 1 | bytes 1 | tf_op jit(solution)/shard_map/pooling/pallas_call | solution.py:30
  19.1 0.9 %collective-permute-done.2.refs_6_.refs_3_ = bf16[256,1024]{1,0:T(8,128)(2,1)S(1)} collective-permute-done((bf16[256,1024]{1,0:T(8,128)(2,1)S(1)}, bf16[256,1024]{1,0:T(8,128)(2,1)S(1)}, u32[]{:S(2)}, u32[]{:S(2)}) %collective-permute-start.2) | collective-permute-done | bytes 524320 | tf_op jit(solution)/shard_map/pooling/ppermute | solution.py:224
  20.0 10.4 %pooling.7 = (bf16[8,1024]{1,0:T(8,128)(2,1)S(1)}, f32[1,512]{1,0:T(1,128)S(1)}, f32[32,2,128]{2,1,0:T(2,128)}) custom-call(bf16[512,512]{1,0:T(8,128)(2,1)S(1)} %get-tuple-element.40.refs_0_, bf16[512,512]{1,0:T(8,128)(2,1)S(1)} %get-tuple-element.41.refs_1_, bf16[512,512]{1,0:T(8,128)(2,1)S(1)} %get-tuple-element.42.refs_2_, ...), custom_call_target="tpu_custom_call" | custom-call | flops 1 | bytes 1 | tf_op jit(solution)/shard_map/pooling/pallas_call | solution.py:30
  30.4 6.1 %all-to-all-start = ((f32[32,2,128]{2,1,0:T(2,128)}), f32[32,2,128]{2,1,0:T(2,128)S(1)}, u32[]{:S(2)}, u32[]{:S(2)}) async-start(f32[32,2,128]{2,1,0:T(2,128)} %get-tuple-element.50), calls=%async_computation | async-start | bytes 65536 | tf_op jit(solution)/shard_map/logits/all_to_all | solution.py:253
  36.5 0.4 mixtures.1.side
  36.9 0.0 copy-start.1
  36.9 6.8 %all-to-all-done.came = f32[32,2,128]{2,1,0:T(2,128)S(1)} async-done(((f32[32,2,128]{2,1,0:T(2,128)}), f32[32,2,128]{2,1,0:T(2,128)S(1)}, u32[]{:S(2)}, u32[]{:S(2)}) %all-to-all-start) | async-done | bytes 32800 | tf_op jit(solution)/shard_map/logits/all_to_all | solution.py:253
  43.7 0.6 logits.1
  44.3 8.9 %all_to_all.20.came = f32[32,2,128]{2,1,0:T(2,128)S(1)} all-to-all(f32[32,2,128]{2,1,0:T(2,128)S(1)} %get-tuple-element.54), channel_id=1, replica_groups=mesh['cam'=4,'clip'=8] {'cam','clip'}, dimensions={0} | all-to-all | bytes 65536 | tf_op jit(solution)/shard_map/row_total_1/all_to_all | solution.py:253
  53.2 0.2 row_total_1.1
  53.5 8.9 %all_to_all.21.came = f32[32,2,128]{2,1,0:T(2,128)S(1)} all-to-all(f32[32,2,128]{2,1,0:T(2,128)S(1)} %get-tuple-element.56), channel_id=1, replica_groups=mesh['cam'=4,'clip'=8] {'cam','clip'}, dimensions={0} | all-to-all | bytes 65536 | tf_op jit(solution)/shard_map/row_total_2/all_to_all | solution.py:253
  62.3 0.4 row_total_2.1
  62.8 0.1 collective-permute-start.3
  62.9 1.1 %collective-permute-done.3.got = f32[16,128]{1,0:T(8,128)S(1)} collective-permute-done((f32[16,128]{1,0:T(8,128)S(1)}, f32[16,128]{1,0:T(8,128)S(1)}, u32[]{:S(2)}, u32[]{:S(2)}) %collective-permute-start.3) | collective-permute-done | bytes 8224 | tf_op jit(solution)/shard_map/row_total_3/ppermute | solution.py:543
  64.0 0.7 row_total_3.1
  64.7 2.6 %all-to-all-start.3 = ((bf16[32,24,128]{2,1,0:T(8,128)(2,1)}), bf16[32,24,128]{2,1,0:T(8,128)(2,1)S(1)}, u32[]{:S(2)}, u32[]{:S(2)}) async-start(bf16[32,24,128]{2,1,0:T(8,128)(2,1)} %row_total_3.1), calls=%async_computation.3 | async-start | bytes 393216 | tf_op jit(solution)/shard_map/row_total_3/all_to_all | solution.py:253
  67.3 0.1 pad_add_fusion.pick
  67.4 0.9 %constant_dynamic-slice_fusion.wp = bf16[256,256]{1,0:T(8,128)(2,1)S(1)} fusion(bf16[1024,256]{1,0:T(8,128)(2,1)} %refs_3_.1, s32[]{:T(128)S(6)} %select_n.34), kind=kLoop, calls=%fused_computation.2 | loop fusion | bytes 262148 | tf_op jit(solution)/shard_map/outputs/dynamic_slice | solution.py:555
  68.3 7.5 %all-to-all-done.3 = bf16[32,24,128]{2,1,0:T(8,128)(2,1)S(1)} async-done(((bf16[32,24,128]{2,1,0:T(8,128)(2,1)}), bf16[32,24,128]{2,1,0:T(8,128)(2,1)S(1)}, u32[]{:S(2)}, u32[]{:S(2)}) %all-to-all-start.3) | async-done | bytes 196640 | tf_op jit(solution)/shard_map/row_total_3/all_to_all | solution.py:253
  75.8 0.0 copy-done.1
  75.8 2.6 %outputs.1 = (f32[16,2048]{1,0:T(8,128)}, f32[256,2048]{1,0:T(8,128)}, f32[128,256]{1,0:T(8,128)}, f32[128,256]{1,0:T(8,128)}) custom-call(s32[2]{0:T(128)S(1)} %pad_add_fusion.pick, bf16[2,2,8,24,128]{4,3,2,1,0:T(8,128)(2,1)S(1)} %bitcast.8, f32[16,256]{1,0:T(8,128)S(1)} %get-tuple-element.61.unit_ref, f32[16,128]{1,0:T(8,128)S(1)} %get-tuple-element.62.norm_ref, ...), custom_call_target="tpu_custom_call" | custom-call | flops 1 | bytes 1 | tf_op jit(solution)/shard_map/outputs/pallas_call | solution.py:30
Async XLA Ops:
  2.5 7.3 %collective-permute-start = (bf16[256,1024]{1,0:T(8,128)(2,1)S(1)}, bf16[256,1024]{1,0:T(8,128)(2,1)S(1)}, u32[]{:S(2)}, u32[]{:S(2)}) collective-permute-start(bf16[256,1024]{1,0:T(8,128)(2,1)S(1)} %get-tuple-element.36.refs_0_), channel_id=1, source_target_pairs={{0,8},{8,0},{16,24},{24,16},{1,9},{9,1},{17,25},{25,17},{2,10},{10... | collective-permute-start | bytes 1572872 | tf_op jit(solution)/shard_map/pooling/ppermute | solution.py:224
  3.0 15.1 %collective-permute-start.1 = (bf16[256,1024]{1,0:T(8,128)(2,1)S(1)}, bf16[256,1024]{1,0:T(8,128)(2,1)S(1)}, u32[]{:S(2)}, u32[]{:S(2)}) collective-permute-start(bf16[256,1024]{1,0:T(8,128)(2,1)S(1)} %get-tuple-element.43), channel_id=1, source_target_pairs={{0,16},{8,24},{16,0},{24,8},{1,17},{9,25},{17,1},{25,9},{2,18},{10... | collective-permute-start | bytes 1572872 | tf_op jit(solution)/shard_map/tokens_of_a_clip/ppermute | solution.py:216
  5.6 1.2 %copy-start = (bf16[256,2048]{1,0:T(8,128)(2,1)S(1)}, bf16[256,2048]{1,0:T(8,128)(2,1)}, u32[]{:S(2)}) copy-start(bf16[256,2048]{1,0:T(8,128)(2,1)} %proto.3) | copy-start | bytes 3145732
  18.1 1.9 %collective-permute-start.2 = (bf16[256,1024]{1,0:T(8,128)(2,1)S(1)}, bf16[256,1024]{1,0:T(8,128)(2,1)S(1)}, u32[]{:S(2)}, u32[]{:S(2)}) collective-permute-start(bf16[256,1024]{1,0:T(8,128)(2,1)S(1)} %collective-permute-done.1.refs_0_.refs_2_), channel_id=1, source_target_pairs={{0,8},{8,0},{16,24},{24,16},{1,9},{9,1},{17,25},{25,17},{2,10},{10... | collective-permute-start | bytes 1572872 | tf_op jit(solution)/shard_map/pooling/ppermute | solution.py:224
  30.4 13.3 %all-to-all-start = ((f32[32,2,128]{2,1,0:T(2,128)}), f32[32,2,128]{2,1,0:T(2,128)S(1)}, u32[]{:S(2)}, u32[]{:S(2)}) async-start(f32[32,2,128]{2,1,0:T(2,128)} %get-tuple-element.50), calls=%async_computation | async-start | bytes 65536 | tf_op jit(solution)/shard_map/logits/all_to_all | solution.py:253
  36.9 38.9 %copy-start.1 = (bf16[256,2048]{1,0:T(8,128)(2,1)S(1)}, bf16[256,2048]{1,0:T(8,128)(2,1)}, u32[]{:S(2)}) copy-start(bf16[256,2048]{1,0:T(8,128)(2,1)} %proto.3) | copy-start | bytes 3145732
  62.8 1.2 %collective-permute-start.3 = (f32[16,128]{1,0:T(8,128)S(1)}, f32[16,128]{1,0:T(8,128)S(1)}, u32[]{:S(2)}, u32[]{:S(2)}) collective-permute-start(f32[16,128]{1,0:T(8,128)S(1)} %get-tuple-element.59), channel_id=1, source_target_pairs={{0,8},{8,0},{16,24},{24,16},{1,9},{9,1},{17,25},{25,17},{2,10},{10... | collective-permute-start | bytes 24584 | tf_op jit(solution)/shard_map/row_total_3/ppermute | solution.py:543
  64.7 11.1 %all-to-all-start.3 = ((bf16[32,24,128]{2,1,0:T(8,128)(2,1)}), bf16[32,24,128]{2,1,0:T(8,128)(2,1)S(1)}, u32[]{:S(2)}, u32[]{:S(2)}) async-start(bf16[32,24,128]{2,1,0:T(8,128)(2,1)} %row_total_3.1), calls=%async_computation.3 | async-start | bytes 393216 | tf_op jit(solution)/shard_map/row_total_3/all_to_all | solution.py:253

commit v5 on v4

--- a/solution.py
+++ b/solution.py
@@ -13,14 +13,12 @@
 NORM_EPS = 1e-06
 LANES = 128
 DIGITS = 3
-CHUNKS = 1
 ALL = ("cam", "clip")
 F32 = jnp.float32
 BF16 = jnp.bfloat16
 TRANSPOSED = (((1,), (1,)), ((), ()))
 OUTER = (((0,), (0,)), ((), ()))
 WHOLE = pl.BlockSpec(memory_space=pltpu.VMEM)
-SCALARS = pl.BlockSpec(memory_space=pltpu.SMEM)
 
 
 def call(
@@ -69,36 +67,103 @@
     )
 
 
-def pool_kernel(parts, late, *refs):
-    early = [refs[3 * i : 3 * i + 3] for i in range(parts)]
-    refs = refs[3 * parts :]
-    x_refs, (wq, wk, wv, wp) = refs[:late], refs[late : late + 4]
-    weight_ref, pooled_ref, message, q_s, kt_s, v_s, w_s = refs[late + 4 :]
-    project_kernel(late, *x_refs, wq, wk, wv, q_s, kt_s, v_s)
-    pieces = early + [(q_s, kt_s, v_s)]
+def head_of(q, head, lane):
+    tile, at = divmod(head * HD, LANES)
+    here = slice(tile * LANES, (tile + 1) * LANES)
+    return jnp.where(lane // HD == at // HD, q[:, here], BF16(0)), here
+
+
+def scores(q_head, kt):
+    e = jnp.exp(jnp.dot(q_head, kt, preferred_element_type=F32))
+    return e, sum(e[:, i : i + LANES] for i in range(0, e.shape[1], LANES))
+
+
+def first_kernel(blocks, *refs):
+    ins, (q_ref, kt_ref, v_ref, exp_ref, sum_ref) = refs[: blocks + 3], refs[blocks + 3 :]
+    project_kernel(blocks, *ins, q_ref, kt_ref, v_ref)
+    rows, cols = q_ref.shape
+    lane = lax.broadcasted_iota(jnp.int32, (rows, LANES), 1)
+    sums = jnp.zeros((rows, LANES), F32)
+    for head in range(cols // HD):
+        q_head, here = head_of(q_ref, head, lane)
+        e, part = scores(q_head, kt_ref[here, :])
+        exp_ref[head * rows : (head + 1) * rows, :] = e.astype(BF16)
+        sums = jnp.where(lane == head, jnp.sum(part, axis=1, keepdims=True), sums)
+    sum_ref[...] = sums
+
+
+def first_blocks(blocks, weights):
+    d, cols = weights[0].shape
+    rows = sum(b.shape[0] for b in blocks)
+    heads = cols // HD
+    return call(
+        functools.partial(first_kernel, len(blocks)),
+        [
+            ((rows, cols), BF16),
+            ((cols, rows), BF16),
+            ((rows, cols), BF16),
+            ((heads * rows, rows), BF16),
+            ((rows, LANES), F32),
+        ],
+        [*blocks, *weights],
+        2 * rows * d * cols * 3,
+        mib=4 + 8 * rows * rows // 2**20,
+    )
+
+
+def pool_kernel(late, step, *refs):
+    q_e, kt_e, v_e, exp_e, sum_e, q_a, kt_a, v_a = refs[:8]
+    x_refs, (wq, wk, wv, wp) = refs[8 : 8 + late], refs[8 + late : 12 + late]
+    weight_ref, pooled_ref, message, q_s, kt_s, v_s, w_s, *buffers = refs[12 + late :]
+    here_already = q_a.shape[0]
+    q_s[:here_already], kt_s[:, :here_already], v_s[:here_already] = q_a[...], kt_a[...], v_a[...]
+    at = here_already
+    for x_ref in x_refs:
+        rows = slice(at, at + x_ref.shape[0])
+        at += x_ref.shape[0]
+        q_s[rows, :], kt_s[:, rows], v_s[rows, :] = project(x_ref[...], wq[...], wk[...], wv[...])
     heads, total = w_s.shape
     cols = heads * HD
-    lane = lax.broadcasted_iota(jnp.int32, (total, LANES), 1)
-
-    @pl.loop(0, cols // LANES)
-    def _(p):
-        here = pl.ds(pl.multiple_of(p * LANES, LANES), LANES)
-        q_pair = jnp.concatenate([q[:, here] for q, _, _ in pieces], axis=0)
-        k_pair = jnp.concatenate([kt[here, :] for _, kt, _ in pieces], axis=1)
-        for e in range(LANES // HD):
-            q_head = jnp.where(lane // HD == e, q_pair, BF16(0))
-            a = jnp.exp(jnp.dot(q_head, k_pair, preferred_element_type=F32))
-            a = a * (1.0 / jnp.sum(a, axis=1, keepdims=True))
-            w = jnp.sum(a, axis=0, keepdims=True) * (1.0 / total)
-            w_s[pl.ds(p * (LANES // HD) + e, 1), :] = w
+    first, fresh = q_e.shape[0], q_s.shape[0]
+    lane_e = lax.broadcasted_iota(jnp.int32, (first, LANES), 1)
+    lane_s = lax.broadcasted_iota(jnp.int32, (fresh, LANES), 1)
+
+    inverse = None
+    for head in range(heads + 1):
+        new, old = buffers[2 * (head % 2) :][:2], buffers[2 * ((head + 1) % 2) :][:2]
+        if head < heads:
+            queries_e, here = head_of(q_e, head, lane_e)
+            queries_s, _ = head_of(q_s, head, lane_s)
+            total_e = jnp.zeros((first, LANES), F32)
+            total_s = jnp.zeros((fresh, LANES), F32)
+        for at in range(0, total, step):
+            keys = slice(at, at + step)
+            at_s = slice(at - first, at - first + step)
+            if head < heads:
+                kt = kt_e[here, keys] if at < first else kt_s[here, at_s]
+                new[0][:, keys], part = scores(queries_s, kt)
+                total_s = total_s + part
+                if at >= first:
+                    new[1][:, at_s], part = scores(queries_e, kt)
+                    total_e = total_e + part
+            if head > 0:
+                if at < first:
+                    a = exp_e[(head - 1) * first : head * first, keys].astype(F32)
+                else:
+                    a = old[1][:, at_s]
+                a = [a * inverse[1], old[0][:, keys] * inverse[0]]
+                if first == fresh:
+                    a = [a[0] + a[1]]
+                w = sum(jnp.sum(part, axis=0, keepdims=True) for part in a)
+                w_s[head - 1 : head, keys] = w * (1.0 / total)
+        if head < heads:
+            total_e = jnp.sum(total_e, axis=1, keepdims=True) + sum_e[:, head : head + 1]
+            inverse = 1.0 / jnp.sum(total_s, axis=1, keepdims=True), 1.0 / total_e
 
     weights = w_s[...].astype(BF16)
     weight_ref[...] = weights
-    out, at = jnp.zeros((heads, cols), F32), 0
-    for _, _, v in pieces:
-        rows = slice(at, at + v.shape[0])
-        at += v.shape[0]
-        out = out + jnp.dot(weights[:, rows], v[...], preferred_element_type=F32)
+    out = jnp.dot(weights[:, :first], v_e[...], preferred_element_type=F32)
+    out = out + jnp.dot(weights[:, first:], v_s[...], preferred_element_type=F32)
     row_head = lax.broadcasted_iota(jnp.int32, out.shape, 0)
     col_head = lax.broadcasted_iota(jnp.int32, out.shape, 1) // HD
     pooled = jnp.sum(jnp.where(row_head == col_head, out, 0.0), axis=0, keepdims=True)
@@ -112,17 +177,18 @@
         message[i] = embed
 
 
-def pool(parts, late, weights, wp, devices):
+def pool(early, ready, late, weights, wp, devices):
     d, cols = weights[0].shape
     heads = cols // HD
-    fresh = sum(b.shape[0] for b in late)
-    total = fresh + sum(q.shape[0] for q, _, _ in parts)
+    first = early[0].shape[0]
+    fresh = ready[0].shape[0] + sum(b.shape[0] for b in late)
+    total = first + fresh
     bottleneck = wp.shape[1]
-    ins = [a for part in parts for a in part] + [*late, *weights, wp]
+    pair = [pltpu.VMEM((fresh, total), F32), pltpu.VMEM((first, fresh), F32)]
     return call(
-        functools.partial(pool_kernel, len(parts), len(late)),
+        functools.partial(pool_kernel, len(late), min(first, fresh, 256)),
         [((heads, total), BF16), ((1, cols), F32), ((devices, bottleneck // LANES, LANES), F32)],
-        ins,
+        [*early, *ready, *late, *weights, wp],
         2 * fresh * d * cols * 3 + 2 * total * total * cols * 4,
         heads * total * total,
         scratch=[
@@ -130,8 +196,10 @@
             pltpu.VMEM((cols, fresh), BF16),
             pltpu.VMEM((fresh, cols), BF16),
             pltpu.VMEM((heads, total), F32),
+            *pair,
+            *pair,
         ],
-        mib=4 + 4 * total * total * 5 // 2**20,
+        mib=12 + 12 * fresh * (total + first) // 2**20,
     )
 
 
@@ -168,26 +236,26 @@
 FAR = pl.BlockSpec(memory_space=pltpu.HBM)
 
 
-def slice_kernel(plan, at, *refs):
+def slice_kernel(plan, *refs):
     ins = 1 + max(which for which, _ in plan)
     outs, sems = refs[ins:-1], refs[-1]
     copies = []
     for i, (which, where) in enumerate(plan):
-        source = refs[which].at[where(at)]
+        source = refs[which].at[where()]
         copies.append(pltpu.make_async_copy(source, outs[i], sems.at[i]))
         copies[-1].start()
     for copy in copies:
         copy.wait()
 
 
-def slices(at, arrays, plan, shapes):
+def slices(arrays, plan, shapes):
     return call(
         functools.partial(slice_kernel, plan),
         [(shape, BF16) for shape in shapes],
-        [at, *(pltpu.with_memory_space_constraint(a, pltpu.HBM) for a in arrays)],
+        [pltpu.with_memory_space_constraint(a, pltpu.HBM) for a in arrays],
         0,
         scratch=[pltpu.SemaphoreType.DMA((len(plan),))],
-        in_specs=[SCALARS] + [FAR] * len(arrays),
+        in_specs=[FAR] * len(arrays),
     )
 
 
@@ -195,25 +263,20 @@
     return lax.optimization_barrier((x, others))[0]
 
 
-def token_piece(s, c, size):
-    return lambda at: (at[s], pl.ds(c * size, size), slice(None))
-
-
-def from_other_groups(tokens, groups, n_cam):
+def token_block(s, clips, ranks):
+    return 0, lambda: ((lax.axis_index("cam") // ranks + s) % clips, slice(None), slice(None))
+
+
+def from_other_groups(tokens, n_cam):
     clips, tok, d = tokens.shape
     ranks = n_cam // clips
-    size = tok // CHUNKS
-    pieces = [(s, c) for c in range(CHUNKS) for s in range(1, clips)]
-    *sent, mine = slices(
-        groups,
-        [tokens],
-        [(0, token_piece(s, c, size)) for s, c in pieces] + [(0, token_piece(0, 0, tok))],
-        [(size, d)] * len(pieces) + [(tok, d)],
-    )
-    held = [[] for _ in range(CHUNKS)]
-    for (s, c), block in zip(pieces, sent):
+    mine, *sent = slices(
+        [tokens], [token_block(s, clips, ranks) for s in range(clips)], [(tok, d)] * clips
+    )
+    held = []
+    for s, block in enumerate(sent, 1):
         perm = [(i, ((i // ranks + s) % clips) * ranks + i % ranks) for i in range(n_cam)]
-        held[c].append((s * ranks, lax.ppermute(block, "cam", perm)))
+        held.append((s * ranks, lax.ppermute(block, "cam", perm)))
     return mine, held
 
 
@@ -303,7 +366,7 @@
 
 
 def third_kernel(
-    parity, came, assign_ref, proto, assign_out, keep_ref, send_ref, digits_ref, grad_ref
+    came, assign_ref, proto, assign_out, keep_ref, send_ref, digits_ref, grad_ref
 ):
     batch = assign_ref.shape[0]
     halves = proto.shape[0] // LANES
@@ -315,7 +378,7 @@
         assign.astype(BF16), proto[...], TRANSPOSED, preferred_element_type=F32
     )
     half = part.shape[1] // 2
-    odd = parity[0] == 1
+    odd = lax.axis_index("cam") % 2 == 1
     low, high = part[:, :half], part[:, half:]
     keep_ref[...] = jnp.where(odd, high, low)
     send_ref[...] = jnp.where(odd, low, high)
@@ -341,7 +404,6 @@
     protos,
     n_cam,
     block,
-    pick,
     came,
     unit_ref,
     norm_ref,
@@ -365,6 +427,7 @@
     clips, ranks, n_clip = came.shape[:3]
     batch, columns = exp_ref.shape
     share = grad_proj.shape[0]
+    cols = clips * wp.shape[0]
     copies = []
 
     def send(source, target):
@@ -387,8 +450,8 @@
         grad_logits = (exp_ref[:, here] * by_prob - assign).astype(BF16)
         for g in range(clips):
             for p in range(n_clip):
-                at, to = g * n_clip + p, p * clips + g
-                codes[to : to + 1, here] = assign[at : at + 1]
+                row, to = g * n_clip + p, p * clips + g
+                codes[to : to + 1, here] = assign[row : row + 1]
         grad = lax.dot_general(unit_b, grad_logits, OUTER, preferred_element_type=F32)
         inverse = scale[:, here]
         unit_proto = proto[:, here].astype(F32) * inverse
@@ -404,12 +467,12 @@
     ) / norm_ref[:, :1]
     grad_embed = grad_embed.astype(BF16)
 
-    def rows(rank, at):
-        picked = [came[g, rank].astype(F32)[:, at, :] for g in range(clips)]
+    def rows(rank, row):
+        picked = [came[g, rank].astype(F32)[:, row, :] for g in range(clips)]
         return jnp.concatenate(picked, axis=0)[:, :share].astype(BF16)
 
     grad_proj[...] = lax.dot_general(
-        rows(pick[0], batch + DIGITS), grad_embed, OUTER, preferred_element_type=F32
+        rows(lax.axis_index("clip") * share // cols, batch + DIGITS), grad_embed, OUTER, preferred_element_type=F32
     )
     send(grad_proj, grad_proj_out)
     grad_pooled = lax.dot_general(
@@ -418,7 +481,7 @@
     col_head = lax.broadcasted_iota(jnp.int32, grad_value.shape, 1) // HD
     value = jnp.zeros(grad_value.shape, F32)
     for head in range(grad_value.shape[1] // HD):
-        mixed = rows(pick[1], batch + DIGITS + 1 + head)
+        mixed = rows(lax.axis_index("cam") // clips, batch + DIGITS + 1 + head)
         out = lax.dot_general(mixed, grad_pooled, OUTER, preferred_element_type=F32)
         value = jnp.where(col_head == head, out, value)
     grad_value[...] = value
@@ -439,14 +502,11 @@
     share = d // n_clip
     bottleneck, columns = prototypes.shape
     protos = columns * devices
-    cam, clip = lax.axis_index("cam"), lax.axis_index("clip")
-    rank = cam % ranks
+    width = heads_here * HD
 
     with jax.named_scope("tokens_of_a_clip"):
         tokens = tokens.reshape(clips, tok, d)
-        groups = [(cam // ranks + s) % clips for s in range(clips)]
-        groups = jnp.stack(groups + [rank * cols]).astype(jnp.int32)
-        mine, held = from_other_groups(tokens, groups, n_cam)
+        mine, held = from_other_groups(tokens, n_cam)
 
     with jax.named_scope("prototypes"):
         scale, proto_b = call(
@@ -458,29 +518,30 @@
         )
 
     with jax.named_scope("pooling"):
-        def columns_of(at):
-            return slice(None), pl.ds(pl.multiple_of(at[clips], cols), cols)
-
-        def rows_of(at):
-            return pl.ds(pl.multiple_of(at[clips], cols), cols), slice(None)
-
-        *weights, wp = slices(
-            groups,
+        def columns_of():
+            start = lax.axis_index("cam") % ranks * cols
+            return slice(None), pl.ds(pl.multiple_of(start, cols), cols)
+
+        def rows_of():
+            start = lax.axis_index("cam") % ranks * cols
+            return pl.ds(pl.multiple_of(start, cols), cols), slice(None)
+
+        def heads_of():
+            start = lax.axis_index("cam") * width
+            return pl.ds(pl.multiple_of(start, width), width), slice(None)
+
+        *weights, wp, proj_rows = slices(
             [w_query, w_key, w_value, w_proj],
-            [(i, columns_of) for i in range(3)] + [(3, rows_of)],
-            [(d, cols)] * 3 + [(cols, bottleneck)],
-        )
-        stages, parts = [relay([(0, mine)], n_cam, ranks)], []
-        parts.append(project_blocks([b for _, b in stages[0]], weights))
-        for blocks in held:
-            blocks = [(camera, after(b, proto_b, *parts)) for camera, b in blocks]
-            stages.append(relay(blocks, n_cam, ranks))
-            if blocks is not held[-1] and len(stages) <= CHUNKS:
-                parts.append(project_blocks([b for _, b in stages[-1]], weights))
-        own = len(held[-1])
-        parts.append(project_blocks([b for _, b in stages[-1][:own]], weights))
-        late = [b for _, b in stages[-1][own:]]
-        key_weights, pooled, message = pool(parts, late, weights, wp, devices)
+            [(i, columns_of) for i in range(3)] + [(3, rows_of), (3, heads_of)],
+            [(d, cols)] * 3 + [(cols, bottleneck), (width, bottleneck)],
+        )
+        stages = [relay([(0, mine)], n_cam, ranks)]
+        early = first_blocks([b for _, b in stages[0]], weights)
+        held = [(camera, after(b, proto_b, *early)) for camera, b in held]
+        stages.append(relay(held, n_cam, ranks))
+        ready = project_blocks([b for _, b in held], weights)
+        late = [b for _, b in stages[1][len(held) :]]
+        key_weights, pooled, message = pool(early, ready, late, weights, wp, devices)
 
     with jax.named_scope("mixtures"):
         cameras, blocks, at = {}, [], 0
@@ -524,7 +585,6 @@
 
     with jax.named_scope("row_total_2"):
         came = exchange(message)
-        parity = (cam % 2).reshape(1)
         assign, keep, send, digits, prob_grad = call(
             third_kernel,
             [
@@ -534,9 +594,8 @@
                 (side.shape[1:], F32),
                 ((batch, bottleneck), F32),
             ],
-            [parity, came, assign, proto_b],
+            [came, assign, proto_b],
             2 * batch * bottleneck * columns,
-            in_specs=[SCALARS] + [WHOLE] * 3,
         )
 
     with jax.named_scope("row_total_3"):
@@ -547,15 +606,11 @@
             [keep, got, digits, side],
             devices * batch * LANES,
         )
-        came = exchange(message)
+        came = exchange(after(message, proj_rows))
 
     with jax.named_scope("outputs"):
-        width = heads_here * HD
-        pick = jnp.stack([clip * share // cols, cam // clips])
-        proj_rows = lax.dynamic_slice_in_dim(w_proj, cam * width, width, 0)
         block = min(columns, 512)
         ins = [
-            pick,
             came.reshape((clips, ranks, n_clip) + came.shape[1:]),
             unit,
             norm,
@@ -580,7 +635,6 @@
             2 * batch * bottleneck * columns,
             scratch=[pltpu.VMEM(*o) for o in outs]
             + [pltpu.SemaphoreType.DMA((columns // block + 3,))],
-            in_specs=[SCALARS] + [WHOLE] * (len(ins) - 1),
             out_specs=[FAR] * len(outs),
             mib=8,
         )

time: 78.7 us -> 75.2 us (0.956)
  blocking collectives: 17.8 us -> 28 us
  waiting for transfers between devices: 22.8 us -> 14.4 us
  starting transfers between devices: 11.9 us -> 9.33 us
  Pallas kernels: 22.8 us -> 21 us
  local copies, waits for them, and re-layouts: 2.15 us -> 1.24 us
    all_to_all x2 -> x3, blocking collectives: 17.8 us -> 28 us  [exchange(): return lax.all_to_all(message, ALL, split_axis=0, concat_axis=0, tiled=True)]
    all_to_all x2 -> x1, waiting for transfers between devices: 14.3 us -> 6.78 us  [exchange(): return lax.all_to_all(message, ALL, split_axis=0, concat_axis=0, tiled=True)]
    all_to_all x2 -> x1, starting transfers between devices: 8.68 us -> 6.12 us  [exchange(): return lax.all_to_all(message, ALL, split_axis=0, concat_axis=0, tiled=True)]
    pallas_call x12, Pallas kernels: 22.8 us -> 21 us  [call(): pl.pallas_call(kernel, out_shape=tuple((jax.ShapeDtypeStruct(*o) for o in...]
    dynamic_slice x1 -> x0, local copies, waits for them, and re-layouts: 0.91 us -> none  [local(): proj_rows = lax.dynamic_slice_in_dim(w_proj, cam * width, width, 0)]
    ppermute x1, waiting for transfers between devices: 6.51 us -> 5.67 us  [from_other_groups(): held.append((s * ranks, lax.ppermute(block, 'cam', perm)))]
  transfers between devices with their start and end apart: 6 -> 5, of which waited for: 5 -> 4; matrix products, arithmetic and copies ran while one was open for 1% -> 0% of each run, Pallas kernels for 8% -> 9%
where the time goes in v5:
time: 75.2 us; the launch traced here: 74.9 us
  blocking collectives  28 us (37%)
  Pallas kernels  21 us (28%)
  waiting for transfers between devices  14.4 us (19%)
  starting transfers between devices  9.33 us (12%)
  local copies, waits for them, and re-layouts  1.24 us (2%)
  between operations  0.88 us (1%)
    all_to_all x3, blocking collectives, exchange(): return lax.all_to_all(message, ALL, split_axis=0, concat_axis=0, tiled=True)  28 us
    pallas_call x12, Pallas kernels, call(): pl.pallas_call(kernel, out_shape=tuple((jax.ShapeDtypeStruct(*o) for o in...  21 us
    all_to_all x1, waiting for transfers between devices, exchange(): return lax.all_to_all(message, ALL, split_axis=0, concat_axis=0, tiled=True)  6.78 us
    all_to_all x1, starting transfers between devices, exchange(): return lax.all_to_all(message, ALL, split_axis=0, concat_axis=0, tiled=True)  6.12 us
    ppermute x1, waiting for transfers between devices, from_other_groups(): held.append((s * ranks, lax.ppermute(block, 'cam', perm)))  5.67 us
    ppermute x1, starting transfers between devices, from_other_groups(): held.append((s * ranks, lax.ppermute(block, 'cam', perm)))  2.56 us
  transfers between devices with their start and end apart: 5, of which 4 were waited for; matrix products, arithmetic and copies ran while one was open for 0% of the time, Pallas kernels for 9%

profile of v5, /device:TPU:0, one launch (start us, length us, event | category | flops | bytes accessed | tf_op | source)
XLA Modules:
  0.0 74.9 jit_solution(10546735632358395818)
XLA Ops:
  0.6 1.2 %tokens_of_a_clip.1 = (bf16[256,1024]{1,0:T(8,128)(2,1)S(1)}, bf16[256,1024]{1,0:T(8,128)(2,1)S(1)}) custom-call(bf16[2,256,1024]{2,1,0:T(8,128)(2,1)} %bitcast.3), custom_call_target="tpu_custom_call" | custom-call | flops 1 | bytes 1 | tf_op jit(solution)/shard_map/tokens_of_a_clip/pallas_call | solution.py:28
  1.9 0.5 collective-permute-start
  2.4 2.6 %collective-permute-start.1 = (bf16[256,1024]{1,0:T(8,128)(2,1)S(1)}, bf16[256,1024]{1,0:T(8,128)(2,1)S(1)}, u32[]{:S(2)}, u32[]{:S(2)}) collective-permute-start(bf16[256,1024]{1,0:T(8,128)(2,1)S(1)} %get-tuple-element.49), channel_id=1, source_target_pairs={{0,16},{8,24},{16,0},{24,8},{1,17},{9,25},{17,1},{25,9},{2,18},{10... | collective-permute-start | bytes 1572872 | tf_op jit(solution)/shard_map/tokens_of_a_clip/ppermute | solution.py:279
  5.0 0.0 copy-start
  5.0 1.2 %copy-done = bf16[256,2048]{1,0:T(8,128)(2,1)S(1)} copy-done((bf16[256,2048]{1,0:T(8,128)(2,1)S(1)}, bf16[256,2048]{1,0:T(8,128)(2,1)}, u32[]{:S(2)}) %copy-start) | copy-done | bytes 1048600
  6.2 0.4 prototypes.1
  6.6 2.1 %pooling.4 = (bf16[1024,512]{1,0:T(8,128)(2,1)S(1)}, bf16[1024,512]{1,0:T(8,128)(2,1)S(1)}, bf16[1024,512]{1,0:T(8,128)(2,1)S(1)}, bf16[512,256]{1,0:T(8,128)(2,1)S(1)}, bf16[256,256]{1,0:T(8,128)(2,1)S(1)}) custom-call(bf16[1024,1024]{1,0:T(8,128)(2,1)} %refs_0_.1, bf16[1024,1024]{1,0:T(8,128)(2,1)} %refs_1_.1, bf16[1024,1024]{1,0:T(8,128)(2,1)} %refs_2_.1, ...), custom_call_target="tpu_custom_call" | custom-call | flops 1 | bytes 1 | tf_op jit(solution)/shard_map/pooling/pallas_call | solution.py:28
  8.7 0.0 collective-permute-done.refs_1_
  8.7 3.1 %pooling.5 = (bf16[512,512]{1,0:T(8,128)(2,1)S(1)}, bf16[512,512]{1,0:T(8,128)(2,1)S(1)}, bf16[512,512]{1,0:T(8,128)(2,1)S(1)}, bf16[4096,512]{1,0:T(8,128)(2,1)S(1)}, f32[512,128]{1,0:T(8,128)S(1)}) custom-call(bf16[256,1024]{1,0:T(8,128)(2,1)S(1)} %get-tuple-element.40.refs_0_, bf16[256,1024]{1,0:T(8,128)(2,1)S(1)} %collective-permute-done.refs_1_, ...), custom_call_target="tpu_custom_call" | custom-call | flops 1 | bytes 1 | tf_op jit(solution)/shard_map/pooling/pallas_call | solution.py:28
  11.8 5.7 %collective-permute-done.1.refs_0_.refs_2_ = bf16[256,1024]{1,0:T(8,128)(2,1)S(1)} collective-permute-done((bf16[256,1024]{1,0:T(8,128)(2,1)S(1)}, bf16[256,1024]{1,0:T(8,128)(2,1)S(1)}, u32[]{:S(2)}, u32[]{:S(2)}) %collective-permute-start.1) | collective-permute-done | bytes 524320 | tf_op jit(solution)/shard_map/tokens_of_a_clip/ppermute | solution.py:279
  17.5 0.0 collective-permute-start.2
  17.5 1.0 %pooling.6 = (bf16[256,512]{1,0:T(8,128)(2,1)S(1)}, bf16[512,256]{1,0:T(8,128)(2,1)S(1)}, bf16[256,512]{1,0:T(8,128)(2,1)S(1)}) custom-call(bf16[256,1024]{1,0:T(8,128)(2,1)S(1)} %collective-permute-done.1.refs_0_.refs_2_, bf16[1024,512]{1,0:T(8,128)(2,1)S(1)} %get-tuple-element.41.refs_2_.refs_1_.refs_9_, ...), custom_call_target="tpu_custom_call" | custom-call | flops 1 | bytes 1 | tf_op jit(solution)/shard_map/pooling/pallas_call | solution.py:28
  18.5 0.9 %collective-permute-done.2.refs_8_.refs_3_ = bf16[256,1024]{1,0:T(8,128)(2,1)S(1)} collective-permute-done((bf16[256,1024]{1,0:T(8,128)(2,1)S(1)}, bf16[256,1024]{1,0:T(8,128)(2,1)S(1)}, u32[]{:S(2)}, u32[]{:S(2)}) %collective-permute-start.2) | collective-permute-done | bytes 524320 | tf_op jit(solution)/shard_map/pooling/ppermute | solution.py:287
  19.4 9.5 %pooling.7 = (bf16[8,1024]{1,0:T(8,128)(2,1)S(1)}, f32[1,512]{1,0:T(1,128)S(1)}, f32[32,2,128]{2,1,0:T(2,128)}) custom-call(bf16[512,512]{1,0:T(8,128)(2,1)S(1)} %get-tuple-element.44.refs_0_, bf16[512,512]{1,0:T(8,128)(2,1)S(1)} %get-tuple-element.45.refs_1_, bf16[512,512]{1,0:T(8,128)(2,1)S(1)} %get-tuple-element.46.refs_2_, ...), custom_call_target="tpu_custom_call" | custom-call | flops 1 | bytes 1 | tf_op jit(solution)/shard_map/pooling/pallas_call | solution.py:28
  28.9 6.1 %all-to-all-start = ((f32[32,2,128]{2,1,0:T(2,128)}), f32[32,2,128]{2,1,0:T(2,128)S(1)}, u32[]{:S(2)}, u32[]{:S(2)}) async-start(f32[32,2,128]{2,1,0:T(2,128)} %get-tuple-element.56), calls=%async_computation | async-start | bytes 65536 | tf_op jit(solution)/shard_map/logits/all_to_all | solution.py:316
  35.0 0.4 mixtures.1.side
  35.4 0.0 copy-start.1
  35.4 6.8 %all-to-all-done.came = f32[32,2,128]{2,1,0:T(2,128)S(1)} async-done(((f32[32,2,128]{2,1,0:T(2,128)}), f32[32,2,128]{2,1,0:T(2,128)S(1)}, u32[]{:S(2)}, u32[]{:S(2)}) %all-to-all-start) | async-done | bytes 32800 | tf_op jit(solution)/shard_map/logits/all_to_all | solution.py:316
  42.2 0.6 logits.1
  42.8 8.9 %all_to_all.20.came = f32[32,2,128]{2,1,0:T(2,128)S(1)} all-to-all(f32[32,2,128]{2,1,0:T(2,128)S(1)} %get-tuple-element.60), channel_id=1, replica_groups=mesh['cam'=4,'clip'=8] {'cam','clip'}, dimensions={0} | all-to-all | bytes 65536 | tf_op jit(solution)/shard_map/row_total_1/all_to_all | solution.py:316
  51.7 0.2 row_total_1.1
  51.9 8.9 %all_to_all.21.came = f32[32,2,128]{2,1,0:T(2,128)S(1)} all-to-all(f32[32,2,128]{2,1,0:T(2,128)S(1)} %get-tuple-element.62), channel_id=1, replica_groups=mesh['cam'=4,'clip'=8] {'cam','clip'}, dimensions={0} | all-to-all | bytes 65536 | tf_op jit(solution)/shard_map/row_total_2/all_to_all | solution.py:316
  60.8 0.4 row_total_2.1
  61.3 0.1 collective-permute-start.3
  61.4 1.1 %collective-permute-done.3.got = f32[16,128]{1,0:T(8,128)S(1)} collective-permute-done((f32[16,128]{1,0:T(8,128)S(1)}, f32[16,128]{1,0:T(8,128)S(1)}, u32[]{:S(2)}, u32[]{:S(2)}) %collective-permute-start.3) | collective-permute-done | bytes 8224 | tf_op jit(solution)/shard_map/row_total_3/ppermute | solution.py:602
  62.5 10.2 %all_to_all.22 = bf16[32,24,128]{2,1,0:T(8,128)(2,1)S(1)} all-to-all(bf16[32,24,128]{2,1,0:T(8,128)(2,1)S(1)} %row_total_3.1), channel_id=1, replica_groups=mesh['cam'=4,'clip'=8] {'cam','clip'}, dimensions={0} | all-to-all | bytes 393216 | tf_op jit(solution)/shard_map/row_total_3/all_to_all | solution.py:316
  72.7 0.0 copy-done.1
  72.7 2.0 %outputs.1 = (f32[16,2048]{1,0:T(8,128)}, f32[256,2048]{1,0:T(8,128)}, f32[128,256]{1,0:T(8,128)}, f32[128,256]{1,0:T(8,128)}) custom-call(bf16[2,2,8,24,128]{4,3,2,1,0:T(8,128)(2,1)S(1)} %bitcast.2, f32[16,256]{1,0:T(8,128)S(1)} %get-tuple-element.69.unit_ref, f32[16,128]{1,0:T(8,128)S(1)} %get-tuple-element.70.norm_ref, ...), custom_call_target="tpu_custom_call" | custom-call | flops 1 | bytes 1 | tf_op jit(solution)/shard_map/outputs/pallas_call | solution.py:28
  (1 shorter events, 0.0 us)
Async XLA Ops:
  1.9 6.8 %collective-permute-start = (bf16[256,1024]{1,0:T(8,128)(2,1)S(1)}, bf16[256,1024]{1,0:T(8,128)(2,1)S(1)}, u32[]{:S(2)}, u32[]{:S(2)}) collective-permute-start(bf16[256,1024]{1,0:T(8,128)(2,1)S(1)} %get-tuple-element.40.refs_0_), channel_id=1, source_target_pairs={{0,8},{8,0},{16,24},{24,16},{1,9},{9,1},{17,25},{25,17},{2,10},{10... | collective-permute-start | bytes 1572872 | tf_op jit(solution)/shard_map/pooling/ppermute | solution.py:287
  2.4 15.1 %collective-permute-start.1 = (bf16[256,1024]{1,0:T(8,128)(2,1)S(1)}, bf16[256,1024]{1,0:T(8,128)(2,1)S(1)}, u32[]{:S(2)}, u32[]{:S(2)}) collective-permute-start(bf16[256,1024]{1,0:T(8,128)(2,1)S(1)} %get-tuple-element.49), channel_id=1, source_target_pairs={{0,16},{8,24},{16,0},{24,8},{1,17},{9,25},{17,1},{25,9},{2,18},{10... | collective-permute-start | bytes 1572872 | tf_op jit(solution)/shard_map/tokens_of_a_clip/ppermute | solution.py:279
  5.0 1.2 %copy-start = (bf16[256,2048]{1,0:T(8,128)(2,1)S(1)}, bf16[256,2048]{1,0:T(8,128)(2,1)}, u32[]{:S(2)}) copy-start(bf16[256,2048]{1,0:T(8,128)(2,1)} %proto.3) | copy-start | bytes 3145732
  17.5 1.9 %collective-permute-start.2 = (bf16[256,1024]{1,0:T(8,128)(2,1)S(1)}, bf16[256,1024]{1,0:T(8,128)(2,1)S(1)}, u32[]{:S(2)}, u32[]{:S(2)}) collective-permute-start(bf16[256,1024]{1,0:T(8,128)(2,1)S(1)} %collective-permute-done.1.refs_0_.refs_2_), channel_id=1, source_target_pairs={{0,8},{8,0},{16,24},{24,16},{1,9},{9,1},{17,25},{25,17},{2,10},{10... | collective-permute-start | bytes 1572872 | tf_op jit(solution)/shard_map/pooling/ppermute | solution.py:287
  28.9 13.3 %all-to-all-start = ((f32[32,2,128]{2,1,0:T(2,128)}), f32[32,2,128]{2,1,0:T(2,128)S(1)}, u32[]{:S(2)}, u32[]{:S(2)}) async-start(f32[32,2,128]{2,1,0:T(2,128)} %get-tuple-element.56), calls=%async_computation | async-start | bytes 65536 | tf_op jit(solution)/shard_map/logits/all_to_all | solution.py:316
  35.4 37.4 %copy-start.1 = (bf16[256,2048]{1,0:T(8,128)(2,1)S(1)}, bf16[256,2048]{1,0:T(8,128)(2,1)}, u32[]{:S(2)}) copy-start(bf16[256,2048]{1,0:T(8,128)(2,1)} %proto.3) | copy-start | bytes 3145732
  61.3 1.2 %collective-permute-start.3 = (f32[16,128]{1,0:T(8,128)S(1)}, f32[16,128]{1,0:T(8,128)S(1)}, u32[]{:S(2)}, u32[]{:S(2)}) collective-permute-start(f32[16,128]{1,0:T(8,128)S(1)} %get-tuple-element.65), channel_id=1, source_target_pairs={{0,8},{8,0},{16,24},{24,16},{1,9},{9,1},{17,25},{25,17},{2,10},{10... | collective-permute-start | bytes 24584 | tf_op jit(solution)/shard_map/row_total_3/ppermute | solution.py:602

commit v6 on v5

--- a/solution.py
+++ b/solution.py
@@ -47,13 +47,8 @@
 def project_kernel(blocks, *refs):
     wq, wk, wv = refs[blocks : blocks + 3]
     q_ref, kt_ref, v_ref = refs[blocks + 3 :]
-    at = 0
-    for x_ref in refs[:blocks]:
-        rows = slice(at, at + x_ref.shape[0])
-        at += x_ref.shape[0]
-        q_ref[rows, :], kt_ref[:, rows], v_ref[rows, :] = project(
-            x_ref[...], wq[...], wk[...], wv[...]
-        )
+    x = jnp.concatenate([x_ref[...] for x_ref in refs[:blocks]], axis=0)
+    q_ref[...], kt_ref[...], v_ref[...] = project(x, wq[...], wk[...], wv[...])
 
 
 def project_blocks(blocks, weights):
@@ -111,59 +106,117 @@
     )
 
 
-def pool_kernel(late, step, *refs):
-    q_e, kt_e, v_e, exp_e, sum_e, q_a, kt_a, v_a = refs[:8]
-    x_refs, (wq, wk, wv, wp) = refs[8 : 8 + late], refs[8 + late : 12 + late]
-    weight_ref, pooled_ref, message, q_s, kt_s, v_s, w_s, *buffers = refs[12 + late :]
-    here_already = q_a.shape[0]
-    q_s[:here_already], kt_s[:, :here_already], v_s[:here_already] = q_a[...], kt_a[...], v_a[...]
-    at = here_already
+def next_kernel(blocks, q_e, kt_e, sum_e, *refs):
+    ins, outs = refs[: blocks + 3], refs[blocks + 3 :]
+    q_n, kt_n, v_n, exp_n, exp_x, sum_n, sum_ref = outs
+    project_kernel(blocks, *ins, q_n, kt_n, v_n)
+    rows, cols = q_n.shape
+    first = q_e.shape[0]
+    lane_n = lax.broadcasted_iota(jnp.int32, (rows, LANES), 1)
+    lane_e = lax.broadcasted_iota(jnp.int32, (first, LANES), 1)
+    sums_n, sums_e = jnp.zeros((rows, LANES), F32), sum_e[...]
+    for head in range(cols // HD):
+        queries_n, here = head_of(q_n, head, lane_n)
+        queries_e, _ = head_of(q_e, head, lane_e)
+        a, part_a = scores(queries_n, kt_e[here, :])
+        b, part_b = scores(queries_n, kt_n[here, :])
+        x, part_x = scores(queries_e, kt_n[here, :])
+        exp_n[head * rows : (head + 1) * rows, :first] = a.astype(BF16)
+        exp_n[head * rows : (head + 1) * rows, first:] = b.astype(BF16)
+        exp_x[head * first : (head + 1) * first, :] = x.astype(BF16)
+        part = jnp.sum(part_a + part_b, axis=1, keepdims=True)
+        sums_n = jnp.where(lane_n == head, part, sums_n)
+        part = jnp.sum(part_x, axis=1, keepdims=True)
+        sums_e = sums_e + jnp.where(lane_e == head, part, 0.0)
+    sum_n[...] = sums_n
+    sum_ref[...] = sums_e
+
+
+def next_blocks(blocks, early, weights):
+    q_e, kt_e, _, _, sum_e = early
+    d, cols = weights[0].shape
+    first = q_e.shape[0]
+    rows = sum(b.shape[0] for b in blocks)
+    heads = cols // HD
+    return call(
+        functools.partial(next_kernel, len(blocks)),
+        [
+            ((rows, cols), BF16),
+            ((cols, rows), BF16),
+            ((rows, cols), BF16),
+            ((heads * rows, first + rows), BF16),
+            ((heads * first, rows), BF16),
+            ((rows, LANES), F32),
+            ((first, LANES), F32),
+        ],
+        [q_e, kt_e, sum_e, *blocks, *weights],
+        2 * rows * d * cols * 3,
+        mib=4 + 24 * first * rows // 2**20,
+    )
+
+
+def pool_kernel(late, *refs):
+    (q_e, kt_e, v_e, exp_e), refs = refs[:4], refs[4:]
+    (q_n, kt_n, v_n, exp_n, exp_x, sum_n, sum_e), refs = refs[:7], refs[7:]
+    (q_a, kt_a, v_a), refs = refs[:3], refs[3:]
+    x_refs, (wq, wk, wv, wp) = refs[:late], refs[late : 4 + late]
+    weight_ref, pooled_ref, message, q_s, kt_s, v_s, w_s = refs[4 + late :]
+    at = q_a.shape[0]
+    q_s[:at], kt_s[:, :at], v_s[:at] = q_a[...], kt_a[...], v_a[...]
     for x_ref in x_refs:
         rows = slice(at, at + x_ref.shape[0])
         at += x_ref.shape[0]
         q_s[rows, :], kt_s[:, rows], v_s[rows, :] = project(x_ref[...], wq[...], wk[...], wv[...])
     heads, total = w_s.shape
     cols = heads * HD
-    first, fresh = q_e.shape[0], q_s.shape[0]
-    lane_e = lax.broadcasted_iota(jnp.int32, (first, LANES), 1)
-    lane_s = lax.broadcasted_iota(jnp.int32, (fresh, LANES), 1)
-
-    inverse = None
-    for head in range(heads + 1):
-        new, old = buffers[2 * (head % 2) :][:2], buffers[2 * ((head + 1) % 2) :][:2]
-        if head < heads:
-            queries_e, here = head_of(q_e, head, lane_e)
-            queries_s, _ = head_of(q_s, head, lane_s)
-            total_e = jnp.zeros((first, LANES), F32)
-            total_s = jnp.zeros((fresh, LANES), F32)
-        for at in range(0, total, step):
-            keys = slice(at, at + step)
-            at_s = slice(at - first, at - first + step)
-            if head < heads:
-                kt = kt_e[here, keys] if at < first else kt_s[here, at_s]
-                new[0][:, keys], part = scores(queries_s, kt)
-                total_s = total_s + part
-                if at >= first:
-                    new[1][:, at_s], part = scores(queries_e, kt)
-                    total_e = total_e + part
-            if head > 0:
-                if at < first:
-                    a = exp_e[(head - 1) * first : head * first, keys].astype(F32)
-                else:
-                    a = old[1][:, at_s]
-                a = [a * inverse[1], old[0][:, keys] * inverse[0]]
-                if first == fresh:
-                    a = [a[0] + a[1]]
-                w = sum(jnp.sum(part, axis=0, keepdims=True) for part in a)
-                w_s[head - 1 : head, keys] = w * (1.0 / total)
-        if head < heads:
-            total_e = jnp.sum(total_e, axis=1, keepdims=True) + sum_e[:, head : head + 1]
-            inverse = 1.0 / jnp.sum(total_s, axis=1, keepdims=True), 1.0 / total_e
+    first, then, fresh = q_e.shape[0], q_n.shape[0], q_s.shape[0]
+    bounds = [0, first, first + then, total]
+
+    def lanes(rows):
+        return lax.broadcasted_iota(jnp.int32, (rows, LANES), 1)
+
+    @pl.loop(0, cols // LANES)
+    def _(tile):
+        here = pl.ds(pl.multiple_of(tile * LANES, LANES), LANES)
+        for e in range(LANES // HD):
+            head = tile * (LANES // HD) + e
+
+            def exps(q, kt):
+                q_head = jnp.where(lanes(q.shape[0]) // HD == e, q[:, here], BF16(0))
+                return jnp.exp(jnp.dot(q_head, kt[here, :], preferred_element_type=F32))
+
+            def row_sum(a):
+                return jnp.sum(a, axis=1, keepdims=True)
+
+            def known(sums):
+                return row_sum(jnp.where(lanes(sums.shape[0]) == head, sums[...], 0.0))
+
+            def kept(a, rows, keys):
+                return a[pl.ds(pl.multiple_of(head * rows, rows), rows), keys].astype(F32)
+
+            new = [exps(q_s, kt) for kt in (kt_e, kt_n, kt_s)]
+            e_s, n_s = exps(q_e, kt_s), exps(q_n, kt_s)
+            by_s = 1.0 / sum(row_sum(a) for a in new)
+            by_e = 1.0 / (known(sum_e) + row_sum(e_s))
+            by_n = 1.0 / (known(sum_n) + row_sum(n_s))
+            columns = [
+                (new[0], kept(exp_e, first, slice(None)), kept(exp_n, then, slice(0, first))),
+                (new[1], kept(exp_x, first, slice(None)), kept(exp_n, then, slice(first, None))),
+                (new[2], e_s, n_s),
+            ]
+            for i, parts in enumerate(columns):
+                w = sum(
+                    jnp.sum(a * by, axis=0, keepdims=True)
+                    for a, by in zip(parts, (by_s, by_e, by_n))
+                )
+                w_s[pl.ds(head, 1), bounds[i] : bounds[i + 1]] = w * (1.0 / total)
 
     weights = w_s[...].astype(BF16)
     weight_ref[...] = weights
-    out = jnp.dot(weights[:, :first], v_e[...], preferred_element_type=F32)
-    out = out + jnp.dot(weights[:, first:], v_s[...], preferred_element_type=F32)
+    out = sum(
+        jnp.dot(weights[:, bounds[i] : bounds[i + 1]], v[...], preferred_element_type=F32)
+        for i, v in enumerate((v_e, v_n, v_s))
+    )
     row_head = lax.broadcasted_iota(jnp.int32, out.shape, 0)
     col_head = lax.broadcasted_iota(jnp.int32, out.shape, 1) // HD
     pooled = jnp.sum(jnp.where(row_head == col_head, out, 0.0), axis=0, keepdims=True)
@@ -177,18 +230,17 @@
         message[i] = embed
 
 
-def pool(early, ready, late, weights, wp, devices):
+def pool(early, after_early, ready, late, weights, wp, devices):
     d, cols = weights[0].shape
     heads = cols // HD
-    first = early[0].shape[0]
+    first, then = early[0].shape[0], after_early[0].shape[0]
     fresh = ready[0].shape[0] + sum(b.shape[0] for b in late)
-    total = first + fresh
+    total = first + then + fresh
     bottleneck = wp.shape[1]
-    pair = [pltpu.VMEM((fresh, total), F32), pltpu.VMEM((first, fresh), F32)]
     return call(
-        functools.partial(pool_kernel, len(late), min(first, fresh, 256)),
+        functools.partial(pool_kernel, len(late)),
         [((heads, total), BF16), ((1, cols), F32), ((devices, bottleneck // LANES, LANES), F32)],
-        [*early, *ready, *late, *weights, wp],
+        [*early[:4], *after_early, *ready, *late, *weights, wp],
         2 * fresh * d * cols * 3 + 2 * total * total * cols * 4,
         heads * total * total,
         scratch=[
@@ -196,10 +248,8 @@
             pltpu.VMEM((cols, fresh), BF16),
             pltpu.VMEM((fresh, cols), BF16),
             pltpu.VMEM((heads, total), F32),
-            *pair,
-            *pair,
         ],
-        mib=12 + 12 * fresh * (total + first) // 2**20,
+        mib=6 + 40 * fresh * total // 2**20,
     )
 
 
@@ -263,28 +313,40 @@
     return lax.optimization_barrier((x, others))[0]
 
 
-def token_block(s, clips, ranks):
-    return 0, lambda: ((lax.axis_index("cam") // ranks + s) % clips, slice(None), slice(None))
+def token_block(s, clips, ranks, start, size):
+    rows = pl.ds(start, size)
+    return 0, lambda: ((lax.axis_index("cam") // ranks + s) % clips, rows, slice(None))
 
 
 def from_other_groups(tokens, n_cam):
     clips, tok, d = tokens.shape
     ranks = n_cam // clips
+    half = tok // 2
+    pieces = [(s, c) for c in range(2) for s in range(1, clips)]
     mine, *sent = slices(
-        [tokens], [token_block(s, clips, ranks) for s in range(clips)], [(tok, d)] * clips
-    )
-    held = []
-    for s, block in enumerate(sent, 1):
-        perm = [(i, ((i // ranks + s) % clips) * ranks + i % ranks) for i in range(n_cam)]
-        held.append((s * ranks, lax.ppermute(block, "cam", perm)))
-    return mine, held
-
-
-def relay(blocks, n_cam, ranks):
+        [tokens],
+        [token_block(0, clips, ranks, 0, tok)]
+        + [token_block(s, clips, ranks, c * half, half) for s, c in pieces],
+        [(tok, d)] + [(half, d)] * len(pieces),
+    )
+    held = [[], []]
+    for (s, c), block in zip(pieces, sent):
+        perm = [
+            (i, ((i // ranks + s) % clips) * ranks + (i % ranks + c) % ranks) for i in range(n_cam)
+        ]
+        held[c].append((s * ranks + c % ranks, lax.ppermute(block, "cam", perm)))
+    return mine, *held
+
+
+def relay(blocks, n_cam, ranks, cuts=1):
     stage = list(blocks)
+    size = blocks[0][1].shape[0] // cuts
+    blocks = [(camera, b[i * size : (i + 1) * size]) for camera, b in blocks for i in range(cuts)]
     for t in range(1, ranks):
         perm = [(i, (i // ranks) * ranks + (i % ranks + t) % ranks) for i in range(n_cam)]
-        stage.extend((camera + t, lax.ppermute(b, "cam", perm)) for camera, b in blocks)
+        for camera, b in blocks:
+            label = camera // ranks * ranks + (camera + t) % ranks
+            stage.append((label, lax.ppermute(b, "cam", perm)))
     return stage
 
 
@@ -506,7 +568,7 @@
 
     with jax.named_scope("tokens_of_a_clip"):
         tokens = tokens.reshape(clips, tok, d)
-        mine, held = from_other_groups(tokens, n_cam)
+        mine, half, rest = from_other_groups(tokens, n_cam)
 
     with jax.named_scope("prototypes"):
         scale, proto_b = call(
@@ -537,11 +599,14 @@
         )
         stages = [relay([(0, mine)], n_cam, ranks)]
         early = first_blocks([b for _, b in stages[0]], weights)
-        held = [(camera, after(b, proto_b, *early)) for camera, b in held]
-        stages.append(relay(held, n_cam, ranks))
-        ready = project_blocks([b for _, b in held], weights)
-        late = [b for _, b in stages[1][len(held) :]]
-        key_weights, pooled, message = pool(early, ready, late, weights, wp, devices)
+        half = [(camera, after(b, proto_b, *early)) for camera, b in half]
+        stages.append(relay(half, n_cam, ranks, 2))
+        then = next_blocks([b for _, b in stages[1]], early, weights)
+        rest = [(camera, after(b, *then)) for camera, b in rest]
+        stages.append(relay(rest, n_cam, ranks))
+        ready = project_blocks([b for _, b in rest], weights)
+        late = [b for _, b in stages[2][len(rest) :]]
+        key_weights, pooled, message = pool(early, then, ready, late, weights, wp, devices)
 
     with jax.named_scope("mixtures"):
         cameras, blocks, at = {}, [], 0

time: 75.2 us -> 73.5 us (0.977)
  waiting for transfers between devices: 14.4 us -> 8.51 us
  local copies, waits for them, and re-layouts: 1.24 us -> 3.46 us
  Pallas kernels: 21 us -> 22.4 us
    ppermute x3 -> x6, waiting for transfers between devices: 6.58 us -> 2.26 us  [the longest x4 1.86 us: relay(): stage.append((label, lax.ppermute(b, 'cam', perm)))]
    unnamed x4 -> x16, local copies, waits for them, and re-layouts: 1.24 us -> 3.44 us
    all_to_all x1, waiting for transfers between devices: 6.78 us -> 5.2 us  [exchange(): return lax.all_to_all(message, ALL, split_axis=0, concat_axis=0, tiled=True)]
    pallas_call x12 -> x13, Pallas kernels: 21 us -> 22.4 us  [call(): pl.pallas_call(kernel, out_shape=tuple((jax.ShapeDtypeStruct(*o) for o in...]
    ppermute x3 -> x6, starting transfers between devices: 3.08 us -> 3.84 us  [the longest x2 2.63 us: from_other_groups(): held[c].append((s * ranks + c % ranks, lax.ppermute(block, 'cam', perm)))]
  transfers between devices with their start and end apart: 5 -> 8, of which waited for: 4 -> 6; matrix products, arithmetic and copies ran while one was open for 0% -> 0% of each run, Pallas kernels for 9% -> 13%
where the time goes in v6:
time: 73.5 us; the launch traced here: 73.2 us
  blocking collectives  28 us (38%)
  Pallas kernels  22.4 us (30%)
  starting transfers between devices  10 us (14%)
  waiting for transfers between devices  8.51 us (12%)
  local copies, waits for them, and re-layouts  3.46 us (5%)
  between operations  0.77 us (1%)
    all_to_all x3, blocking collectives, exchange(): return lax.all_to_all(message, ALL, split_axis=0, concat_axis=0, tiled=True)  28 us
    pallas_call x13, Pallas kernels, call(): pl.pallas_call(kernel, out_shape=tuple((jax.ShapeDtypeStruct(*o) for o in...  22.4 us
    all_to_all x1, starting transfers between devices, exchange(): return lax.all_to_all(message, ALL, split_axis=0, concat_axis=0, tiled=True)  6.08 us
    all_to_all x1, waiting for transfers between devices, exchange(): return lax.all_to_all(message, ALL, split_axis=0, concat_axis=0, tiled=True)  5.2 us
    unnamed x16, local copies, waits for them, and re-layouts  3.44 us
    ppermute x2, starting transfers between devices, from_other_groups(): held[c].append((s * ranks + c % ranks, lax.ppermute(block, 'cam', perm)))  2.63 us
    ppermute x4, waiting for transfers between devices, relay(): stage.append((label, lax.ppermute(b, 'cam', perm)))  1.86 us
  transfers between devices with their start and end apart: 8, of which 6 were waited for; matrix products, arithmetic and copies ran while one was open for 0% of the time, Pallas kernels for 13%

profile of v6, /device:TPU:0, one launch (start us, length us, event | category | flops | bytes accessed | tf_op | source)
XLA Modules:
  0.0 73.2 jit_solution(18050562574322389077)
XLA Ops:
  0.6 1.2 %tokens_of_a_clip.1 = (bf16[256,1024]{1,0:T(8,128)(2,1)S(1)}, bf16[128,1024]{1,0:T(8,128)(2,1)S(1)}, bf16[128,1024]{1,0:T(8,128)(2,1)S(1)}) custom-call(bf16[2,256,1024]{2,1,0:T(8,128)(2,1)} %bitcast.3), custom_call_target="tpu_custom_call" | custom-call | flops 1 | bytes 1 | tf_op jit(solution)/shard_map/tokens_of_a_clip/pallas_call | solution.py:28
  1.9 0.5 collective-permute-start
  2.4 2.6 %collective-permute-start.1 = (bf16[128,1024]{1,0:T(8,128)(2,1)S(1)}, bf16[128,1024]{1,0:T(8,128)(2,1)S(1)}, u32[]{:S(2)}, u32[]{:S(2)}) collective-permute-start(bf16[128,1024]{1,0:T(8,128)(2,1)S(1)} %get-tuple-element.58), channel_id=1, source_target_pairs={{0,16},{8,24},{16,0},{24,8},{1,17},{9,25},{17,1},{25,9},{2,18},{10... | collective-permute-start | bytes 786440 | tf_op jit(solution)/shard_map/tokens_of_a_clip/ppermute | solution.py:337
  5.0 0.1 collective-permute-start.4
  5.0 0.0 copy-start
  5.0 1.2 %copy-done = bf16[256,2048]{1,0:T(8,128)(2,1)S(1)} copy-done((bf16[256,2048]{1,0:T(8,128)(2,1)S(1)}, bf16[256,2048]{1,0:T(8,128)(2,1)}, u32[]{:S(2)}) %copy-start) | copy-done | bytes 1048600
  6.2 0.4 prototypes.1
  6.6 2.1 %pooling.5 = (bf16[1024,512]{1,0:T(8,128)(2,1)S(1)}, bf16[1024,512]{1,0:T(8,128)(2,1)S(1)}, bf16[1024,512]{1,0:T(8,128)(2,1)S(1)}, bf16[512,256]{1,0:T(8,128)(2,1)S(1)}, bf16[256,256]{1,0:T(8,128)(2,1)S(1)}) custom-call(bf16[1024,1024]{1,0:T(8,128)(2,1)} %refs_0_.1, bf16[1024,1024]{1,0:T(8,128)(2,1)} %refs_1_.1, bf16[1024,1024]{1,0:T(8,128)(2,1)} %refs_2_.1, ...), custom_call_target="tpu_custom_call" | custom-call | flops 1 | bytes 1 | tf_op jit(solution)/shard_map/pooling/pallas_call | solution.py:28
  8.7 0.0 copy-start.6
  8.7 0.6 copy-done.6
  9.4 0.0 collective-permute-done.refs_1_
  9.4 3.1 %pooling.6 = (bf16[512,512]{1,0:T(8,128)(2,1)S(1)}, bf16[512,512]{1,0:T(8,128)(2,1)S(1)}, bf16[512,512]{1,0:T(8,128)(2,1)S(1)}, bf16[4096,512]{1,0:T(8,128)(2,1)S(1)}, f32[512,128]{1,0:T(8,128)S(1)}) custom-call(bf16[256,1024]{1,0:T(8,128)(2,1)S(1)} %get-tuple-element.49.refs_0_, bf16[256,1024]{1,0:T(8,128)(2,1)S(1)} %collective-permute-done.refs_1_, ...), custom_call_target="tpu_custom_call" | custom-call | flops 1 | bytes 1 | tf_op jit(solution)/shard_map/pooling/pallas_call | solution.py:28
  12.5 0.0 collective-permute-done.1.refs_0_.refs_2_
  12.5 0.2 collective-permute-start.3
  12.7 0.4 collective-permute-start.2
  13.1 0.8 %collective-permute-done.3.refs_2_.refs_4_ = bf16[64,1024]{1,0:T(8,128)(2,1)S(1)} collective-permute-done((bf16[64,1024]{1,0:T(8,128)(2,1)S(1)}, bf16[64,1024]{1,0:T(8,128)(2,1)S(1)}, u32[]{:S(2)}, u32[]{:S(2)}) %collective-permute-start.3) | collective-permute-done | bytes 131104 | tf_op jit(solution)/shard_map/pooling/ppermute | solution.py:349
  13.9 0.2 collective-permute-done.2.refs_1_.refs_3_
  14.1 0.0 copy-start.2
  14.1 2.7 %pooling.7 = (bf16[256,512]{1,0:T(8,128)(2,1)S(1)}, bf16[512,256]{1,0:T(8,128)(2,1)S(1)}, bf16[256,512]{1,0:T(8,128)(2,1)S(1)}, bf16[2048,768]{1,0:T(8,128)(2,1)...) custom-call(bf16[512,512]{1,0:T(8,128)(2,1)S(1)} %get-tuple-element.53.q_e.refs_0_, ...), custom_call_target="tpu_custom_call" | custom-call | flops 1 | bytes 1 | tf_op jit(solution)/shard_map/pooling/pallas_call | solution.py:28
  16.8 0.0 copy-done.2
  16.8 0.4 collective-permute-done.4.refs_0_.refs_5_
  17.2 0.1 collective-permute-start.5
  17.3 0.6 pooling.8
  17.9 0.8 %collective-permute-done.5.refs_14_.refs_6_ = bf16[128,1024]{1,0:T(8,128)(2,1)S(1)} collective-permute-done((bf16[128,1024]{1,0:T(8,128)(2,1)S(1)}, bf16[128,1024]{1,0:T(8,128)(2,1)S(1)}, u32[]{:S(2)}, u32[]{:S(2)}) %collective-permute-start.5) | collective-permute-done | bytes 262176 | tf_op jit(solution)/shard_map/pooling/ppermute | solution.py:349
  18.7 7.8 %pooling.9 = (bf16[8,1024]{1,0:T(8,128)(2,1)S(1)}, f32[1,512]{1,0:T(1,128)S(1)}, f32[32,2,128]{2,1,0:T(2,128)}) custom-call(bf16[512,512]{1,0:T(8,128)(2,1)S(1)} %get-tuple-element.53.q_e.refs_0_, bf16[512,512]{1,0:T(8,128)(2,1)S(1)} %get-tuple-element.54.kt_e.refs_1_, bf16[512,512]{1,0:T(8,128)(2,1)S(1)} %get-tuple-element.55.refs_2_, ...), custom_call_target="tpu_custom_call" | custom-call | flops 1 | bytes 1 | tf_op jit(solution)/shard_map/pooling/pallas_call | solution.py:28
  26.6 6.1 %all-to-all-start = ((f32[32,2,128]{2,1,0:T(2,128)}), f32[32,2,128]{2,1,0:T(2,128)}, u32[]{:S(2)}, u32[]{:S(2)}) async-start(f32[32,2,128]{2,1,0:T(2,128)} %get-tuple-element.74), calls=%async_computation | async-start | bytes 65536 | tf_op jit(solution)/shard_map/logits/all_to_all | solution.py:378
  32.7 0.0 copy-start.3
  32.7 0.9 %copy-done.3 = bf16[64,1024]{1,0:T(8,128)(2,1)S(1)} copy-done((bf16[64,1024]{1,0:T(8,128)(2,1)S(1)}, bf16[64,1024]{1,0:T(8,128)(2,1)}, u32[]{:S(2)}) %copy-start.3) | copy-done | bytes 131096
  33.6 0.4 mixtures.1.side
  34.0 0.0 copy-start.4
  34.0 0.6 copy-done.4
  34.6 0.0 copy-start.1
  34.6 0.0 copy-start.7
  34.6 5.2 %all-to-all-done.came = f32[32,2,128]{2,1,0:T(2,128)} async-done(((f32[32,2,128]{2,1,0:T(2,128)}), f32[32,2,128]{2,1,0:T(2,128)}, u32[]{:S(2)}, u32[]{:S(2)}) %all-to-all-start) | async-done | bytes 32800 | tf_op jit(solution)/shard_map/logits/all_to_all | solution.py:378
  39.8 0.0 copy-start.5
  39.8 1.4 %logits.1 = (f32[16,256]{1,0:T(8,128)S(1)}, f32[16,128]{1,0:T(8,128)S(1)}, f32[16,2048]{1,0:T(8,128)S(1)}, f32[16,2048]{1,0:T(8,128)S(1)}, f32[32,2,128]{2,1,0:T(2,128)S(1)}) custom-call(f32[32,2,128]{2,1,0:T(2,128)} %all-to-all-done.came, bf16[256,2048]{1,0:T(8,128)(2,1)S(1)} %get-tuple-element.59.proto), custom_call_target="tpu_custom_call" | custom-call | flops 1 | bytes 1 | tf_op jit(solution)/shard_map/logits/pallas_call | solution.py:28
  41.3 8.9 %all_to_all.20.came = f32[32,2,128]{2,1,0:T(2,128)S(1)} all-to-all(f32[32,2,128]{2,1,0:T(2,128)S(1)} %get-tuple-element.78), channel_id=1, replica_groups=mesh['cam'=4,'clip'=8] {'cam','clip'}, dimensions={0} | all-to-all | bytes 65536 | tf_op jit(solution)/shard_map/row_total_1/all_to_all | solution.py:378
  50.1 0.2 row_total_1.1
  50.4 8.9 %all_to_all.21.came = f32[32,2,128]{2,1,0:T(2,128)S(1)} all-to-all(f32[32,2,128]{2,1,0:T(2,128)S(1)} %get-tuple-element.80), channel_id=1, replica_groups=mesh['cam'=4,'clip'=8] {'cam','clip'}, dimensions={0} | all-to-all | bytes 65536 | tf_op jit(solution)/shard_map/row_total_2/all_to_all | solution.py:378
  59.3 0.4 row_total_2.1
  59.7 0.1 collective-permute-start.6
  59.9 1.1 %collective-permute-done.6.got = f32[16,128]{1,0:T(8,128)S(1)} collective-permute-done((f32[16,128]{1,0:T(8,128)S(1)}, f32[16,128]{1,0:T(8,128)S(1)}, u32[]{:S(2)}, u32[]{:S(2)}) %collective-permute-start.6) | collective-permute-done | bytes 8224 | tf_op jit(solution)/shard_map/row_total_3/ppermute | solution.py:667
  60.9 0.0 copy-done.5
  60.9 10.2 %all_to_all.22 = bf16[32,24,128]{2,1,0:T(8,128)(2,1)S(1)} all-to-all(bf16[32,24,128]{2,1,0:T(8,128)(2,1)S(1)} %row_total_3.1), channel_id=1, replica_groups=mesh['cam'=4,'clip'=8] {'cam','clip'}, dimensions={0} | all-to-all | bytes 393216 | tf_op jit(solution)/shard_map/row_total_3/all_to_all | solution.py:378
  71.2 0.0 copy-done.1
  71.2 0.0 copy-done.7
  71.2 2.0 %outputs.1 = (f32[16,2048]{1,0:T(8,128)}, f32[256,2048]{1,0:T(8,128)}, f32[128,256]{1,0:T(8,128)}, f32[128,256]{1,0:T(8,128)}) custom-call(bf16[2,2,8,24,128]{4,3,2,1,0:T(8,128)(2,1)S(1)} %bitcast.2, f32[16,256]{1,0:T(8,128)S(1)} %get-tuple-element.87.unit_ref, f32[16,128]{1,0:T(8,128)S(1)} %get-tuple-element.88.norm_ref, ...), custom_call_target="tpu_custom_call" | custom-call | flops 1 | bytes 1 | tf_op jit(solution)/shard_map/outputs/pallas_call | solution.py:28
  (2 shorter events, 0.0 us)
Async XLA Ops:
  1.9 7.5 %collective-permute-start = (bf16[256,1024]{1,0:T(8,128)(2,1)S(1)}, bf16[256,1024]{1,0:T(8,128)(2,1)S(1)}, u32[]{:S(2)}, u32[]{:S(2)}) collective-permute-start(bf16[256,1024]{1,0:T(8,128)(2,1)S(1)} %get-tuple-element.49.refs_0_), channel_id=1, source_target_pairs={{0,8},{8,0},{16,24},{24,16},{1,9},{9,1},{17,25},{25,17},{2,10},{10... | collective-permute-start | bytes 1572872 | tf_op jit(solution)/shard_map/pooling/ppermute | solution.py:349
  2.4 10.1 %collective-permute-start.1 = (bf16[128,1024]{1,0:T(8,128)(2,1)S(1)}, bf16[128,1024]{1,0:T(8,128)(2,1)S(1)}, u32[]{:S(2)}, u32[]{:S(2)}) collective-permute-start(bf16[128,1024]{1,0:T(8,128)(2,1)S(1)} %get-tuple-element.58), channel_id=1, source_target_pairs={{0,16},{8,24},{16,0},{24,8},{1,17},{9,25},{17,1},{25,9},{2,18},{10... | collective-permute-start | bytes 786440 | tf_op jit(solution)/shard_map/tokens_of_a_clip/ppermute | solution.py:337
  5.0 12.3 %collective-permute-start.4 = (bf16[128,1024]{1,0:T(8,128)(2,1)S(1)}, bf16[128,1024]{1,0:T(8,128)(2,1)S(1)}, u32[]{:S(2)}, u32[]{:S(2)}) collective-permute-start(bf16[128,1024]{1,0:T(8,128)(2,1)S(1)} %get-tuple-element.68), channel_id=1, source_target_pairs={{0,24},{8,16},{16,8},{24,0},{1,25},{9,17},{17,9},{25,1},{2,26},{10... | collective-permute-start | bytes 786440 | tf_op jit(solution)/shard_map/tokens_of_a_clip/ppermute | solution.py:337
  5.0 1.2 %copy-start = (bf16[256,2048]{1,0:T(8,128)(2,1)S(1)}, bf16[256,2048]{1,0:T(8,128)(2,1)}, u32[]{:S(2)}) copy-start(bf16[256,2048]{1,0:T(8,128)(2,1)} %proto.3) | copy-start | bytes 3145732
  8.7 0.7 copy-start.6
  12.5 1.4 %collective-permute-start.3 = (bf16[64,1024]{1,0:T(8,128)(2,1)S(1)}, bf16[64,1024]{1,0:T(8,128)(2,1)S(1)}, u32[]{:S(2)}, u32[]{:S(2)}) collective-permute-start(bf16[64,1024]{1,0:T(8,128)(2,1)S(1)} %get-tuple-element.94), channel_id=1, source_target_pairs={{0,8},{8,0},{16,24},{24,16},{1,9},{9,1},{17,25},{25,17},{2,10},{10... | collective-permute-start | bytes 393224 | tf_op jit(solution)/shard_map/pooling/ppermute | solution.py:349
  12.7 1.4 %collective-permute-start.2 = (bf16[64,1024]{1,0:T(8,128)(2,1)S(1)}, bf16[64,1024]{1,0:T(8,128)(2,1)S(1)}, u32[]{:S(2)}, u32[]{:S(2)}) collective-permute-start(bf16[64,1024]{1,0:T(8,128)(2,1)S(1)} %get-tuple-element.95), channel_id=1, source_target_pairs={{0,8},{8,0},{16,24},{24,16},{1,9},{9,1},{17,25},{25,17},{2,10},{10... | collective-permute-start | bytes 393224 | tf_op jit(solution)/shard_map/pooling/ppermute | solution.py:349
  14.1 2.7 %copy-start.2 = (bf16[64,1024]{1,0:T(8,128)(2,1)}, bf16[64,1024]{1,0:T(8,128)(2,1)S(1)}, u32[]{:S(2)}) copy-start(bf16[64,1024]{1,0:T(8,128)(2,1)S(1)} %collective-permute-done.2.refs_1_.refs_3_) | copy-start | bytes 393220
  17.2 1.5 %collective-permute-start.5 = (bf16[128,1024]{1,0:T(8,128)(2,1)S(1)}, bf16[128,1024]{1,0:T(8,128)(2,1)S(1)}, u32[]{:S(2)}, u32[]{:S(2)}) collective-permute-start(bf16[128,1024]{1,0:T(8,128)(2,1)S(1)} %collective-permute-done.4.refs_0_.refs_5_), channel_id=1, source_target_pairs={{0,8},{8,0},{16,24},{24,16},{1,9},{9,1},{17,25},{25,17},{2,10},{10... | collective-permute-start | bytes 786440 | tf_op jit(solution)/shard_map/pooling/ppermute | solution.py:349
  26.6 13.2 %all-to-all-start = ((f32[32,2,128]{2,1,0:T(2,128)}), f32[32,2,128]{2,1,0:T(2,128)}, u32[]{:S(2)}, u32[]{:S(2)}) async-start(f32[32,2,128]{2,1,0:T(2,128)} %get-tuple-element.74), calls=%async_computation | async-start | bytes 65536 | tf_op jit(solution)/shard_map/logits/all_to_all | solution.py:378
  32.7 0.9 %copy-start.3 = (bf16[64,1024]{1,0:T(8,128)(2,1)S(1)}, bf16[64,1024]{1,0:T(8,128)(2,1)}, u32[]{:S(2)}) copy-start(bf16[64,1024]{1,0:T(8,128)(2,1)} %copy-done.2) | copy-start | bytes 393220
  34.0 0.7 copy-start.4
  34.6 36.6 %copy-start.1 = (bf16[256,2048]{1,0:T(8,128)(2,1)S(1)}, bf16[256,2048]{1,0:T(8,128)(2,1)}, u32[]{:S(2)}) copy-start(bf16[256,2048]{1,0:T(8,128)(2,1)} %proto.3) | copy-start | bytes 3145732
  34.6 36.6 %copy-start.7 = (bf16[256,256]{1,0:T(8,128)(2,1)S(1)}, bf16[256,256]{1,0:T(8,128)(2,1)}, u32[]{:S(2)}) copy-start(bf16[256,256]{1,0:T(8,128)(2,1)} %copy-done.6) | copy-start | bytes 393220
  39.8 21.1 %copy-start.5 = (f32[32,8,128]{2,1,0:T(8,128)S(1)}, f32[32,8,128]{2,1,0:T(8,128)}, u32[]{:S(2)}) copy-start(f32[32,8,128]{2,1,0:T(8,128)} %copy-done.4) | copy-start | bytes 393220
  59.7 1.2 %collective-permute-start.6 = (f32[16,128]{1,0:T(8,128)S(1)}, f32[16,128]{1,0:T(8,128)S(1)}, u32[]{:S(2)}, u32[]{:S(2)}) collective-permute-start(f32[16,128]{1,0:T(8,128)S(1)} %get-tuple-element.83), channel_id=1, source_target_pairs={{0,8},{8,0},{16,24},{24,16},{1,9},{9,1},{17,25},{25,17},{2,10},{10... | collective-permute-start | bytes 24584 | tf_op jit(solution)/shard_map/row_total_3/ppermute | solution.py:667

commit v7 on v6

--- a/solution.py
+++ b/solution.py
@@ -82,12 +82,16 @@
     for head in range(cols // HD):
         q_head, here = head_of(q_ref, head, lane)
         e, part = scores(q_head, kt_ref[here, :])
-        exp_ref[head * rows : (head + 1) * rows, :] = e.astype(BF16)
+        exp_ref[head * rows : (head + 1) * rows, :] = e.astype(exp_ref.dtype)
         sums = jnp.where(lane == head, jnp.sum(part, axis=1, keepdims=True), sums)
     sum_ref[...] = sums
 
 
-def first_blocks(blocks, weights):
+def kept_type(heads, rows):
+    return F32 if 4 * heads * rows * rows <= 20 * 2**20 else BF16
+
+
+def first_blocks(blocks, weights, kept):
     d, cols = weights[0].shape
     rows = sum(b.shape[0] for b in blocks)
     heads = cols // HD
@@ -97,7 +101,7 @@
             ((rows, cols), BF16),
             ((cols, rows), BF16),
             ((rows, cols), BF16),
-            ((heads * rows, rows), BF16),
+            ((heads * rows, rows), kept),
             ((rows, LANES), F32),
         ],
         [*blocks, *weights],
@@ -121,9 +125,9 @@
         a, part_a = scores(queries_n, kt_e[here, :])
         b, part_b = scores(queries_n, kt_n[here, :])
         x, part_x = scores(queries_e, kt_n[here, :])
-        exp_n[head * rows : (head + 1) * rows, :first] = a.astype(BF16)
-        exp_n[head * rows : (head + 1) * rows, first:] = b.astype(BF16)
-        exp_x[head * first : (head + 1) * first, :] = x.astype(BF16)
+        exp_n[head * rows : (head + 1) * rows, :first] = a.astype(exp_n.dtype)
+        exp_n[head * rows : (head + 1) * rows, first:] = b.astype(exp_n.dtype)
+        exp_x[head * first : (head + 1) * first, :] = x.astype(exp_x.dtype)
         part = jnp.sum(part_a + part_b, axis=1, keepdims=True)
         sums_n = jnp.where(lane_n == head, part, sums_n)
         part = jnp.sum(part_x, axis=1, keepdims=True)
@@ -144,8 +148,8 @@
             ((rows, cols), BF16),
             ((cols, rows), BF16),
             ((rows, cols), BF16),
-            ((heads * rows, first + rows), BF16),
-            ((heads * first, rows), BF16),
+            ((heads * rows, first + rows), early[3].dtype),
+            ((heads * first, rows), early[3].dtype),
             ((rows, LANES), F32),
             ((first, LANES), F32),
         ],
@@ -275,7 +279,6 @@
         j, p = divmod(i % (clips * n_clip), n_clip)
         side[i] = jnp.concatenate(
             [
-                jnp.zeros((DIGITS, LANES), F32),
                 lanes(pooled_ref[...], i % (pooled_ref.shape[1] // share)),
                 lanes(mix[j * heads_here : (j + 1) * heads_here], p),
             ],
@@ -370,6 +373,32 @@
     return jnp.sum(jnp.where(lane == row, line, 0.0), axis=1, keepdims=True)
 
 
+def digit_rows(batch, columns):
+    return -(-columns * DIGITS // (LANES // batch))
+
+
+def pack(*columns):
+    batch = columns[0].shape[0]
+    slots = LANES // batch
+    lines = [jnp.zeros((1, LANES), F32)] * digit_rows(batch, len(columns))
+    for i, rest in enumerate(columns):
+        for slot in range(i * DIGITS, (i + 1) * DIGITS):
+            digit = rest.astype(BF16).astype(F32)
+            rest = rest - digit
+            row, at = divmod(slot, slots)
+            lines[row] = lines[row] + to_lanes(digit, at * batch)
+    return jnp.concatenate(lines, axis=0)
+
+
+def unpack(lines, batch, i):
+    slots = LANES // batch
+    column = jnp.zeros((batch, 1), F32)
+    for slot in range(i * DIGITS, (i + 1) * DIGITS):
+        row, at = divmod(slot, slots)
+        column = column + from_lanes(lines[row : row + 1], batch, at * batch)
+    return column
+
+
 def spread(column):
     return jnp.broadcast_to(column, (column.shape[0], LANES))
 
@@ -379,7 +408,7 @@
 
 
 def logits_kernel(
-    clips, ranks, n_clip, came, proto, unit_ref, norm_ref, exp_ref, assign_ref, message
+    clips, ranks, n_clip, came, proto, side, unit_ref, norm_ref, exp_ref, assign_ref, message
 ):
     rows = []
     for g in range(clips):
@@ -401,28 +430,32 @@
         exponents.astype(BF16), proto[...], TRANSPOSED, preferred_element_type=F32
     )
     batch = part.shape[0]
-    line = to_lanes(jnp.sum(assign, axis=1, keepdims=True)) + to_lanes(
-        jnp.sum(exponents, axis=1, keepdims=True), batch
+    lines = pack(
+        jnp.sum(assign, axis=1, keepdims=True), jnp.sum(exponents, axis=1, keepdims=True)
     )
     halves = part.shape[1] // LANES
+    high = part.astype(BF16).astype(F32)
+    low = part - high
     for i in range(message.shape[0]):
         if i < halves * batch:
             h, b = divmod(i, batch)
-            piece = part[b : b + 1, h * LANES : (h + 1) * LANES]
+            here = slice(h * LANES, (h + 1) * LANES)
+            piece = [high[b : b + 1, here], low[b : b + 1, here]]
         else:
-            piece = jnp.zeros((1, LANES), F32)
-        message[i] = jnp.concatenate([piece, line], axis=0)
+            piece = [jnp.zeros((2, LANES), F32)]
+        message[i] = jnp.concatenate([*piece, lines, side[i]], axis=0).astype(BF16)
 
 
 def second_kernel(came, assign_ref, assign_out, message, total_ref):
     batch = assign_ref.shape[0]
-    came = jnp.sum(came[...], axis=0)
-    total_ref[...] = spread(from_lanes(came[1:2], batch, batch))
-    assign = assign_ref[...] / from_lanes(came[1:2], batch)
+    came = jnp.sum(came[...].astype(F32), axis=0)
+    lines = came[2 : 2 + digit_rows(batch, 2)]
+    total_ref[...] = spread(unpack(lines, batch, 1))
+    assign = assign_ref[...] / unpack(lines, batch, 0)
     assign = assign / jnp.sum(assign, axis=0, keepdims=True)
     assign_out[...] = assign
     line = to_lanes(jnp.sum(assign, axis=1, keepdims=True))
-    out = jnp.concatenate([came[0:1], line], axis=0)
+    out = jnp.concatenate([came[0:1] + came[1:2], line], axis=0)
     for i in range(message.shape[0]):
         message[i] = out
 
@@ -444,22 +477,21 @@
     low, high = part[:, :half], part[:, half:]
     keep_ref[...] = jnp.where(odd, high, low)
     send_ref[...] = jnp.where(odd, low, high)
-    rest = to_lanes(jnp.sum(assign, axis=1, keepdims=True))
-    digits_ref[...] = jnp.zeros(digits_ref.shape, F32)
-    for i in range(DIGITS):
-        digit = rest.astype(BF16).astype(F32)
-        digits_ref[i : i + 1, :] = digit
-        rest = rest - digit
+    digits_ref[...] = pack(jnp.sum(assign, axis=1, keepdims=True))
     for h in range(halves):
         for b in range(batch):
             grad_ref[b : b + 1, h * LANES : (h + 1) * LANES] = came[h * batch + b][0:1]
 
 
-def message_kernel(keep, got, digits, side, message):
-    part = (keep[...] + got[...]).astype(BF16)
-    batch = part.shape[0]
-    message[:, :batch, :] = jnp.broadcast_to(part[None], (message.shape[0],) + part.shape)
-    message[:, batch:, :] = (side[...] + digits[...][None]).astype(BF16)
+def message_kernel(keep, got, digits, message):
+    rows = jnp.concatenate([keep[...] + got[...], digits[...]], axis=0)
+    width = message.shape[2] // LANES
+    rows = [rows[i : i + 1] for i in range(rows.shape[0])]
+    rows += [jnp.zeros((1, LANES), F32)] * (2 * width - len(rows))
+    long = [jnp.concatenate(rows[i * width : (i + 1) * width], axis=1) for i in range(2)]
+    out = jnp.concatenate(long, axis=0).astype(BF16)
+    for i in range(message.shape[0]):
+        message[i] = out
 
 
 def output_kernel(
@@ -467,6 +499,7 @@
     n_cam,
     block,
     came,
+    came_side,
     unit_ref,
     norm_ref,
     exp_ref,
@@ -500,8 +533,16 @@
     for cam in range(n_cam):
         part = jnp.sum(came[cam // ranks, cam % ranks].astype(F32), axis=0)
         sums[cam % 2] = sums[cam % 2] + part
-    line = jnp.sum((sums[0] + sums[1])[batch : batch + DIGITS], axis=0, keepdims=True)
-    by_assign = protos / from_lanes(line, batch)
+    long = came.shape[4] // LANES
+
+    def short(x, start, stop):
+        places = [divmod(i, long) for i in range(start, stop)]
+        return jnp.concatenate(
+            [x[r : r + 1, i * LANES : (i + 1) * LANES] for r, i in places], axis=0
+        )
+
+    lines = short(sums[0] + sums[1], batch, batch + digit_rows(batch, 1))
+    by_assign = protos / unpack(lines, batch, 0)
     by_prob = protos / total_ref[:, :1]
     unit = unit_ref[...]
     unit_b = unit.astype(BF16)
@@ -522,19 +563,21 @@
         send(proto_grad.at[:, here], proto_grad_out.at[:, here])
     send(codes, codes_out)
 
-    assign_grad = jnp.concatenate([s[:batch] for s in sums], axis=1)
+    assign_grad = jnp.concatenate([short(s, 0, batch) for s in sums], axis=1)
     grad_unit = prob_grad[...] * by_prob - assign_grad * by_assign
     grad_embed = (
         grad_unit - unit * jnp.sum(unit * grad_unit, axis=1, keepdims=True)
     ) / norm_ref[:, :1]
     grad_embed = grad_embed.astype(BF16)
 
+    side = 2 + digit_rows(batch, 2)
+
     def rows(rank, row):
-        picked = [came[g, rank].astype(F32)[:, row, :] for g in range(clips)]
+        picked = [came_side[g, rank].astype(F32)[:, row, :] for g in range(clips)]
         return jnp.concatenate(picked, axis=0)[:, :share].astype(BF16)
 
     grad_proj[...] = lax.dot_general(
-        rows(lax.axis_index("clip") * share // cols, batch + DIGITS), grad_embed, OUTER, preferred_element_type=F32
+        rows(lax.axis_index("clip") * share // cols, side), grad_embed, OUTER, preferred_element_type=F32
     )
     send(grad_proj, grad_proj_out)
     grad_pooled = lax.dot_general(
@@ -543,7 +586,7 @@
     col_head = lax.broadcasted_iota(jnp.int32, grad_value.shape, 1) // HD
     value = jnp.zeros(grad_value.shape, F32)
     for head in range(grad_value.shape[1] // HD):
-        mixed = rows(lax.axis_index("cam") // clips, batch + DIGITS + 1 + head)
+        mixed = rows(lax.axis_index("cam") // clips, side + 1 + head)
         out = lax.dot_general(mixed, grad_pooled, OUTER, preferred_element_type=F32)
         value = jnp.where(col_head == head, out, value)
     grad_value[...] = value
@@ -598,7 +641,8 @@
             [(d, cols)] * 3 + [(cols, bottleneck), (width, bottleneck)],
         )
         stages = [relay([(0, mine)], n_cam, ranks)]
-        early = first_blocks([b for _, b in stages[0]], weights)
+        kept = kept_type(heads, n_cam * tok - (n_cam - ranks) * tok // 2)
+        early = first_blocks([b for _, b in stages[0]], weights, kept)
         half = [(camera, after(b, proto_b, *early)) for camera, b in half]
         stages.append(relay(half, n_cam, ranks, 2))
         then = next_blocks([b for _, b in stages[1]], early, weights)
@@ -617,7 +661,7 @@
                 at += block.shape[0]
         (side,) = call(
             functools.partial(mixture_kernel, list(cameras.values()), clips, n_clip),
-            [((devices, DIGITS + 1 + heads_here, LANES), F32)],
+            [((devices, 1 + heads_here, LANES), F32)],
             [key_weights, pooled, *blocks],
             2 * at * d * 32,
             mib=8,
@@ -632,15 +676,15 @@
                 ((batch, LANES), F32),
                 ((batch, columns), F32),
                 ((batch, columns), F32),
-                ((devices, 2, LANES), F32),
+                ((devices, 2 + digit_rows(batch, 2) + side.shape[1], LANES), BF16),
             ],
-            [came, proto_b],
+            [came, proto_b, side],
             4 * batch * bottleneck * columns,
             2 * batch * columns,
         )
 
     with jax.named_scope("row_total_1"):
-        came = exchange(message)
+        came_side = came = exchange(message)
         assign, message, total = call(
             second_kernel,
             [((batch, columns), F32), ((devices, 2, LANES), F32), ((batch, LANES), F32)],
@@ -656,7 +700,7 @@
                 ((batch, columns), F32),
                 ((batch, bottleneck // 2), F32),
                 ((batch, bottleneck // 2), F32),
-                (side.shape[1:], F32),
+                ((digit_rows(batch, 1), LANES), F32),
                 ((batch, bottleneck), F32),
             ],
             [came, assign, proto_b],
@@ -667,8 +711,8 @@
         got = lax.ppermute(send, "cam", [(i, i ^ 1) for i in range(n_cam)])
         (message,) = call(
             message_kernel,
-            [((devices, batch + side.shape[1], LANES), BF16)],
-            [keep, got, digits, side],
+            [((devices, 2, -(-(batch + digits.shape[0]) // 2) * LANES), BF16)],
+            [keep, got, digits],
             devices * batch * LANES,
         )
         came = exchange(after(message, proj_rows))
@@ -677,6 +721,7 @@
         block = min(columns, 512)
         ins = [
             came.reshape((clips, ranks, n_clip) + came.shape[1:]),
+            came_side.reshape((clips, ranks, n_clip) + came_side.shape[1:]),
             unit,
             norm,
             exponents,

time: 73.5 us -> 71.6 us (0.974)
  local copies, waits for them, and re-layouts: 3.46 us -> 1.25 us
  waiting for transfers between devices: 8.51 us -> 10.7 us
  Pallas kernels: 22.4 us -> 21.3 us
    unnamed x16 -> x4, local copies, waits for them, and re-layouts: 3.44 us -> 1.23 us
    all_to_all x1, waiting for transfers between devices: 5.2 us -> 6.78 us  [exchange(): return lax.all_to_all(message, ALL, split_axis=0, concat_axis=0, tiled=True)]
    pallas_call x13, Pallas kernels: 22.4 us -> 21.3 us  [call(): pl.pallas_call(kernel, out_shape=tuple((jax.ShapeDtypeStruct(*o) for o in...]
  transfers between devices with their start and end apart: 8 -> 8, of which waited for: 6 -> 7; matrix products, arithmetic and copies ran while one was open for 0% -> 0% of each run, Pallas kernels for 13% -> 13%
where the time goes in v7:
time: 71.6 us; the launch traced here: 71.3 us
  blocking collectives  27.4 us (38%)
  Pallas kernels  21.3 us (30%)
  waiting for transfers between devices  10.7 us (15%)
  starting transfers between devices  9.91 us (14%)
  local copies, waits for them, and re-layouts  1.25 us (2%)
  between operations  0.75 us (1%)
    all_to_all x3, blocking collectives, exchange(): return lax.all_to_all(message, ALL, split_axis=0, concat_axis=0, tiled=True)  27.4 us
    pallas_call x13, Pallas kernels, call(): pl.pallas_call(kernel, out_shape=tuple((jax.ShapeDtypeStruct(*o) for o in...  21.3 us
    all_to_all x1, waiting for transfers between devices, exchange(): return lax.all_to_all(message, ALL, split_axis=0, concat_axis=0, tiled=True)  6.78 us
    all_to_all x1, starting transfers between devices, exchange(): return lax.all_to_all(message, ALL, split_axis=0, concat_axis=0, tiled=True)  5.95 us
    ppermute x2, starting transfers between devices, from_other_groups(): held[c].append((s * ranks + c % ranks, lax.ppermute(block, 'cam', perm)))  2.63 us
    ppermute x4, waiting for transfers between devices, relay(): stage.append((label, lax.ppermute(b, 'cam', perm)))  1.86 us
  transfers between devices with their start and end apart: 8, of which 7 were waited for; matrix products, arithmetic and copies ran while one was open for 0% of the time, Pallas kernels for 13%

profile of v7, /device:TPU:0, one launch (start us, length us, event | category | flops | bytes accessed | tf_op | source)
XLA Modules:
  0.0 71.3 jit_solution(2747166922563912170)
XLA Ops:
  0.6 1.2 %tokens_of_a_clip.1 = (bf16[256,1024]{1,0:T(8,128)(2,1)S(1)}, bf16[128,1024]{1,0:T(8,128)(2,1)S(1)}, bf16[128,1024]{1,0:T(8,128)(2,1)S(1)}) custom-call(bf16[2,256,1024]{2,1,0:T(8,128)(2,1)} %bitcast.5), custom_call_target="tpu_custom_call" | custom-call | flops 1 | bytes 1 | tf_op jit(solution)/shard_map/tokens_of_a_clip/pallas_call | solution.py:28
  1.9 0.5 collective-permute-start
  2.4 2.6 %collective-permute-start.1 = (bf16[128,1024]{1,0:T(8,128)(2,1)S(1)}, bf16[128,1024]{1,0:T(8,128)(2,1)S(1)}, u32[]{:S(2)}, u32[]{:S(2)}) collective-permute-start(bf16[128,1024]{1,0:T(8,128)(2,1)S(1)} %get-tuple-element.58), channel_id=1, source_target_pairs={{0,16},{8,24},{16,0},{24,8},{1,17},{9,25},{17,1},{25,9},{2,18},{10... | collective-permute-start | bytes 786440 | tf_op jit(solution)/shard_map/tokens_of_a_clip/ppermute | solution.py:340
  5.0 0.1 collective-permute-start.4
  5.0 0.0 copy-start
  5.0 1.2 %copy-done = bf16[256,2048]{1,0:T(8,128)(2,1)S(1)} copy-done((bf16[256,2048]{1,0:T(8,128)(2,1)S(1)}, bf16[256,2048]{1,0:T(8,128)(2,1)}, u32[]{:S(2)}) %copy-start) | copy-done | bytes 1048600
  6.2 0.4 prototypes.1
  6.6 2.1 %pooling.5 = (bf16[1024,512]{1,0:T(8,128)(2,1)S(1)}, bf16[1024,512]{1,0:T(8,128)(2,1)S(1)}, bf16[1024,512]{1,0:T(8,128)(2,1)S(1)}, bf16[512,256]{1,0:T(8,128)(2,1)S(1)}, bf16[256,256]{1,0:T(8,128)(2,1)S(1)}) custom-call(bf16[1024,1024]{1,0:T(8,128)(2,1)} %refs_0_.1, bf16[1024,1024]{1,0:T(8,128)(2,1)} %refs_1_.1, bf16[1024,1024]{1,0:T(8,128)(2,1)} %refs_2_.1, ...), custom_call_target="tpu_custom_call" | custom-call | flops 1 | bytes 1 | tf_op jit(solution)/shard_map/pooling/pallas_call | solution.py:28
  8.7 0.0 collective-permute-done.refs_1_
  8.7 3.1 %pooling.6 = (bf16[512,512]{1,0:T(8,128)(2,1)S(1)}, bf16[512,512]{1,0:T(8,128)(2,1)S(1)}, bf16[512,512]{1,0:T(8,128)(2,1)S(1)}, f32[4096,512]{1,0:T(8,128)S(1)}, f32[512,128]{1,0:T(8,128)S(1)}) custom-call(bf16[256,1024]{1,0:T(8,128)(2,1)S(1)} %get-tuple-element.49.refs_0_, bf16[256,1024]{1,0:T(8,128)(2,1)S(1)} %collective-permute-done.refs_1_, ...), custom_call_target="tpu_custom_call" | custom-call | flops 1 | bytes 1 | tf_op jit(solution)/shard_map/pooling/pallas_call | solution.py:28
  11.9 0.2 collective-permute-done.1.refs_0_.refs_2_
  12.1 0.1 collective-permute-start.3
  12.2 0.5 collective-permute-start.2
  12.7 0.8 %collective-permute-done.3.refs_2_.refs_4_ = bf16[64,1024]{1,0:T(8,128)(2,1)S(1)} collective-permute-done((bf16[64,1024]{1,0:T(8,128)(2,1)S(1)}, bf16[64,1024]{1,0:T(8,128)(2,1)S(1)}, u32[]{:S(2)}, u32[]{:S(2)}) %collective-permute-start.3) | collective-permute-done | bytes 131104 | tf_op jit(solution)/shard_map/pooling/ppermute | solution.py:352
  13.5 0.2 collective-permute-done.2.refs_1_.refs_3_
  13.7 2.7 %pooling.7 = (bf16[256,512]{1,0:T(8,128)(2,1)S(1)}, bf16[512,256]{1,0:T(8,128)(2,1)S(1)}, bf16[256,512]{1,0:T(8,128)(2,1)S(1)}, f32[2048,768]{1,0:T(8,128)S(1)},...) custom-call(bf16[512,512]{1,0:T(8,128)(2,1)S(1)} %get-tuple-element.53.q_e.refs_0_, ...), custom_call_target="tpu_custom_call" | custom-call | flops 1 | bytes 1 | tf_op jit(solution)/shard_map/pooling/pallas_call | solution.py:28
  16.4 0.8 %collective-permute-done.4.refs_0_.refs_5_ = bf16[128,1024]{1,0:T(8,128)(2,1)S(1)} collective-permute-done((bf16[128,1024]{1,0:T(8,128)(2,1)S(1)}, bf16[128,1024]{1,0:T(8,128)(2,1)S(1)}, u32[]{:S(2)}, u32[]{:S(2)}) %collective-permute-start.4) | collective-permute-done | bytes 262176 | tf_op jit(solution)/shard_map/tokens_of_a_clip/ppermute | solution.py:340
  17.2 0.1 collective-permute-start.5
  17.3 0.6 pooling.8
  17.9 0.8 %collective-permute-done.5.refs_14_.refs_6_ = bf16[128,1024]{1,0:T(8,128)(2,1)S(1)} collective-permute-done((bf16[128,1024]{1,0:T(8,128)(2,1)S(1)}, bf16[128,1024]{1,0:T(8,128)(2,1)S(1)}, u32[]{:S(2)}, u32[]{:S(2)}) %collective-permute-start.5) | collective-permute-done | bytes 262176 | tf_op jit(solution)/shard_map/pooling/ppermute | solution.py:352
  18.7 7.5 %pooling.9 = (bf16[8,1024]{1,0:T(8,128)(2,1)S(1)}, f32[1,512]{1,0:T(1,128)S(1)}, f32[32,2,128]{2,1,0:T(2,128)}) custom-call(bf16[512,512]{1,0:T(8,128)(2,1)S(1)} %get-tuple-element.53.q_e.refs_0_, bf16[512,512]{1,0:T(8,128)(2,1)S(1)} %get-tuple-element.54.kt_e.refs_1_, bf16[512,512]{1,0:T(8,128)(2,1)S(1)} %get-tuple-element.55.refs_2_, ...), custom_call_target="tpu_custom_call" | custom-call | flops 1 | bytes 1 | tf_op jit(solution)/shard_map/pooling/pallas_call | solution.py:28
  26.2 5.9 %all-to-all-start = ((f32[32,2,128]{2,1,0:T(2,128)}), f32[32,2,128]{2,1,0:T(2,128)S(1)}, u32[]{:S(2)}, u32[]{:S(2)}) async-start(f32[32,2,128]{2,1,0:T(2,128)} %get-tuple-element.74), calls=%async_computation | async-start | bytes 65536 | tf_op jit(solution)/shard_map/logits/all_to_all | solution.py:407
  32.2 0.4 mixtures.1.side
  32.6 0.0 copy-start.1
  32.6 6.8 %all-to-all-done.came = f32[32,2,128]{2,1,0:T(2,128)S(1)} async-done(((f32[32,2,128]{2,1,0:T(2,128)}), f32[32,2,128]{2,1,0:T(2,128)S(1)}, u32[]{:S(2)}, u32[]{:S(2)}) %all-to-all-start) | async-done | bytes 32800 | tf_op jit(solution)/shard_map/logits/all_to_all | solution.py:407
  39.3 0.7 logits.1
  40.0 9.0 %all_to_all.20.came = bf16[32,8,128]{2,1,0:T(8,128)(2,1)S(1)} all-to-all(bf16[32,8,128]{2,1,0:T(8,128)(2,1)S(1)} %get-tuple-element.78), channel_id=1, replica_groups=mesh['cam'=4,'clip'=8] {'cam','clip'}, dimensions={0} | all-to-all | bytes 131072 | tf_op jit(solution)/shard_map/row_total_1/all_to_all | solution.py:407
  49.0 0.2 row_total_1.1
  49.2 8.9 %all_to_all.21.came = f32[32,2,128]{2,1,0:T(2,128)S(1)} all-to-all(f32[32,2,128]{2,1,0:T(2,128)S(1)} %get-tuple-element.80), channel_id=1, replica_groups=mesh['cam'=4,'clip'=8] {'cam','clip'}, dimensions={0} | all-to-all | bytes 65536 | tf_op jit(solution)/shard_map/row_total_2/all_to_all | solution.py:407
  58.1 0.4 row_total_2.1
  58.6 0.1 collective-permute-start.6
  58.7 1.1 %collective-permute-done.6.got = f32[16,128]{1,0:T(8,128)S(1)} collective-permute-done((f32[16,128]{1,0:T(8,128)S(1)}, f32[16,128]{1,0:T(8,128)S(1)}, u32[]{:S(2)}, u32[]{:S(2)}) %collective-permute-start.6) | collective-permute-done | bytes 8224 | tf_op jit(solution)/shard_map/row_total_3/ppermute | solution.py:711
  59.8 9.5 %all_to_all.22 = bf16[32,2,1152]{2,1,0:T(2,128)(2,1)S(1)} all-to-all(bf16[32,2,1152]{2,1,0:T(2,128)(2,1)S(1)} %row_total_3.1), channel_id=1, replica_groups=mesh['cam'=4,'clip'=8] {'cam','clip'}, dimensions={0} | all-to-all | bytes 294912 | tf_op jit(solution)/shard_map/row_total_3/all_to_all | solution.py:407
  69.3 0.0 copy-done.1
  69.3 2.0 %outputs.1 = (f32[16,2048]{1,0:T(8,128)}, f32[256,2048]{1,0:T(8,128)}, f32[128,256]{1,0:T(8,128)}, f32[128,256]{1,0:T(8,128)}) custom-call(bf16[2,2,8,2,1152]{4,3,2,1,0:T(2,128)(2,1)S(1)} %bitcast.3, bf16[2,2,8,8,128]{4,3,2,1,0:T(8,128)(2,1)S(1)} %bitcast.4, f32[16,256]{1,0:T(8,128)S(1)} %get-tuple-element.87.unit_ref, ...), custom_call_target="tpu_custom_call" | custom-call | flops 1 | bytes 1 | tf_op jit(solution)/shard_map/outputs/pallas_call | solution.py:28
  (2 shorter events, 0.0 us)
Async XLA Ops:
  1.9 6.9 %collective-permute-start = (bf16[256,1024]{1,0:T(8,128)(2,1)S(1)}, bf16[256,1024]{1,0:T(8,128)(2,1)S(1)}, u32[]{:S(2)}, u32[]{:S(2)}) collective-permute-start(bf16[256,1024]{1,0:T(8,128)(2,1)S(1)} %get-tuple-element.49.refs_0_), channel_id=1, source_target_pairs={{0,8},{8,0},{16,24},{24,16},{1,9},{9,1},{17,25},{25,17},{2,10},{10... | collective-permute-start | bytes 1572872 | tf_op jit(solution)/shard_map/pooling/ppermute | solution.py:352
  2.4 9.7 %collective-permute-start.1 = (bf16[128,1024]{1,0:T(8,128)(2,1)S(1)}, bf16[128,1024]{1,0:T(8,128)(2,1)S(1)}, u32[]{:S(2)}, u32[]{:S(2)}) collective-permute-start(bf16[128,1024]{1,0:T(8,128)(2,1)S(1)} %get-tuple-element.58), channel_id=1, source_target_pairs={{0,16},{8,24},{16,0},{24,8},{1,17},{9,25},{17,1},{25,9},{2,18},{10... | collective-permute-start | bytes 786440 | tf_op jit(solution)/shard_map/tokens_of_a_clip/ppermute | solution.py:340
  5.0 12.3 %collective-permute-start.4 = (bf16[128,1024]{1,0:T(8,128)(2,1)S(1)}, bf16[128,1024]{1,0:T(8,128)(2,1)S(1)}, u32[]{:S(2)}, u32[]{:S(2)}) collective-permute-start(bf16[128,1024]{1,0:T(8,128)(2,1)S(1)} %get-tuple-element.68), channel_id=1, source_target_pairs={{0,24},{8,16},{16,8},{24,0},{1,25},{9,17},{17,9},{25,1},{2,26},{10... | collective-permute-start | bytes 786440 | tf_op jit(solution)/shard_map/tokens_of_a_clip/ppermute | solution.py:340
  5.0 1.2 %copy-start = (bf16[256,2048]{1,0:T(8,128)(2,1)S(1)}, bf16[256,2048]{1,0:T(8,128)(2,1)}, u32[]{:S(2)}) copy-start(bf16[256,2048]{1,0:T(8,128)(2,1)} %proto.3) | copy-start | bytes 3145732
  12.1 1.4 %collective-permute-start.3 = (bf16[64,1024]{1,0:T(8,128)(2,1)S(1)}, bf16[64,1024]{1,0:T(8,128)(2,1)S(1)}, u32[]{:S(2)}, u32[]{:S(2)}) collective-permute-start(bf16[64,1024]{1,0:T(8,128)(2,1)S(1)} %get-tuple-element.94), channel_id=1, source_target_pairs={{0,8},{8,0},{16,24},{24,16},{1,9},{9,1},{17,25},{25,17},{2,10},{10... | collective-permute-start | bytes 393224 | tf_op jit(solution)/shard_map/pooling/ppermute | solution.py:352
  12.2 1.5 %collective-permute-start.2 = (bf16[64,1024]{1,0:T(8,128)(2,1)S(1)}, bf16[64,1024]{1,0:T(8,128)(2,1)S(1)}, u32[]{:S(2)}, u32[]{:S(2)}) collective-permute-start(bf16[64,1024]{1,0:T(8,128)(2,1)S(1)} %get-tuple-element.95), channel_id=1, source_target_pairs={{0,8},{8,0},{16,24},{24,16},{1,9},{9,1},{17,25},{25,17},{2,10},{10... | collective-permute-start | bytes 393224 | tf_op jit(solution)/shard_map/pooling/ppermute | solution.py:352
  17.2 1.5 %collective-permute-start.5 = (bf16[128,1024]{1,0:T(8,128)(2,1)S(1)}, bf16[128,1024]{1,0:T(8,128)(2,1)S(1)}, u32[]{:S(2)}, u32[]{:S(2)}) collective-permute-start(bf16[128,1024]{1,0:T(8,128)(2,1)S(1)} %collective-permute-done.4.refs_0_.refs_5_), channel_id=1, source_target_pairs={{0,8},{8,0},{16,24},{24,16},{1,9},{9,1},{17,25},{25,17},{2,10},{10... | collective-permute-start | bytes 786440 | tf_op jit(solution)/shard_map/pooling/ppermute | solution.py:352
  26.2 13.1 %all-to-all-start = ((f32[32,2,128]{2,1,0:T(2,128)}), f32[32,2,128]{2,1,0:T(2,128)S(1)}, u32[]{:S(2)}, u32[]{:S(2)}) async-start(f32[32,2,128]{2,1,0:T(2,128)} %get-tuple-element.74), calls=%async_computation | async-start | bytes 65536 | tf_op jit(solution)/shard_map/logits/all_to_all | solution.py:407
  32.6 36.8 %copy-start.1 = (bf16[256,2048]{1,0:T(8,128)(2,1)S(1)}, bf16[256,2048]{1,0:T(8,128)(2,1)}, u32[]{:S(2)}) copy-start(bf16[256,2048]{1,0:T(8,128)(2,1)} %proto.3) | copy-start | bytes 3145732
  58.6 1.2 %collective-permute-start.6 = (f32[16,128]{1,0:T(8,128)S(1)}, f32[16,128]{1,0:T(8,128)S(1)}, u32[]{:S(2)}, u32[]{:S(2)}) collective-permute-start(f32[16,128]{1,0:T(8,128)S(1)} %get-tuple-element.83), channel_id=1, source_target_pairs={{0,8},{8,0},{16,24},{24,16},{1,9},{9,1},{17,25},{25,17},{2,10},{10... | collective-permute-start | bytes 24584 | tf_op jit(solution)/shard_map/row_total_3/ppermute | solution.py:711

commit v8 on v7

--- a/solution.py
+++ b/solution.py
@@ -193,16 +193,19 @@
                 return jnp.sum(a, axis=1, keepdims=True)
 
             def known(sums):
-                return row_sum(jnp.where(lanes(sums.shape[0]) == head, sums[...], 0.0))
+                return jnp.where(lanes(sums.shape[0]) == head, sums[...], 0.0)
+
+            def lane_sums(a):
+                return sum(a[:, i : i + LANES] for i in range(0, a.shape[1], LANES))
 
             def kept(a, rows, keys):
                 return a[pl.ds(pl.multiple_of(head * rows, rows), rows), keys].astype(F32)
 
             new = [exps(q_s, kt) for kt in (kt_e, kt_n, kt_s)]
             e_s, n_s = exps(q_e, kt_s), exps(q_n, kt_s)
-            by_s = 1.0 / sum(row_sum(a) for a in new)
-            by_e = 1.0 / (known(sum_e) + row_sum(e_s))
-            by_n = 1.0 / (known(sum_n) + row_sum(n_s))
+            by_s = 1.0 / row_sum(sum(lane_sums(a) for a in new))
+            by_e = 1.0 / row_sum(known(sum_e) + lane_sums(e_s))
+            by_n = 1.0 / row_sum(known(sum_n) + lane_sums(n_s))
             columns = [
                 (new[0], kept(exp_e, first, slice(None)), kept(exp_n, then, slice(0, first))),
                 (new[1], kept(exp_x, first, slice(None)), kept(exp_n, then, slice(first, None))),

time: 71.6 us -> 71.4 us (level)
  no operation moved by 1% of the time
where the time goes in v8:
time: 71.4 us; the launch traced here: 71.1 us
  blocking collectives  27.4 us (38%)
  Pallas kernels  21.1 us (30%)
  waiting for transfers between devices  10.7 us (15%)
  starting transfers between devices  9.88 us (14%)
  local copies, waits for them, and re-layouts  1.25 us (2%)
  between operations  0.75 us (1%)
    all_to_all x3, blocking collectives, exchange(): return lax.all_to_all(message, ALL, split_axis=0, concat_axis=0, tiled=True)  27.4 us
    pallas_call x13, Pallas kernels, call(): pl.pallas_call(kernel, out_shape=tuple((jax.ShapeDtypeStruct(*o) for o in...  21.1 us
    all_to_all x1, waiting for transfers between devices, exchange(): return lax.all_to_all(message, ALL, split_axis=0, concat_axis=0, tiled=True)  6.78 us
    all_to_all x1, starting transfers between devices, exchange(): return lax.all_to_all(message, ALL, split_axis=0, concat_axis=0, tiled=True)  5.93 us
    ppermute x2, starting transfers between devices, from_other_groups(): held[c].append((s * ranks + c % ranks, lax.ppermute(block, 'cam', perm)))  2.63 us
    ppermute x4, waiting for transfers between devices, relay(): stage.append((label, lax.ppermute(b, 'cam', perm)))  1.86 us
  transfers between devices with their start and end apart: 8, of which 7 were waited for; matrix products, arithmetic and copies ran while one was open for 0% of the time, Pallas kernels for 13%

profile of v8, /device:TPU:0, one launch (start us, length us, event | category | flops | bytes accessed | tf_op | source)
XLA Modules:
  0.0 71.1 jit_solution(8358927253750273798)
XLA Ops:
  0.6 1.2 %tokens_of_a_clip.1 = (bf16[256,1024]{1,0:T(8,128)(2,1)S(1)}, bf16[128,1024]{1,0:T(8,128)(2,1)S(1)}, bf16[128,1024]{1,0:T(8,128)(2,1)S(1)}) custom-call(bf16[2,256,1024]{2,1,0:T(8,128)(2,1)} %bitcast.5), custom_call_target="tpu_custom_call" | custom-call | flops 1 | bytes 1 | tf_op jit(solution)/shard_map/tokens_of_a_clip/pallas_call | solution.py:28
  1.9 0.5 collective-permute-start
  2.4 2.6 %collective-permute-start.1 = (bf16[128,1024]{1,0:T(8,128)(2,1)S(1)}, bf16[128,1024]{1,0:T(8,128)(2,1)S(1)}, u32[]{:S(2)}, u32[]{:S(2)}) collective-permute-start(bf16[128,1024]{1,0:T(8,128)(2,1)S(1)} %get-tuple-element.58), channel_id=1, source_target_pairs={{0,16},{8,24},{16,0},{24,8},{1,17},{9,25},{17,1},{25,9},{2,18},{10... | collective-permute-start | bytes 786440 | tf_op jit(solution)/shard_map/tokens_of_a_clip/ppermute | solution.py:343
  5.0 0.1 collective-permute-start.4
  5.0 0.0 copy-start
  5.0 1.2 %copy-done = bf16[256,2048]{1,0:T(8,128)(2,1)S(1)} copy-done((bf16[256,2048]{1,0:T(8,128)(2,1)S(1)}, bf16[256,2048]{1,0:T(8,128)(2,1)}, u32[]{:S(2)}) %copy-start) | copy-done | bytes 1048600
  6.2 0.4 prototypes.1
  6.6 2.1 %pooling.5 = (bf16[1024,512]{1,0:T(8,128)(2,1)S(1)}, bf16[1024,512]{1,0:T(8,128)(2,1)S(1)}, bf16[1024,512]{1,0:T(8,128)(2,1)S(1)}, bf16[512,256]{1,0:T(8,128)(2,1)S(1)}, bf16[256,256]{1,0:T(8,128)(2,1)S(1)}) custom-call(bf16[1024,1024]{1,0:T(8,128)(2,1)} %refs_0_.1, bf16[1024,1024]{1,0:T(8,128)(2,1)} %refs_1_.1, bf16[1024,1024]{1,0:T(8,128)(2,1)} %refs_2_.1, ...), custom_call_target="tpu_custom_call" | custom-call | flops 1 | bytes 1 | tf_op jit(solution)/shard_map/pooling/pallas_call | solution.py:28
  8.7 0.0 collective-permute-done.refs_1_
  8.7 3.1 %pooling.6 = (bf16[512,512]{1,0:T(8,128)(2,1)S(1)}, bf16[512,512]{1,0:T(8,128)(2,1)S(1)}, bf16[512,512]{1,0:T(8,128)(2,1)S(1)}, f32[4096,512]{1,0:T(8,128)S(1)}, f32[512,128]{1,0:T(8,128)S(1)}) custom-call(bf16[256,1024]{1,0:T(8,128)(2,1)S(1)} %get-tuple-element.49.refs_0_, bf16[256,1024]{1,0:T(8,128)(2,1)S(1)} %collective-permute-done.refs_1_, ...), custom_call_target="tpu_custom_call" | custom-call | flops 1 | bytes 1 | tf_op jit(solution)/shard_map/pooling/pallas_call | solution.py:28
  11.9 0.2 collective-permute-done.1.refs_0_.refs_2_
  12.1 0.1 collective-permute-start.3
  12.2 0.5 collective-permute-start.2
  12.7 0.8 %collective-permute-done.3.refs_2_.refs_4_ = bf16[64,1024]{1,0:T(8,128)(2,1)S(1)} collective-permute-done((bf16[64,1024]{1,0:T(8,128)(2,1)S(1)}, bf16[64,1024]{1,0:T(8,128)(2,1)S(1)}, u32[]{:S(2)}, u32[]{:S(2)}) %collective-permute-start.3) | collective-permute-done | bytes 131104 | tf_op jit(solution)/shard_map/pooling/ppermute | solution.py:355
  13.5 0.2 collective-permute-done.2.refs_1_.refs_3_
  13.7 2.7 %pooling.7 = (bf16[256,512]{1,0:T(8,128)(2,1)S(1)}, bf16[512,256]{1,0:T(8,128)(2,1)S(1)}, bf16[256,512]{1,0:T(8,128)(2,1)S(1)}, f32[2048,768]{1,0:T(8,128)S(1)},...) custom-call(bf16[512,512]{1,0:T(8,128)(2,1)S(1)} %get-tuple-element.53.q_e.refs_0_, ...), custom_call_target="tpu_custom_call" | custom-call | flops 1 | bytes 1 | tf_op jit(solution)/shard_map/pooling/pallas_call | solution.py:28
  16.4 0.8 %collective-permute-done.4.refs_0_.refs_5_ = bf16[128,1024]{1,0:T(8,128)(2,1)S(1)} collective-permute-done((bf16[128,1024]{1,0:T(8,128)(2,1)S(1)}, bf16[128,1024]{1,0:T(8,128)(2,1)S(1)}, u32[]{:S(2)}, u32[]{:S(2)}) %collective-permute-start.4) | collective-permute-done | bytes 262176 | tf_op jit(solution)/shard_map/tokens_of_a_clip/ppermute | solution.py:343
  17.2 0.1 collective-permute-start.5
  17.3 0.6 pooling.8
  17.9 0.8 %collective-permute-done.5.refs_14_.refs_6_ = bf16[128,1024]{1,0:T(8,128)(2,1)S(1)} collective-permute-done((bf16[128,1024]{1,0:T(8,128)(2,1)S(1)}, bf16[128,1024]{1,0:T(8,128)(2,1)S(1)}, u32[]{:S(2)}, u32[]{:S(2)}) %collective-permute-start.5) | collective-permute-done | bytes 262176 | tf_op jit(solution)/shard_map/pooling/ppermute | solution.py:355
  18.7 7.2 %pooling.9 = (bf16[8,1024]{1,0:T(8,128)(2,1)S(1)}, f32[1,512]{1,0:T(1,128)S(1)}, f32[32,2,128]{2,1,0:T(2,128)}) custom-call(bf16[512,512]{1,0:T(8,128)(2,1)S(1)} %get-tuple-element.53.q_e.refs_0_, bf16[512,512]{1,0:T(8,128)(2,1)S(1)} %get-tuple-element.54.kt_e.refs_1_, bf16[512,512]{1,0:T(8,128)(2,1)S(1)} %get-tuple-element.55.refs_2_, ...), custom_call_target="tpu_custom_call" | custom-call | flops 1 | bytes 1 | tf_op jit(solution)/shard_map/pooling/pallas_call | solution.py:28
  26.0 5.9 %all-to-all-start = ((f32[32,2,128]{2,1,0:T(2,128)}), f32[32,2,128]{2,1,0:T(2,128)S(1)}, u32[]{:S(2)}, u32[]{:S(2)}) async-start(f32[32,2,128]{2,1,0:T(2,128)} %get-tuple-element.74), calls=%async_computation | async-start | bytes 65536 | tf_op jit(solution)/shard_map/logits/all_to_all | solution.py:410
  31.9 0.4 mixtures.1.side
  32.3 0.0 copy-start.1
  32.3 6.8 %all-to-all-done.came = f32[32,2,128]{2,1,0:T(2,128)S(1)} async-done(((f32[32,2,128]{2,1,0:T(2,128)}), f32[32,2,128]{2,1,0:T(2,128)S(1)}, u32[]{:S(2)}, u32[]{:S(2)}) %all-to-all-start) | async-done | bytes 32800 | tf_op jit(solution)/shard_map/logits/all_to_all | solution.py:410
  39.1 0.7 logits.1
  39.8 9.0 %all_to_all.20.came = bf16[32,8,128]{2,1,0:T(8,128)(2,1)S(1)} all-to-all(bf16[32,8,128]{2,1,0:T(8,128)(2,1)S(1)} %get-tuple-element.78), channel_id=1, replica_groups=mesh['cam'=4,'clip'=8] {'cam','clip'}, dimensions={0} | all-to-all | bytes 131072 | tf_op jit(solution)/shard_map/row_total_1/all_to_all | solution.py:410
  48.7 0.2 row_total_1.1
  49.0 8.9 %all_to_all.21.came = f32[32,2,128]{2,1,0:T(2,128)S(1)} all-to-all(f32[32,2,128]{2,1,0:T(2,128)S(1)} %get-tuple-element.80), channel_id=1, replica_groups=mesh['cam'=4,'clip'=8] {'cam','clip'}, dimensions={0} | all-to-all | bytes 65536 | tf_op jit(solution)/shard_map/row_total_2/all_to_all | solution.py:410
  57.9 0.4 row_total_2.1
  58.3 0.1 collective-permute-start.6
  58.4 1.1 %collective-permute-done.6.got = f32[16,128]{1,0:T(8,128)S(1)} collective-permute-done((f32[16,128]{1,0:T(8,128)S(1)}, f32[16,128]{1,0:T(8,128)S(1)}, u32[]{:S(2)}, u32[]{:S(2)}) %collective-permute-start.6) | collective-permute-done | bytes 8224 | tf_op jit(solution)/shard_map/row_total_3/ppermute | solution.py:714
  59.5 9.5 %all_to_all.22 = bf16[32,2,1152]{2,1,0:T(2,128)(2,1)S(1)} all-to-all(bf16[32,2,1152]{2,1,0:T(2,128)(2,1)S(1)} %row_total_3.1), channel_id=1, replica_groups=mesh['cam'=4,'clip'=8] {'cam','clip'}, dimensions={0} | all-to-all | bytes 294912 | tf_op jit(solution)/shard_map/row_total_3/all_to_all | solution.py:410
  69.1 0.0 copy-done.1
  69.1 2.0 %outputs.1 = (f32[16,2048]{1,0:T(8,128)}, f32[256,2048]{1,0:T(8,128)}, f32[128,256]{1,0:T(8,128)}, f32[128,256]{1,0:T(8,128)}) custom-call(bf16[2,2,8,2,1152]{4,3,2,1,0:T(2,128)(2,1)S(1)} %bitcast.3, bf16[2,2,8,8,128]{4,3,2,1,0:T(8,128)(2,1)S(1)} %bitcast.4, f32[16,256]{1,0:T(8,128)S(1)} %get-tuple-element.87.unit_ref, ...), custom_call_target="tpu_custom_call" | custom-call | flops 1 | bytes 1 | tf_op jit(solution)/shard_map/outputs/pallas_call | solution.py:28
  (2 shorter events, 0.0 us)
Async XLA Ops:
  1.9 6.9 %collective-permute-start = (bf16[256,1024]{1,0:T(8,128)(2,1)S(1)}, bf16[256,1024]{1,0:T(8,128)(2,1)S(1)}, u32[]{:S(2)}, u32[]{:S(2)}) collective-permute-start(bf16[256,1024]{1,0:T(8,128)(2,1)S(1)} %get-tuple-element.49.refs_0_), channel_id=1, source_target_pairs={{0,8},{8,0},{16,24},{24,16},{1,9},{9,1},{17,25},{25,17},{2,10},{10... | collective-permute-start | bytes 1572872 | tf_op jit(solution)/shard_map/pooling/ppermute | solution.py:355
  2.4 9.7 %collective-permute-start.1 = (bf16[128,1024]{1,0:T(8,128)(2,1)S(1)}, bf16[128,1024]{1,0:T(8,128)(2,1)S(1)}, u32[]{:S(2)}, u32[]{:S(2)}) collective-permute-start(bf16[128,1024]{1,0:T(8,128)(2,1)S(1)} %get-tuple-element.58), channel_id=1, source_target_pairs={{0,16},{8,24},{16,0},{24,8},{1,17},{9,25},{17,1},{25,9},{2,18},{10... | collective-permute-start | bytes 786440 | tf_op jit(solution)/shard_map/tokens_of_a_clip/ppermute | solution.py:343
  5.0 12.3 %collective-permute-start.4 = (bf16[128,1024]{1,0:T(8,128)(2,1)S(1)}, bf16[128,1024]{1,0:T(8,128)(2,1)S(1)}, u32[]{:S(2)}, u32[]{:S(2)}) collective-permute-start(bf16[128,1024]{1,0:T(8,128)(2,1)S(1)} %get-tuple-element.68), channel_id=1, source_target_pairs={{0,24},{8,16},{16,8},{24,0},{1,25},{9,17},{17,9},{25,1},{2,26},{10... | collective-permute-start | bytes 786440 | tf_op jit(solution)/shard_map/tokens_of_a_clip/ppermute | solution.py:343
  5.0 1.2 %copy-start = (bf16[256,2048]{1,0:T(8,128)(2,1)S(1)}, bf16[256,2048]{1,0:T(8,128)(2,1)}, u32[]{:S(2)}) copy-start(bf16[256,2048]{1,0:T(8,128)(2,1)} %proto.3) | copy-start | bytes 3145732
  12.1 1.4 %collective-permute-start.3 = (bf16[64,1024]{1,0:T(8,128)(2,1)S(1)}, bf16[64,1024]{1,0:T(8,128)(2,1)S(1)}, u32[]{:S(2)}, u32[]{:S(2)}) collective-permute-start(bf16[64,1024]{1,0:T(8,128)(2,1)S(1)} %get-tuple-element.94), channel_id=1, source_target_pairs={{0,8},{8,0},{16,24},{24,16},{1,9},{9,1},{17,25},{25,17},{2,10},{10... | collective-permute-start | bytes 393224 | tf_op jit(solution)/shard_map/pooling/ppermute | solution.py:355
  12.2 1.5 %collective-permute-start.2 = (bf16[64,1024]{1,0:T(8,128)(2,1)S(1)}, bf16[64,1024]{1,0:T(8,128)(2,1)S(1)}, u32[]{:S(2)}, u32[]{:S(2)}) collective-permute-start(bf16[64,1024]{1,0:T(8,128)(2,1)S(1)} %get-tuple-element.95), channel_id=1, source_target_pairs={{0,8},{8,0},{16,24},{24,16},{1,9},{9,1},{17,25},{25,17},{2,10},{10... | collective-permute-start | bytes 393224 | tf_op jit(solution)/shard_map/pooling/ppermute | solution.py:355
  17.2 1.5 %collective-permute-start.5 = (bf16[128,1024]{1,0:T(8,128)(2,1)S(1)}, bf16[128,1024]{1,0:T(8,128)(2,1)S(1)}, u32[]{:S(2)}, u32[]{:S(2)}) collective-permute-start(bf16[128,1024]{1,0:T(8,128)(2,1)S(1)} %collective-permute-done.4.refs_0_.refs_5_), channel_id=1, source_target_pairs={{0,8},{8,0},{16,24},{24,16},{1,9},{9,1},{17,25},{25,17},{2,10},{10... | collective-permute-start | bytes 786440 | tf_op jit(solution)/shard_map/pooling/ppermute | solution.py:355
  26.0 13.1 %all-to-all-start = ((f32[32,2,128]{2,1,0:T(2,128)}), f32[32,2,128]{2,1,0:T(2,128)S(1)}, u32[]{:S(2)}, u32[]{:S(2)}) async-start(f32[32,2,128]{2,1,0:T(2,128)} %get-tuple-element.74), calls=%async_computation | async-start | bytes 65536 | tf_op jit(solution)/shard_map/logits/all_to_all | solution.py:410
  32.3 36.8 %copy-start.1 = (bf16[256,2048]{1,0:T(8,128)(2,1)S(1)}, bf16[256,2048]{1,0:T(8,128)(2,1)}, u32[]{:S(2)}) copy-start(bf16[256,2048]{1,0:T(8,128)(2,1)} %proto.3) | copy-start | bytes 3145732
  58.3 1.2 %collective-permute-start.6 = (f32[16,128]{1,0:T(8,128)S(1)}, f32[16,128]{1,0:T(8,128)S(1)}, u32[]{:S(2)}, u32[]{:S(2)}) collective-permute-start(f32[16,128]{1,0:T(8,128)S(1)} %get-tuple-element.83), channel_id=1, source_target_pairs={{0,8},{8,0},{16,24},{24,16},{1,9},{9,1},{17,25},{25,17},{2,10},{10... | collective-permute-start | bytes 24584 | tf_op jit(solution)/shard_map/row_total_3/ppermute | solution.py:714

commit v9 on v8

--- a/solution.py
+++ b/solution.py
@@ -179,7 +179,7 @@
     def lanes(rows):
         return lax.broadcasted_iota(jnp.int32, (rows, LANES), 1)
 
-    @pl.loop(0, cols // LANES)
+    @pl.loop(0, cols // LANES, unroll=2 if exp_e.dtype == F32 else 1)
     def _(tile):
         here = pl.ds(pl.multiple_of(tile * LANES, LANES), LANES)
         for e in range(LANES // HD):
@@ -721,7 +721,7 @@
         came = exchange(after(message, proj_rows))
 
     with jax.named_scope("outputs"):
-        block = min(columns, 512)
+        block = min(columns, 256)
         ins = [
             came.reshape((clips, ranks, n_clip) + came.shape[1:]),
             came_side.reshape((clips, ranks, n_clip) + came_side.shape[1:]),

time: 71.4 us -> 71.2 us (level)
  no operation moved by 1% of the time
where the time goes in v9:
time: 71.2 us; the launch traced here: 70.9 us
  blocking collectives  27.4 us (38%)
  Pallas kernels  21 us (29%)
  waiting for transfers between devices  10.7 us (15%)
  starting transfers between devices  9.87 us (14%)
  local copies, waits for them, and re-layouts  1.25 us (2%)
  between operations  0.75 us (1%)
    all_to_all x3, blocking collectives, exchange(): return lax.all_to_all(message, ALL, split_axis=0, concat_axis=0, tiled=True)  27.4 us
    pallas_call x13, Pallas kernels, call(): pl.pallas_call(kernel, out_shape=tuple((jax.ShapeDtypeStruct(*o) for o in...  21 us
    all_to_all x1, waiting for transfers between devices, exchange(): return lax.all_to_all(message, ALL, split_axis=0, concat_axis=0, tiled=True)  6.78 us
    all_to_all x1, starting transfers between devices, exchange(): return lax.all_to_all(message, ALL, split_axis=0, concat_axis=0, tiled=True)  5.91 us
    ppermute x2, starting transfers between devices, from_other_groups(): held[c].append((s * ranks + c % ranks, lax.ppermute(block, 'cam', perm)))  2.63 us
    ppermute x4, waiting for transfers between devices, relay(): stage.append((label, lax.ppermute(b, 'cam', perm)))  1.86 us
  transfers between devices with their start and end apart: 8, of which 7 were waited for; matrix products, arithmetic and copies ran while one was open for 0% of the time, Pallas kernels for 13%

profile of v9, /device:TPU:0, one launch (start us, length us, event | category | flops | bytes accessed | tf_op | source)
XLA Modules:
  0.0 70.9 jit_solution(11056044426878275432)
XLA Ops:
  0.6 1.2 %tokens_of_a_clip.1 = (bf16[256,1024]{1,0:T(8,128)(2,1)S(1)}, bf16[128,1024]{1,0:T(8,128)(2,1)S(1)}, bf16[128,1024]{1,0:T(8,128)(2,1)S(1)}) custom-call(bf16[2,256,1024]{2,1,0:T(8,128)(2,1)} %bitcast.5), custom_call_target="tpu_custom_call" | custom-call | flops 1 | bytes 1 | tf_op jit(solution)/shard_map/tokens_of_a_clip/pallas_call | solution.py:28
  1.9 0.5 collective-permute-start
  2.4 2.6 %collective-permute-start.1 = (bf16[128,1024]{1,0:T(8,128)(2,1)S(1)}, bf16[128,1024]{1,0:T(8,128)(2,1)S(1)}, u32[]{:S(2)}, u32[]{:S(2)}) collective-permute-start(bf16[128,1024]{1,0:T(8,128)(2,1)S(1)} %get-tuple-element.58), channel_id=1, source_target_pairs={{0,16},{8,24},{16,0},{24,8},{1,17},{9,25},{17,1},{25,9},{2,18},{10... | collective-permute-start | bytes 786440 | tf_op jit(solution)/shard_map/tokens_of_a_clip/ppermute | solution.py:343
  5.0 0.1 collective-permute-start.4
  5.0 0.0 copy-start
  5.0 1.2 %copy-done = bf16[256,2048]{1,0:T(8,128)(2,1)S(1)} copy-done((bf16[256,2048]{1,0:T(8,128)(2,1)S(1)}, bf16[256,2048]{1,0:T(8,128)(2,1)}, u32[]{:S(2)}) %copy-start) | copy-done | bytes 1048600
  6.2 0.4 prototypes.1
  6.6 2.1 %pooling.5 = (bf16[1024,512]{1,0:T(8,128)(2,1)S(1)}, bf16[1024,512]{1,0:T(8,128)(2,1)S(1)}, bf16[1024,512]{1,0:T(8,128)(2,1)S(1)}, bf16[512,256]{1,0:T(8,128)(2,1)S(1)}, bf16[256,256]{1,0:T(8,128)(2,1)S(1)}) custom-call(bf16[1024,1024]{1,0:T(8,128)(2,1)} %refs_0_.1, bf16[1024,1024]{1,0:T(8,128)(2,1)} %refs_1_.1, bf16[1024,1024]{1,0:T(8,128)(2,1)} %refs_2_.1, ...), custom_call_target="tpu_custom_call" | custom-call | flops 1 | bytes 1 | tf_op jit(solution)/shard_map/pooling/pallas_call | solution.py:28
  8.7 0.0 collective-permute-done.refs_1_
  8.7 3.1 %pooling.6 = (bf16[512,512]{1,0:T(8,128)(2,1)S(1)}, bf16[512,512]{1,0:T(8,128)(2,1)S(1)}, bf16[512,512]{1,0:T(8,128)(2,1)S(1)}, f32[4096,512]{1,0:T(8,128)S(1)}, f32[512,128]{1,0:T(8,128)S(1)}) custom-call(bf16[256,1024]{1,0:T(8,128)(2,1)S(1)} %get-tuple-element.49.refs_0_, bf16[256,1024]{1,0:T(8,128)(2,1)S(1)} %collective-permute-done.refs_1_, ...), custom_call_target="tpu_custom_call" | custom-call | flops 1 | bytes 1 | tf_op jit(solution)/shard_map/pooling/pallas_call | solution.py:28
  11.9 0.2 collective-permute-done.1.refs_0_.refs_2_
  12.1 0.1 collective-permute-start.3
  12.2 0.5 collective-permute-start.2
  12.7 0.8 %collective-permute-done.3.refs_2_.refs_4_ = bf16[64,1024]{1,0:T(8,128)(2,1)S(1)} collective-permute-done((bf16[64,1024]{1,0:T(8,128)(2,1)S(1)}, bf16[64,1024]{1,0:T(8,128)(2,1)S(1)}, u32[]{:S(2)}, u32[]{:S(2)}) %collective-permute-start.3) | collective-permute-done | bytes 131104 | tf_op jit(solution)/shard_map/pooling/ppermute | solution.py:355
  13.5 0.2 collective-permute-done.2.refs_1_.refs_3_
  13.7 2.7 %pooling.7 = (bf16[256,512]{1,0:T(8,128)(2,1)S(1)}, bf16[512,256]{1,0:T(8,128)(2,1)S(1)}, bf16[256,512]{1,0:T(8,128)(2,1)S(1)}, f32[2048,768]{1,0:T(8,128)S(1)},...) custom-call(bf16[512,512]{1,0:T(8,128)(2,1)S(1)} %get-tuple-element.53.q_e.refs_0_, ...), custom_call_target="tpu_custom_call" | custom-call | flops 1 | bytes 1 | tf_op jit(solution)/shard_map/pooling/pallas_call | solution.py:28
  16.4 0.8 %collective-permute-done.4.refs_0_.refs_5_ = bf16[128,1024]{1,0:T(8,128)(2,1)S(1)} collective-permute-done((bf16[128,1024]{1,0:T(8,128)(2,1)S(1)}, bf16[128,1024]{1,0:T(8,128)(2,1)S(1)}, u32[]{:S(2)}, u32[]{:S(2)}) %collective-permute-start.4) | collective-permute-done | bytes 262176 | tf_op jit(solution)/shard_map/tokens_of_a_clip/ppermute | solution.py:343
  17.2 0.1 collective-permute-start.5
  17.3 0.6 pooling.8
  17.9 0.8 %collective-permute-done.5.refs_14_.refs_6_ = bf16[128,1024]{1,0:T(8,128)(2,1)S(1)} collective-permute-done((bf16[128,1024]{1,0:T(8,128)(2,1)S(1)}, bf16[128,1024]{1,0:T(8,128)(2,1)S(1)}, u32[]{:S(2)}, u32[]{:S(2)}) %collective-permute-start.5) | collective-permute-done | bytes 262176 | tf_op jit(solution)/shard_map/pooling/ppermute | solution.py:355
  18.7 7.1 %pooling.9 = (bf16[8,1024]{1,0:T(8,128)(2,1)S(1)}, f32[1,512]{1,0:T(1,128)S(1)}, f32[32,2,128]{2,1,0:T(2,128)}) custom-call(bf16[512,512]{1,0:T(8,128)(2,1)S(1)} %get-tuple-element.53.q_e.refs_0_, bf16[512,512]{1,0:T(8,128)(2,1)S(1)} %get-tuple-element.54.kt_e.refs_1_, bf16[512,512]{1,0:T(8,128)(2,1)S(1)} %get-tuple-element.55.refs_2_, ...), custom_call_target="tpu_custom_call" | custom-call | flops 1 | bytes 1 | tf_op jit(solution)/shard_map/pooling/pallas_call | solution.py:28
  25.9 5.9 %all-to-all-start = ((f32[32,2,128]{2,1,0:T(2,128)}), f32[32,2,128]{2,1,0:T(2,128)S(1)}, u32[]{:S(2)}, u32[]{:S(2)}) async-start(f32[32,2,128]{2,1,0:T(2,128)} %get-tuple-element.74), calls=%async_computation | async-start | bytes 65536 | tf_op jit(solution)/shard_map/logits/all_to_all | solution.py:410
  31.8 0.4 mixtures.1.side
  32.2 0.0 copy-start.1
  32.2 6.8 %all-to-all-done.came = f32[32,2,128]{2,1,0:T(2,128)S(1)} async-done(((f32[32,2,128]{2,1,0:T(2,128)}), f32[32,2,128]{2,1,0:T(2,128)S(1)}, u32[]{:S(2)}, u32[]{:S(2)}) %all-to-all-start) | async-done | bytes 32800 | tf_op jit(solution)/shard_map/logits/all_to_all | solution.py:410
  39.0 0.7 logits.1
  39.6 9.0 %all_to_all.20.came = bf16[32,8,128]{2,1,0:T(8,128)(2,1)S(1)} all-to-all(bf16[32,8,128]{2,1,0:T(8,128)(2,1)S(1)} %get-tuple-element.78), channel_id=1, replica_groups=mesh['cam'=4,'clip'=8] {'cam','clip'}, dimensions={0} | all-to-all | bytes 131072 | tf_op jit(solution)/shard_map/row_total_1/all_to_all | solution.py:410
  48.6 0.2 row_total_1.1
  48.9 8.9 %all_to_all.21.came = f32[32,2,128]{2,1,0:T(2,128)S(1)} all-to-all(f32[32,2,128]{2,1,0:T(2,128)S(1)} %get-tuple-element.80), channel_id=1, replica_groups=mesh['cam'=4,'clip'=8] {'cam','clip'}, dimensions={0} | all-to-all | bytes 65536 | tf_op jit(solution)/shard_map/row_total_2/all_to_all | solution.py:410
  57.7 0.4 row_total_2.1
  58.2 0.1 collective-permute-start.6
  58.3 1.1 %collective-permute-done.6.got = f32[16,128]{1,0:T(8,128)S(1)} collective-permute-done((f32[16,128]{1,0:T(8,128)S(1)}, f32[16,128]{1,0:T(8,128)S(1)}, u32[]{:S(2)}, u32[]{:S(2)}) %collective-permute-start.6) | collective-permute-done | bytes 8224 | tf_op jit(solution)/shard_map/row_total_3/ppermute | solution.py:714
  59.4 9.5 %all_to_all.22 = bf16[32,2,1152]{2,1,0:T(2,128)(2,1)S(1)} all-to-all(bf16[32,2,1152]{2,1,0:T(2,128)(2,1)S(1)} %row_total_3.1), channel_id=1, replica_groups=mesh['cam'=4,'clip'=8] {'cam','clip'}, dimensions={0} | all-to-all | bytes 294912 | tf_op jit(solution)/shard_map/row_total_3/all_to_all | solution.py:410
  68.9 0.0 copy-done.1
  68.9 2.0 %outputs.1 = (f32[16,2048]{1,0:T(8,128)}, f32[256,2048]{1,0:T(8,128)}, f32[128,256]{1,0:T(8,128)}, f32[128,256]{1,0:T(8,128)}) custom-call(bf16[2,2,8,2,1152]{4,3,2,1,0:T(2,128)(2,1)S(1)} %bitcast.3, bf16[2,2,8,8,128]{4,3,2,1,0:T(8,128)(2,1)S(1)} %bitcast.4, f32[16,256]{1,0:T(8,128)S(1)} %get-tuple-element.87.unit_ref, ...), custom_call_target="tpu_custom_call" | custom-call | flops 1 | bytes 1 | tf_op jit(solution)/shard_map/outputs/pallas_call | solution.py:28
  (2 shorter events, 0.0 us)
Async XLA Ops:
  1.9 6.9 %collective-permute-start = (bf16[256,1024]{1,0:T(8,128)(2,1)S(1)}, bf16[256,1024]{1,0:T(8,128)(2,1)S(1)}, u32[]{:S(2)}, u32[]{:S(2)}) collective-permute-start(bf16[256,1024]{1,0:T(8,128)(2,1)S(1)} %get-tuple-element.49.refs_0_), channel_id=1, source_target_pairs={{0,8},{8,0},{16,24},{24,16},{1,9},{9,1},{17,25},{25,17},{2,10},{10... | collective-permute-start | bytes 1572872 | tf_op jit(solution)/shard_map/pooling/ppermute | solution.py:355
  2.4 9.7 %collective-permute-start.1 = (bf16[128,1024]{1,0:T(8,128)(2,1)S(1)}, bf16[128,1024]{1,0:T(8,128)(2,1)S(1)}, u32[]{:S(2)}, u32[]{:S(2)}) collective-permute-start(bf16[128,1024]{1,0:T(8,128)(2,1)S(1)} %get-tuple-element.58), channel_id=1, source_target_pairs={{0,16},{8,24},{16,0},{24,8},{1,17},{9,25},{17,1},{25,9},{2,18},{10... | collective-permute-start | bytes 786440 | tf_op jit(solution)/shard_map/tokens_of_a_clip/ppermute | solution.py:343
  5.0 12.3 %collective-permute-start.4 = (bf16[128,1024]{1,0:T(8,128)(2,1)S(1)}, bf16[128,1024]{1,0:T(8,128)(2,1)S(1)}, u32[]{:S(2)}, u32[]{:S(2)}) collective-permute-start(bf16[128,1024]{1,0:T(8,128)(2,1)S(1)} %get-tuple-element.68), channel_id=1, source_target_pairs={{0,24},{8,16},{16,8},{24,0},{1,25},{9,17},{17,9},{25,1},{2,26},{10... | collective-permute-start | bytes 786440 | tf_op jit(solution)/shard_map/tokens_of_a_clip/ppermute | solution.py:343
  5.0 1.2 %copy-start = (bf16[256,2048]{1,0:T(8,128)(2,1)S(1)}, bf16[256,2048]{1,0:T(8,128)(2,1)}, u32[]{:S(2)}) copy-start(bf16[256,2048]{1,0:T(8,128)(2,1)} %proto.3) | copy-start | bytes 3145732
  12.1 1.4 %collective-permute-start.3 = (bf16[64,1024]{1,0:T(8,128)(2,1)S(1)}, bf16[64,1024]{1,0:T(8,128)(2,1)S(1)}, u32[]{:S(2)}, u32[]{:S(2)}) collective-permute-start(bf16[64,1024]{1,0:T(8,128)(2,1)S(1)} %get-tuple-element.94), channel_id=1, source_target_pairs={{0,8},{8,0},{16,24},{24,16},{1,9},{9,1},{17,25},{25,17},{2,10},{10... | collective-permute-start | bytes 393224 | tf_op jit(solution)/shard_map/pooling/ppermute | solution.py:355
  12.2 1.5 %collective-permute-start.2 = (bf16[64,1024]{1,0:T(8,128)(2,1)S(1)}, bf16[64,1024]{1,0:T(8,128)(2,1)S(1)}, u32[]{:S(2)}, u32[]{:S(2)}) collective-permute-start(bf16[64,1024]{1,0:T(8,128)(2,1)S(1)} %get-tuple-element.95), channel_id=1, source_target_pairs={{0,8},{8,0},{16,24},{24,16},{1,9},{9,1},{17,25},{25,17},{2,10},{10... | collective-permute-start | bytes 393224 | tf_op jit(solution)/shard_map/pooling/ppermute | solution.py:355
  17.2 1.5 %collective-permute-start.5 = (bf16[128,1024]{1,0:T(8,128)(2,1)S(1)}, bf16[128,1024]{1,0:T(8,128)(2,1)S(1)}, u32[]{:S(2)}, u32[]{:S(2)}) collective-permute-start(bf16[128,1024]{1,0:T(8,128)(2,1)S(1)} %collective-permute-done.4.refs_0_.refs_5_), channel_id=1, source_target_pairs={{0,8},{8,0},{16,24},{24,16},{1,9},{9,1},{17,25},{25,17},{2,10},{10... | collective-permute-start | bytes 786440 | tf_op jit(solution)/shard_map/pooling/ppermute | solution.py:355
  25.9 13.1 %all-to-all-start = ((f32[32,2,128]{2,1,0:T(2,128)}), f32[32,2,128]{2,1,0:T(2,128)S(1)}, u32[]{:S(2)}, u32[]{:S(2)}) async-start(f32[32,2,128]{2,1,0:T(2,128)} %get-tuple-element.74), calls=%async_computation | async-start | bytes 65536 | tf_op jit(solution)/shard_map/logits/all_to_all | solution.py:410
  32.2 36.8 %copy-start.1 = (bf16[256,2048]{1,0:T(8,128)(2,1)S(1)}, bf16[256,2048]{1,0:T(8,128)(2,1)}, u32[]{:S(2)}) copy-start(bf16[256,2048]{1,0:T(8,128)(2,1)} %proto.3) | copy-start | bytes 3145732
  58.2 1.2 %collective-permute-start.6 = (f32[16,128]{1,0:T(8,128)S(1)}, f32[16,128]{1,0:T(8,128)S(1)}, u32[]{:S(2)}, u32[]{:S(2)}) collective-permute-start(f32[16,128]{1,0:T(8,128)S(1)} %get-tuple-element.83), channel_id=1, source_target_pairs={{0,8},{8,0},{16,24},{24,16},{1,9},{9,1},{17,25},{25,17},{2,10},{10... | collective-permute-start | bytes 24584 | tf_op jit(solution)/shard_map/row_total_3/ppermute | solution.py:714
